TPU v7x, 256 devices: a whole 4x4x8 slice. The times are simulated.
256 devices in a mesh: pb: 16 (over x_hi, y, core), ka: 16 (over x_lo, z).
Axes of the slice: x: 4 (x_hi: 2, x_lo: 2; x = x_hi * 2 + x_lo), y: 4, z: 8, core: 2. Of those that a mesh axis runs over, the one named last changes fastest.
Arguments:
- query: float32 [32768, 128], P(('pb', 'ka')), may hold values from -6 to 6
- keys: float32 [32768, 128], P(('ka', 'pb')), may hold values from -6 to 6
- values: float32 [32768, 128], P(('ka', 'pb')), may hold values from -6 to 6
- attn_out: float32 [32768, 128], P(('pb', 'ka')), may hold values from -6 to 6
- out_grad: float32 [32768, 128], P(('pb', 'ka')), may hold values from -6 to 6
- row_lse: float32 [1, 32768], P(None, ('pb', 'ka')), may hold values from 5 to 7
Outputs:
- query_grad: float32 [32768, 128], P(('pb', 'ka'))
- key_grad: float32 [32768, 128], P(('ka', 'pb'))
- value_grad: float32 [32768, 128], P(('ka', 'pb'))
All inputs are finite; a program needn't handle non-finite values.
Results may differ from a plain program's by a relative error of at most 0.0003.
Values sent between devices are 32-bit elements; how exact they have to be, the bound alone decides.
No kernel may reach another device: no remote copies, remote signals or barrier semaphores. Data moves between devices by JAX's collectives and lax.ppermute only.
A program may use at most 128 MiB of HBM per device.

v0:
```python
import math

import jax
import jax.numpy as jnp
from jax import lax
from jax.sharding import PartitionSpec as P

D_HEAD = 128
HEADS = 1


def dot_full(a, b):
    return jnp.dot(a, b, precision=lax.Precision.HIGHEST, preferred_element_type=jnp.float32)


def row_term(grad_rows, out_rows):
    count = grad_rows.shape[0]
    return jnp.sum((grad_rows * out_rows).reshape(count, HEADS, D_HEAD), axis=-1).T


def score_tile(q_head, k_head, v_head, g_head, lse_row, delta_row, scale):
    scores = dot_full(q_head, k_head.T) * scale
    probs = jnp.exp(scores - lse_row[:, None])
    dprob = dot_full(g_head, v_head.T)
    dscore = probs * (dprob - delta_row[:, None])
    return (probs, dscore)


def send_query_grad(partial_value):
    return lax.psum_scatter(partial_value, "ka", scatter_dimension=0, tiled=True)


def send_key_grads(k_part, v_part):
    return (
        lax.psum_scatter(k_part, "pb", scatter_dimension=0, tiled=True),
        lax.psum_scatter(v_part, "pb", scatter_dimension=0, tiled=True),
    )


def on_device(query, keys, values, attn_out, out_grad, row_lse):
    scale = 1.0 / math.sqrt(D_HEAD)
    q_blk, g_blk, o_blk = (
        lax.all_gather(query, "ka", axis=0, tiled=True),
        lax.all_gather(out_grad, "ka", axis=0, tiled=True),
        lax.all_gather(attn_out, "ka", axis=0, tiled=True),
    )
    lse_blk = lax.all_gather(row_lse, "ka", axis=1, tiled=True)
    delta_blk = row_term(g_blk, o_blk)
    k_blk, v_blk = (
        lax.all_gather(keys, "pb", axis=0, tiled=True),
        lax.all_gather(values, "pb", axis=0, tiled=True),
    )
    q_list, k_list, v_list = ([], [], [])
    probs, dscore = score_tile(q_blk, k_blk, v_blk, g_blk, lse_blk[0], delta_blk[0], scale)
    q_list.append(dot_full(dscore, k_blk) * scale)
    k_list.append(dot_full(dscore.T, q_blk) * scale)
    v_list.append(dot_full(probs.T, g_blk))
    query_grad = send_query_grad(q_list[0])
    key_grad, value_grad = send_key_grads(k_list[0], v_list[0])
    return (query_grad, key_grad, value_grad)


def solution(mesh):
    placed = (
        P(("pb", "ka"), None),
        P(("ka", "pb"), None),
        P(("ka", "pb"), None),
        P(("pb", "ka"), None),
        P(("pb", "ka"), None),
        P(None, ("pb", "ka")),
    )
    return jax.shard_map(
        on_device,
        mesh=mesh,
        in_specs=placed,
        out_specs=(P(("pb", "ka"), None), P(("ka", "pb"), None), P(("ka", "pb"), None)),
        check_vma=False,
    )
```

profile of v0, /device:TPU:2, one launch (start us, length us, event | category | flops | bytes accessed | tf_op | source)
XLA Modules:
  0.0 605.5 jit_solution(12350473101231558836)
XLA Ops:
  7.2 0.0 all-gather.14.cloned.1.call-start
  7.2 0.7 all-gather.14.cloned.1.call-update
  7.9 0.0 all-gather.10.cloned.1.call-start
  7.9 0.7 all-gather.10.cloned.1.call-update
  8.6 0.0 all-gather.6.cloned.1.call-start
  8.7 0.7 all-gather.6.cloned.1.call-update
  9.4 0.0 all-gather.8.cloned.1.call-start
  9.4 0.5 all-gather.8.cloned.1.call-update
  10.0 0.0 all-gather.12.cloned.1.call-start
  10.0 0.5 all-gather.12.cloned.1.call-update
  10.5 0.0 reduce-scatter.6.cloned.1.call-start
  10.6 35.3 %all_gather.20 = f32[1,2048]{1,0:T(1,128)S(1)} all-gather(f32[1,128]{1,0:T(1,128)} %param.11), channel_id=1, replica_groups=mesh['pb'=16,'ka'=16] {'ka'}, dimensions={1}, use_global_device_ids=true | all-gather | bytes 8704 | tf_op jit(solution)/shard_map/all_gather | solution.py:47
  45.9 35.3 %all-gather.14.cloned.1.call-done = f32[2048,128]{1,0:T(8,128)} async-done(((f32[128,128]{1,0:T(8,128)}), f32[2048,128]{1,0:T(8,128)}) %all-gather.14.cloned.1.call-update) | async-done | bytes 1048592 | tf_op jit(solution)/shard_map/all_gather | solution.py:45
  81.2 68.3 %all-gather.10.cloned.1.call-done = f32[2048,128]{1,0:T(8,128)} async-done(((f32[128,128]{1,0:T(8,128)}), f32[2048,128]{1,0:T(8,128)}) %all-gather.10.cloned.1.call-update) | async-done | bytes 1048592 | tf_op jit(solution)/shard_map/all_gather | solution.py:44
  149.5 0.0 copy-start.1
  149.5 2.6 multiply_reduce_fusion
  152.1 65.9 %all-gather.6.cloned.1.call-done = f32[2048,128]{1,0:T(8,128)} async-done(((f32[128,128]{1,0:T(8,128)}), f32[2048,128]{1,0:T(8,128)}) %all-gather.6.cloned.1.call-update) | async-done | bytes 1048592 | tf_op jit(solution)/shard_map/all_gather | solution.py:43
  218.0 50.0 %all-gather.8.cloned.1.call-done = f32[2048,128]{1,0:T(8,128)} async-done(((f32[128,128]{1,0:T(8,128)}), f32[2048,128]{1,0:T(8,128)}) %all-gather.8.cloned.1.call-update) | async-done | bytes 1048592 | tf_op jit(solution)/shard_map/all_gather | solution.py:50
  268.0 17.4 %fusion.4 = f32[2048,2048]{1,0:T(8,128)} fusion(f32[2048,128]{1,0:T(8,128)} %all-gather.6.cloned.1.call-done, f32[2048,128]{1,0:T(8,128)} %all-gather.8.cloned.1.call-done), kind=kOutput, calls=%fused_computation.9 | convolution fusion | flops 6442450944 | bytes 18874368 | tf_op jit(solution)/shard_map/dot_general | solution.py:13
  285.4 33.9 %all-gather.12.cloned.1.call-done = f32[2048,128]{1,0:T(8,128)} async-done(((f32[128,128]{1,0:T(8,128)}), f32[2048,128]{1,0:T(8,128)}) %all-gather.12.cloned.1.call-update) | async-done | bytes 1048592 | tf_op jit(solution)/shard_map/all_gather | solution.py:51
  319.3 0.0 copy-done.1
  319.3 19.0 %subtract_multiply_fusion = f32[2048,2048]{1,0:T(8,128)S(1)} fusion(f32[2048,2048]{1,0:T(8,128)} %fusion.4, f32[2048,128]{1,0:T(8,128)S(1)} %copy-done.1, f32[2048,128]{1,0:T(8,128)} %all-gather.12.cloned.1.call-done, f32[2048]{0:T(1024)} %multiply_reduce_fusion, f32[2048]{0:T(1024)S(1)} %bitcast.10), kind=kOutput, calls=%fused_computation | convolution fusion | flops 6459228160 | bytes 35667968 | tf_op jit(solution)/shard_map/dot_general | solution.py:13
  338.3 0.0 copy-start
  338.3 5.7 copy-done
  344.0 28.7 %convolution_multiply_fusion = f32[2048,128]{1,0:T(8,128)} fusion(f32[2048,2048]{1,0:T(8,128)S(1)} %subtract_multiply_fusion, f32[2048,128]{1,0:T(8,128)} %all-gather.6.cloned.1.call-done), kind=kOutput, calls=%fused_computation.5 | convolution fusion | flops 6442713088 | bytes 18874368 | tf_op jit(solution)/shard_map/dot_general | solution.py:13
  372.7 0.0 copy-start.2
  372.7 0.0 reduce-scatter.6.cloned.1.call-update
  372.7 0.0 reduce-scatter.8.cloned.1.call-start
  372.8 31.6 %fusion = f32[2048,128]{1,0:T(8,128)} fusion(f32[2048,128]{1,0:T(8,128)S(1)} %copy-done.1, f32[2048,2048]{1,0:T(8,128)} %fusion.4, f32[2048]{0:T(1024)S(1)} %bitcast.11), kind=kOutput, calls=%fused_computation.2 | convolution fusion | flops 6450839552 | bytes 18882560 | tf_op jit(solution)/shard_map/dot_general | solution.py:13
  404.4 0.0 reduce-scatter.8.cloned.1.call-update
  404.4 0.0 reduce-scatter.4.cloned.1.call-start
  404.5 0.0 copy-done.2
  404.5 17.2 %convolution_multiply_fusion.1 = f32[2048,128]{1,0:T(8,128)} fusion(f32[2048,2048]{1,0:T(8,128)} %copy-done, f32[2048,128]{1,0:T(8,128)S(1)} %copy-done.2), kind=kOutput, calls=%fused_computation.6 | convolution fusion | flops 6442713088 | bytes 18874368 | tf_op jit(solution)/shard_map/dot_general | solution.py:13
  421.7 0.0 reduce-scatter.4.cloned.1.call-update
  421.7 24.7 %reduce-scatter.6.cloned.1.call-done = f32[128,128]{1,0:T(8,128)} async-done(((f32[2048,128]{1,0:T(8,128)}), f32[128,128]{1,0:T(8,128)}) %reduce-scatter.6.cloned.1.call-update) | async-done | bytes 65552 | tf_op jit(solution)/shard_map/reduce_scatter | solution.py:35
  446.4 78.8 %reduce-scatter.8.cloned.1.call-done = f32[128,128]{1,0:T(8,128)} async-done(((f32[2048,128]{1,0:T(8,128)}), f32[128,128]{1,0:T(8,128)}) %reduce-scatter.8.cloned.1.call-update) | async-done | bytes 65552 | tf_op jit(solution)/shard_map/reduce_scatter | solution.py:36
  525.2 73.5 %reduce-scatter.4.cloned.1.call-done = f32[128,128]{1,0:T(8,128)} async-done(((f32[2048,128]{1,0:T(8,128)}), f32[128,128]{1,0:T(8,128)}) %reduce-scatter.4.cloned.1.call-update) | async-done | bytes 65552 | tf_op jit(solution)/shard_map/reduce_scatter | solution.py:30
Async XLA Ops:
  7.2 74.0 %all-gather.14.cloned.1.call-start = ((), (), s32[]{:S(2)}) async-start(), calls=%async_computation.7 | async-start | bytes 1114112 | tf_op jit(solution)/shard_map/all_gather | solution.py:45
  7.9 141.6 %all-gather.10.cloned.1.call-start = ((), (), s32[]{:S(2)}) async-start(), calls=%async_computation.5 | async-start | bytes 1114112 | tf_op jit(solution)/shard_map/all_gather | solution.py:44
  8.6 209.4 %all-gather.6.cloned.1.call-start = ((), (), s32[]{:S(2)}) async-start(), calls=%async_computation.3 | async-start | bytes 1114112 | tf_op jit(solution)/shard_map/all_gather | solution.py:43
  9.4 258.6 %all-gather.8.cloned.1.call-start = ((), (), s32[]{:S(2)}) async-start(), calls=%async_computation.4 | async-start | bytes 1114112 | tf_op jit(solution)/shard_map/all_gather | solution.py:50
  10.0 309.3 %all-gather.12.cloned.1.call-start = ((), (), s32[]{:S(2)}) async-start(), calls=%async_computation.6 | async-start | bytes 1114112 | tf_op jit(solution)/shard_map/all_gather | solution.py:51
  10.5 435.8 %reduce-scatter.6.cloned.1.call-start = ((), (), s32[]{:S(2)}) async-start(), calls=%async_computation.9 | async-start | bytes 1114112 | tf_op jit(solution)/shard_map/reduce_scatter | solution.py:35
  149.5 169.7 %copy-start.1 = (f32[2048,128]{1,0:T(8,128)S(1)}, f32[2048,128]{1,0:T(8,128)}, u32[]{:S(2)}) copy-start(f32[2048,128]{1,0:T(8,128)} %all-gather.10.cloned.1.call-done) | copy-start | bytes 3145732
  338.3 5.7 copy-start
  372.7 31.8 %copy-start.2 = (f32[2048,128]{1,0:T(8,128)S(1)}, f32[2048,128]{1,0:T(8,128)}, u32[]{:S(2)}) copy-start(f32[2048,128]{1,0:T(8,128)} %all-gather.8.cloned.1.call-done) | copy-start | bytes 3145732
  372.7 152.5 %reduce-scatter.8.cloned.1.call-start = ((), (), s32[]{:S(2)}) async-start(), calls=%async_computation.10 | async-start | bytes 1114112 | tf_op jit(solution)/shard_map/reduce_scatter | solution.py:36
  404.4 194.3 %reduce-scatter.4.cloned.1.call-start = ((), (), s32[]{:S(2)}) async-start(), calls=%async_computation.8 | async-start | bytes 1114112 | tf_op jit(solution)/shard_map/reduce_scatter | solution.py:30
Sparse Core Ops, SparseCore 0:
  9.8 71.3 all-gather.13
  83.0 66.5 all-gather.9
  151.3 66.6 all-gather.5
  220.6 47.3 all-gather.7
  270.6 48.6 all-gather.11
  372.8 73.4 reduce-scatter.5
  451.6 73.6 reduce-scatter.7
  528.3 70.3 reduce-scatter.3
where the time goes:
time: 606 us
  waiting for transfers between devices  434 us (72%)
  matrix products  114 us (19%)
  blocking collectives  35.3 us (6%)
  between operations  14.2 us (2%)
    dot_general x5, matrix products, dot_full(): jnp.dot(a, b, precision=lax.Precision.HIGHEST, preferred_element_type=jnp...  114 us
    reduce_scatter x1, waiting for transfers between devices, send_key_grads(): lax.psum_scatter(v_part, 'pb', scatter_dimension=0, tiled=True)  78.8 us
    reduce_scatter x1, waiting for transfers between devices, send_query_grad(): lax.psum_scatter(partial_value, 'ka', scatter_dimension=0, tiled=True)  73.5 us
    all_gather x1, waiting for transfers between devices, on_device(): lax.all_gather(out_grad, 'ka', axis=0, tiled=True)  68.3 us
    all_gather x1, waiting for transfers between devices, on_device(): lax.all_gather(query, 'ka', axis=0, tiled=True)  65.9 us
    all_gather x1, waiting for transfers between devices, on_device(): lax.all_gather(keys, 'pb', axis=0, tiled=True)  50 us
    all_gather x1, blocking collectives, on_device(): lse_blk = lax.all_gather(row_lse, 'ka', axis=1, tiled=True)  35.3 us
    all_gather x1, waiting for transfers between devices, on_device(): lax.all_gather(attn_out, 'ka', axis=0, tiled=True)  35.3 us
  transfers between devices with their start and end apart: 8, of which 8 were waited for; matrix products, arithmetic and copies ran while one was open for 11% of the time, Pallas kernels for 0%

commit v1 on v0

v1 whole, which is shorter than its diff:
```python
import functools
import math

import jax
import jax.numpy as jnp
from jax import lax
from jax.experimental import pallas as pl
from jax.experimental.pallas import tpu as pltpu
from jax.sharding import Mesh, PartitionSpec as P

D = 128
SCALE = 1.0 / math.sqrt(D)
LOG2E = math.log2(math.e)
LN2 = math.log(2.0)
BF16 = jnp.bfloat16
F32 = jnp.float32

AXES = ("xh", "y", "c", "xl", "z")
PLANE = ("xh", "y", "xl")
COLUMN = ("c", "z")
ROWS = 128
BLOCKS = 16
TOKENS = ROWS * BLOCKS
PACK = 2 * ROWS + 8
KEY_BLOCKS = 4
TK = KEY_BLOCKS * ROWS
TQ = 512


def split(x):
    high = x.astype(BF16)
    return high, (x - high.astype(F32)).astype(BF16)


def split3(x):
    a = x.astype(BF16)
    rest = x - a.astype(F32)
    b = rest.astype(BF16)
    return a, b, (rest - b.astype(F32)).astype(BF16)


def dot(a, b):
    return jnp.dot(a, b, preferred_element_type=F32)


def load_queries(qg_ref, base, factor, row_at, row_factor, turned, wide, narrow):
    zeros = jnp.zeros((ROWS, ROWS), BF16)
    sub = lax.broadcasted_iota(jnp.int32, (ROWS, ROWS), 0)
    for b in range(BLOCKS):
        at = slice(b * ROWS, (b + 1) * ROWS)
        x = qg_ref[b, base : base + ROWS, :] * factor
        high, low = split(x)
        wide[at, :ROWS] = high
        wide[at, ROWS:] = low
        narrow[at, :ROWS] = high
        narrow[at, ROWS:] = zeros
        high, low = split(x.T)
        turned[:ROWS, at] = high
        turned[ROWS : 2 * ROWS, at] = low
        turned[2 * ROWS : 3 * ROWS, at] = high
        first, second, third = split3(qg_ref[b, row_at : row_at + 1, :] * -row_factor)
        tail = jnp.where(
            sub == 0,
            first.astype(F32),
            jnp.where(sub == 1, second.astype(F32), jnp.where(sub == 2, third.astype(F32), 0.0)),
        )
        turned[3 * ROWS :, at] = tail.astype(BF16)


def tile_kernel(
    core_ref, qg_ref, kv_ref, dq_ref, theirs_ref, mine_ref, qt, gt, q_wide, q_narrow, g_wide, g_narrow, dqt
):
    step = pl.program_id(0)
    steps = BLOCKS // KEY_BLOCKS

    @pl.when(step == 0)
    def _():
        load_queries(qg_ref, 0, SCALE * LOG2E, 2 * ROWS, LOG2E, qt, q_wide, q_narrow)
        load_queries(qg_ref, ROWS, 1.0, 2 * ROWS + 1, 1.0, gt, g_wide, g_narrow)
        dqt[...] = jnp.zeros_like(dqt)

    ones = (lax.broadcasted_iota(jnp.int32, (TK, ROWS), 1) < 3).astype(F32).astype(BF16)
    k = kv_ref[:, :ROWS, :].reshape(TK, D)
    v = kv_ref[:, ROWS:, :].reshape(TK, D)
    k_high, k_low = split(k)
    v_high, v_low = split(v)
    k_all = jnp.concatenate([k_high, k_high, k_low, ones], 1)
    v_all = jnp.concatenate([v_high, v_high, v_low, ones], 1)
    kt_high, kt_low = split(k.T)
    kt_both = jnp.concatenate([kt_high, kt_low], 0)
    dv = jnp.zeros((TK, 2 * D), F32)
    dk = jnp.zeros((TK, 2 * D), F32)
    for j in range(TOKENS // TQ):
        at = slice(j * TQ, (j + 1) * TQ)
        probs = jnp.exp2(dot(k_all, qt[:, at]))
        dprob = dot(v_all, gt[:, at])
        high, low = split(probs)
        dv += dot(high, g_wide[at, :]) + dot(low, g_narrow[at, :])
        high, low = split(probs * dprob)
        dk += dot(high, q_wide[at, :]) + dot(low, q_narrow[at, :])
        part = dot(kt_both, high)
        dqt[:, at] = dqt[:, at] + (part[:D] + part[D:] + dot(kt_high, low))
    dk = (dk[:, :D] + dk[:, D:]) * LN2
    dv = dv[:, :D] + dv[:, D:]

    def store(ref):
        ref[:, :ROWS, :] = dk.reshape(KEY_BLOCKS, ROWS, D)
        ref[:, ROWS:, :] = dv.reshape(KEY_BLOCKS, ROWS, D)

    @pl.when(step < steps // 2)
    def _():
        store(theirs_ref)

    @pl.when(step >= steps // 2)
    def _():
        store(mine_ref)

    @pl.when(step == steps - 1)
    def _():
        for b in range(BLOCKS):
            dq_ref[b] = (dqt[:, b * ROWS : (b + 1) * ROWS] * SCALE).T


def tile_grads(core, qg, kv):
    steps = BLOCKS // KEY_BLOCKS
    half = steps // 2
    block = (KEY_BLOCKS, 2 * ROWS, D)
    grid_spec = pltpu.PrefetchScalarGridSpec(
        num_scalar_prefetch=1,
        grid=(steps,),
        in_specs=[
            pl.BlockSpec((BLOCKS, PACK, D), lambda i, c: (0, 0, 0)),
            pl.BlockSpec(block, lambda i, c: ((i + half * (1 - c[0])) % steps, 0, 0)),
        ],
        out_specs=[
            pl.BlockSpec((BLOCKS, ROWS, D), lambda i, c: (0, 0, 0)),
            pl.BlockSpec(block, lambda i, c: (jnp.minimum(i, half - 1), 0, 0)),
            pl.BlockSpec(block, lambda i, c: (jnp.maximum(i - half, 0), 0, 0)),
        ],
        scratch_shapes=[pltpu.VMEM((4 * ROWS, TOKENS), BF16)] * 2
        + [pltpu.VMEM((TOKENS, 2 * D), BF16)] * 4
        + [pltpu.VMEM((D, TOKENS), F32)],
    )
    return pl.pallas_call(
        tile_kernel,
        grid_spec=grid_spec,
        out_shape=[
            jax.ShapeDtypeStruct((BLOCKS, ROWS, D), F32),
            jax.ShapeDtypeStruct((BLOCKS // 2, 2 * ROWS, D), F32),
            jax.ShapeDtypeStruct((BLOCKS // 2, 2 * ROWS, D), F32),
        ],
        compiler_params=pltpu.CompilerParams(vmem_limit_bytes=48 * 1024 * 1024),
        cost_estimate=pl.CostEstimate(flops=20 * 2 * TOKENS * TOKENS * D, bytes_accessed=8 << 20, transcendentals=TOKENS * TOKENS),
    )(core, qg, kv)


def on_device(query, keys, values, attn_out, out_grad, row_lse):
    delta = jnp.sum(out_grad * attn_out, axis=-1)[None, :]
    pack = jnp.concatenate([query, out_grad, row_lse, delta, jnp.zeros((6, D), F32)], 0)
    kv = lax.all_gather(jnp.concatenate([keys, values], 0)[None], COLUMN, axis=0, tiled=True)
    qg = lax.all_to_all(jnp.broadcast_to(pack[None], (BLOCKS, PACK, D)), PLANE, 0, 0)
    core = lax.axis_index("c")
    dq, theirs, mine = tile_grads(core.astype(jnp.int32)[None], qg, kv)
    dkv = mine + lax.ppermute(theirs, "c", [(0, 1), (1, 0)])
    dkv = lax.psum_scatter(dkv, "z", scatter_dimension=0, tiled=True)
    dq = jnp.sum(lax.all_to_all(dq, PLANE, 0, 0), axis=0)
    return dq, dkv[0, :ROWS], dkv[0, ROWS:]


def solution(mesh):
    fine = Mesh(mesh.devices.reshape(2, 4, 2, 2, 8), AXES)
    rows = P(("xh", "y", "c", "xl", "z"), None)
    cols = P(("xl", "z", "xh", "y", "c"), None)
    return jax.shard_map(
        on_device,
        mesh=fine,
        in_specs=(rows, cols, cols, rows, rows, P(None, ("xh", "y", "c", "xl", "z"))),
        out_specs=(rows, cols, cols),
        check_vma=False,
    )
```

time: 606 us -> 134 us (0.22)
  waiting for transfers between devices: 434 us -> 51.6 us
  matrix products: 114 us -> 0 us
  Pallas kernels: 0 us -> 25.2 us
  blocking collectives: 35.3 us -> 23 us
  starting transfers between devices: 0.31 us -> 7.64 us
    all_gather x5 -> x1, waiting for transfers between devices: 253 us -> 0.79 us  [on_device(): lax.all_gather(jnp.concatenate([keys, values], 0)[None], COLUMN, axis=0,...]
    reduce_scatter x3 -> x1, waiting for transfers between devices: 177 us -> 17.7 us  [on_device(): dkv = lax.psum_scatter(dkv, 'z', scatter_dimension=0, tiled=True)]
    dot_general x5 -> x0, matrix products: 114 us -> none  [dot_full(): jnp.dot(a, b, precision=lax.Precision.HIGHEST, preferred_element_type=jnp...]
    all_gather x1 -> x0, blocking collectives: 35.3 us -> none  [on_device(): lse_blk = lax.all_gather(row_lse, 'ka', axis=1, tiled=True)]
    all_to_all x0 -> x1, waiting for transfers between devices: none -> 30.4 us  [on_device(): lax.all_to_all(jnp.broadcast_to(pack[None], (BLOCKS, PACK, D)), PLANE, 0, 0)]
    pallas_call x0 -> x1, Pallas kernels: none -> 25.2 us  [tile_grads(): pl.pallas_call(tile_kernel, grid_spec=grid_spec, out_shape=[jax.ShapeDtyp...]
    all_to_all x0 -> x1, blocking collectives: none -> 23 us  [on_device(): dq = jnp.sum(lax.all_to_all(dq, PLANE, 0, 0), axis=0)]
    all_to_all x0 -> x1, starting transfers between devices: none -> 7.48 us  [on_device(): lax.all_to_all(jnp.broadcast_to(pack[None], (BLOCKS, PACK, D)), PLANE, 0, 0)]
  transfers between devices with their start and end apart: 8 -> 4, of which waited for: 8 -> 4; matrix products, arithmetic and copies ran while one was open for 11% -> 4% of each run, Pallas kernels for 0% -> 0%
where the time goes in v1:
time: 134 us; the launch traced here: 133 us
  waiting for transfers between devices  51.6 us (39%)
  Pallas kernels  25.2 us (19%)
  blocking collectives  23 us (17%)
  between operations  14.1 us (11%)
  starting transfers between devices  7.64 us (6%)
  local copies, waits for them, and re-layouts  7.57 us (6%)
  other arithmetic  4.26 us (3%)
    all_to_all x1, waiting for transfers between devices, on_device(): lax.all_to_all(jnp.broadcast_to(pack[None], (BLOCKS, PACK, D)), PLANE, 0, 0)  30.4 us
    pallas_call x1, Pallas kernels, tile_grads(): pl.pallas_call(tile_kernel, grid_spec=grid_spec, out_shape=[jax.ShapeDtyp...  25.2 us
    all_to_all x1, blocking collectives, on_device(): dq = jnp.sum(lax.all_to_all(dq, PLANE, 0, 0), axis=0)  23 us
    reduce_scatter x1, waiting for transfers between devices, on_device(): dkv = lax.psum_scatter(dkv, 'z', scatter_dimension=0, tiled=True)  17.7 us
    all_to_all x1, starting transfers between devices, on_device(): lax.all_to_all(jnp.broadcast_to(pack[None], (BLOCKS, PACK, D)), PLANE, 0, 0)  7.48 us
  transfers between devices with their start and end apart: 4, of which 4 were waited for; matrix products, arithmetic and copies ran while one was open for 4% of the time, Pallas kernels for 0%

profile of v1, /device:TPU:2, one launch (start us, length us, event | category | flops | bytes accessed | tf_op | source)
XLA Modules:
  0.0 133.3 jit_solution(15918636279418437660)
XLA Ops:
  7.2 0.0 all-gather.3.cloned.1.call-start
  7.2 1.5 %pad_maximum_fusion = f32[256,128]{1,0:T(8,128)} fusion(f32[128,128]{1,0:T(8,128)} %param.8, f32[128,128]{1,0:T(8,128)} %param.7), kind=kLoop, calls=%fused_computation | loop fusion | flops 32768 | bytes 262144 | tf_op jit(solution)/shard_map/concatenate | solution.py:160
  8.7 0.0 all-gather.3.cloned.1.call-update
  8.8 1.0 multiply_reduce_fusion
  9.8 2.4 %concatenate.6 = f32[264,128]{1,0:T(8,128)S(1)} concatenate(f32[128,128]{1,0:T(8,128)} %param.6, f32[128,128]{1,0:T(8,128)} %param.10, f32[1,128]{1,0:T(1,128)} %param.11, f32[1,128]{1,0:T(1,128)S(1)} %bitcast.8, f32[6,128]{1,0:T(8,128)S(1)} %broadcast_in_dim.20), dimensions={0} | concatenate | bytes 270336 | tf_op jit(solution)/shard_map/concatenate | solution.py:159
  12.1 1.5 %broadcast_in_dim.21 = f32[16,264,128]{2,1,0:T(8,128)} broadcast(f32[264,128]{1,0:T(8,128)S(1)} %concatenate.6), dimensions={1,2} | broadcast | bytes 2297856 | tf_op jit(solution)/shard_map/broadcast_in_dim | solution.py:161
  13.6 7.5 %all-to-all-start = ((f32[16,264,128]{2,1,0:T(8,128)}), f32[16,264,128]{2,1,0:T(8,128)S(1)}, u32[]{:S(2)}, u32[]{:S(2)}) async-start(f32[16,264,128]{2,1,0:T(8,128)} %broadcast_in_dim.21), calls=%async_computation | async-start | bytes 4325376 | tf_op jit(solution)/shard_map/all_to_all | solution.py:161
  21.1 0.0 reduce-scatter.2.cloned.1.call-start
  21.1 30.4 %all-to-all-done.qg_ref = f32[16,264,128]{2,1,0:T(8,128)S(1)} async-done(((f32[16,264,128]{2,1,0:T(8,128)}), f32[16,264,128]{2,1,0:T(8,128)S(1)}, u32[]{:S(2)}, u32[]{:S(2)}) %all-to-all-start) | async-done | bytes 2162720 | tf_op jit(solution)/shard_map/all_to_all | solution.py:161
  51.6 0.0 copy-start.1
  51.6 0.8 all-gather.3.cloned.1.call-done
  52.4 0.6 copy-done.1
  53.0 0.0 copy-start
  53.0 1.6 %copy-done = f32[4096,128]{1,0:T(8,128)S(1)} copy-done((f32[4096,128]{1,0:T(8,128)S(1)}, f32[4096,128]{1,0:T(8,128)}, u32[]{:S(2)}) %copy-start) | copy-done | bytes 2097176
  54.5 25.2 %shard_map.85 = (f32[16,128,128]{2,1,0:T(8,128)S(1)}, f32[8,256,128]{2,1,0:T(8,128)S(1)}, f32[8,256,128]{2,1,0:T(8,128)S(1)}) custom-call(s32[1]{0:T(128)} %bitcast.core_ref, f32[16,264,128]{2,1,0:T(8,128)} %copy-done.1, f32[16,256,128]{2,1,0:T(8,128)S(1)} %bitcast.7), custom_call_target="tpu_custom_call" | custom-call | flops 21474836480 | bytes 8388608 | tf_op jit(solution)/shard_map/pallas_call | solution.py:144
  79.8 0.1 collective-permute-start
  79.9 2.6 %collective-permute-done = f32[8,256,128]{2,1,0:T(8,128)S(1)} collective-permute-done((f32[8,256,128]{2,1,0:T(8,128)S(1)}, f32[8,256,128]{2,1,0:T(8,128)S(1)}, u32[]{:S(2)}, u32[]{:S(2)}) %collective-permute-start) | collective-permute-done | bytes 1048608 | tf_op jit(solution)/shard_map/ppermute | solution.py:164
  82.5 1.1 add.5
  83.6 0.0 reduce-scatter.2.cloned.1.call-update
  83.6 23.0 %all_to_all.10 = f32[16,128,128]{2,1,0:T(8,128)S(1)} all-to-all(f32[16,128,128]{2,1,0:T(8,128)S(1)} %get-tuple-element.6), channel_id=1, replica_groups=mesh['xh'=2,'y'=4,'c'=2,'xl'=2,'z'=8] {'xh','y','xl'}, dimensions={0} | all-to-all | bytes 2097152 | tf_op jit(solution)/shard_map/all_to_all | solution.py:166
  106.6 0.7 reduce_sum.19
  107.3 17.7 %reduce-scatter.2.cloned.1.call-done = f32[1,256,128]{2,1,0:T(8,128)} async-done(((f32[8,256,128]{2,1,0:T(8,128)}), f32[1,256,128]{2,1,0:T(8,128)}) %reduce-scatter.2.cloned.1.call-update) | async-done | bytes 131088 | tf_op jit(solution)/shard_map/reduce_scatter | solution.py:165
  125.0 1.5 %slice_bitcast_fusion = (f32[128,128]{1,0:T(8,128)}, f32[128,128]{1,0:T(8,128)}) fusion(f32[1,256,128]{2,1,0:T(8,128)} %reduce-scatter.2.cloned.1.call-done), kind=kLoop, calls=%fused_computation.1 | loop fusion | bytes 262144 | tf_op jit(solution)/shard_map/squeeze | solution.py:167
  (1 shorter events, 0.0 us)
Async XLA Ops:
  7.2 45.2 %all-gather.3.cloned.1.call-start = ((), (), s32[]{:S(2)}) async-start(), calls=%async_computation.4 | async-start | bytes 2228224 | tf_op jit(solution)/shard_map/all_gather | solution.py:160
  13.6 38.0 %all-to-all-start = ((f32[16,264,128]{2,1,0:T(8,128)}), f32[16,264,128]{2,1,0:T(8,128)S(1)}, u32[]{:S(2)}, u32[]{:S(2)}) async-start(f32[16,264,128]{2,1,0:T(8,128)} %broadcast_in_dim.21), calls=%async_computation | async-start | bytes 4325376 | tf_op jit(solution)/shard_map/all_to_all | solution.py:161
  21.1 103.9 %reduce-scatter.2.cloned.1.call-start = ((), (), s32[]{:S(2)}) async-start(), calls=%async_computation.3 | async-start | bytes 1179648 | tf_op jit(solution)/shard_map/reduce_scatter | solution.py:165
  51.6 1.4 %copy-start.1 = (f32[16,264,128]{2,1,0:T(8,128)}, f32[16,264,128]{2,1,0:T(8,128)S(1)}, u32[]{:S(2)}) copy-start(f32[16,264,128]{2,1,0:T(8,128)S(1)} %all-to-all-done.qg_ref) | copy-start | bytes 6488068
  53.0 1.6 %copy-start = (f32[4096,128]{1,0:T(8,128)S(1)}, f32[4096,128]{1,0:T(8,128)}, u32[]{:S(2)}) copy-start(f32[4096,128]{1,0:T(8,128)} %all-gather.3.cloned.1.call-done) | copy-start | bytes 6291460
  79.8 2.7 %collective-permute-start = (f32[8,256,128]{2,1,0:T(8,128)S(1)}, f32[8,256,128]{2,1,0:T(8,128)S(1)}, u32[]{:S(2)}, u32[]{:S(2)}) collective-permute-start(f32[8,256,128]{2,1,0:T(8,128)S(1)} %get-tuple-element.8), channel_id=1, source_target_pairs={{0,16},{16,0},{1,17},{17,1},{2,18},{18,2},{3,19},{19,3},{4,20},{20... | collective-permute-start | bytes 3145736 | tf_op jit(solution)/shard_map/ppermute | solution.py:164
Sparse Core Ops, SparseCore 0:
  9.8 42.5 all-gather.2
  83.7 41.1 reduce-scatter.1

commit v2 on v1

v2 whole, which is shorter than its diff:
```python
import math

import jax
import jax.numpy as jnp
from jax import lax
from jax.experimental import pallas as pl
from jax.experimental.pallas import tpu as pltpu
from jax.sharding import Mesh, PartitionSpec as P

D = 128
SCALE = 1.0 / math.sqrt(D)
LOG2E = math.log2(math.e)
LN2 = math.log(2.0)
BF16 = jnp.bfloat16
F32 = jnp.float32

AXES = ("xh", "y", "c", "xl", "z")
PLANE = ("xh", "y", "xl")
COLUMN = ("c", "z")
DEPTH = 8
ROWS = 128
HALF = ROWS // 2
BLOCKS = 16
TOKENS = ROWS * BLOCKS
PACK = 2 * ROWS + 8
CHUNKS = 4
TQ = TOKENS // CHUNKS
TK = BLOCKS * HALF

SWAP = [(0, 1), (1, 0)]


def shape(*dims, dtype=F32):
    return jax.ShapeDtypeStruct(dims, dtype)


def split(x):
    high = x.astype(BF16)
    return high, (x - high.astype(F32)).astype(BF16)


def split3(x):
    a = x.astype(BF16)
    rest = x - a.astype(F32)
    b = rest.astype(BF16)
    return a, b, (rest - b.astype(F32)).astype(BF16)


def dot(a, b):
    return jnp.dot(a, b, preferred_element_type=F32)


def pack_kernel(q, k, v, o, g, lse, own, copies):
    own[:ROWS] = q[...]
    own[ROWS : 2 * ROWS] = g[...]
    delta = jnp.sum((g[...] * o[...]).T, axis=0, keepdims=True)
    own[2 * ROWS :] = jnp.concatenate([lse[...], delta, jnp.zeros((6, D), F32)], 0)
    for b in range(BLOCKS):
        copies[b, :HALF] = k[:HALF]
        copies[b, HALF : 2 * HALF] = v[:HALF]
        copies[b, 2 * HALF : 3 * HALF] = k[HALF:]
        copies[b, 3 * HALF :] = v[HALF:]


def pack(query, keys, values, attn_out, out_grad, row_lse):
    return pl.pallas_call(pack_kernel, out_shape=[shape(PACK, D), shape(BLOCKS, 2 * ROWS, D)])(
        query, keys, values, attn_out, out_grad, row_lse
    )


def load_block(x_ref, base, factor, row_at, row_factor, at, turned, wide):
    x = x_ref[base : base + ROWS, :] * factor
    high, low = split(x)
    wide[at, :D] = high
    wide[at, D:] = low
    high, low = split(x.T)
    turned[:D, at] = high
    turned[D : 2 * D, at] = low
    turned[2 * D : 3 * D, at] = high
    a, b, c = split3(x_ref[row_at : row_at + 1, :] * -row_factor)
    sub = lax.broadcasted_iota(jnp.int32, (D, ROWS), 0)
    tail = jnp.where(sub == 0, a.astype(F32), jnp.where(sub == 1, b.astype(F32), jnp.where(sub == 2, c.astype(F32), 0.0)))
    turned[3 * D :, at] = tail.astype(BF16)


def tile_kernel(*refs):
    packs, kv_ref, mine, theirs, dkv_ref = refs[:BLOCKS], *refs[BLOCKS : BLOCKS + 4]
    qt, gt, q_wide, g_wide = refs[BLOCKS + 4 : BLOCKS + 8]
    ones = (lax.broadcasted_iota(jnp.int32, (TK, D), 1) < 3).astype(F32).astype(BF16)
    k = kv_ref[:, :HALF, :].reshape(TK, D)
    v = kv_ref[:, HALF:, :].reshape(TK, D)
    k_high, k_low = split(k)
    v_high, v_low = split(v)
    k_all = jnp.concatenate([k_high, k_high, k_low, ones], 1)
    v_all = jnp.concatenate([v_high, v_high, v_low, ones], 1)
    kt_high, kt_low = split(k.T)
    kt_both = jnp.concatenate([kt_high, kt_low], 0)
    dv = jnp.zeros((TK, 2 * D), F32)
    dk = jnp.zeros((TK, 2 * D), F32)
    for j in range(CHUNKS):
        for b in range(4 * j, 4 * j + 4):
            at = slice(b * ROWS, (b + 1) * ROWS)
            load_block(packs[b], 0, SCALE * LOG2E, 2 * ROWS, LOG2E, at, qt, q_wide)
            load_block(packs[b], ROWS, 1.0, 2 * ROWS + 1, 1.0, at, gt, g_wide)
        at = slice(j * TQ, (j + 1) * TQ)
        probs = jnp.exp2(dot(k_all, qt[:, at]))
        dprob = dot(v_all, gt[:, at])
        high, low = split(probs)
        dv += dot(high, g_wide[at, :]) + dot(low, g_wide[at, :])
        high, low = split(probs * dprob)
        dk += dot(high, q_wide[at, :]) + dot(low, q_wide[at, :])
        part = dot(kt_both, high)
        part = (part[:D] + part[D:] + dot(kt_high, low)) * SCALE
        for b in range(2):
            mine[j, b] = part[:, b * ROWS : (b + 1) * ROWS].T
            theirs[j, b] = part[:, (b + 2) * ROWS : (b + 3) * ROWS].T
    dkv_ref[:, :HALF, :] = ((dk[:, :D] + dk[:, D:]) * LN2).reshape(BLOCKS, HALF, D)
    dkv_ref[:, HALF:, :] = (dv[:, :D] + dv[:, D:]).reshape(BLOCKS, HALF, D)


def tile_grads(packs, kv, at):
    half = (CHUNKS, 2, ROWS, D)
    return pl.pallas_call(
        tile_kernel,
        grid=(1,),
        in_specs=[pl.BlockSpec((PACK, D), lambda i: (0, 0))] * BLOCKS + [pl.BlockSpec((BLOCKS, ROWS, D), lambda i: (0, at, 0))],
        out_specs=[
            pl.BlockSpec(half, lambda i: (0, 0, 0, 0)),
            pl.BlockSpec(half, lambda i: (0, 0, 0, 0)),
            pl.BlockSpec((BLOCKS, ROWS, D), lambda i: (0, 0, 0)),
        ],
        out_shape=[shape(*half), shape(*half), shape(BLOCKS, ROWS, D)],
        scratch_shapes=[pltpu.VMEM((4 * D, TOKENS), BF16)] * 2 + [pltpu.VMEM((TOKENS, 2 * D), BF16)] * 2,
        compiler_params=pltpu.CompilerParams(vmem_limit_bytes=32 * 1024 * 1024),
        cost_estimate=pl.CostEstimate(flops=12_000_000_000, bytes_accessed=8 << 20, transcendentals=TOKENS * TK),
    )(*packs, kv)


def swap(x):
    return lax.ppermute(x, "c", SWAP)


def along(x, step):
    pairs = [(z, (z + step) % DEPTH) for z in range(DEPTH)]
    pairs += [(DEPTH + z, DEPTH + (z - step) % DEPTH) for z in range(DEPTH)]
    return lax.ppermute(x, COLUMN, pairs)


def on_device(query, keys, values, attn_out, out_grad, row_lse):
    own, kv = pack(query, keys, values, attn_out, out_grad, row_lse)
    kv = lax.all_to_all(kv, PLANE, 0, 0)
    other = swap(own)
    a, b = own, other
    packs = []
    for j in range(1, CHUNKS):
        a, b = along(a, 1), along(b, 1)
        packs += [swap(b), swap(a), b, a]
    far = along(a, 1)
    packs = [own, far, other, swap(far)] + packs
    packs = [pltpu.with_memory_space_constraint(x, pltpu.HBM) for x in packs]
    kv = pltpu.with_memory_space_constraint(kv, pltpu.HBM)
    mine1, theirs1, dkv1 = tile_grads(packs, kv, 0)
    dkv1 = lax.all_to_all(dkv1, PLANE, 0, 0)
    mine2, theirs2, dkv2 = tile_grads(packs, kv, 1)
    theirs2, dkv1 = lax.optimization_barrier((theirs2, dkv1))
    dq = (mine1 + swap(theirs1)) + (mine2 + swap(theirs2))
    r1 = along(dq[1], 1)
    r2 = along(dq[2], 2)
    r3 = along(dq[3], 3)
    r4 = along(dq[0, 1], 4)
    dkv2 = lax.all_to_all(dkv2, PLANE, 0, 0)
    r1, r2, r3, r4, dkv2 = lax.optimization_barrier((r1, r2, r3, r4, dkv2))
    query_grad = (dq[0, 0] + r4) + (r1[0] + r2[0] + r3[0]) + swap(r1[1] + r2[1] + r3[1])
    s1 = jnp.sum(dkv1, axis=0)
    s2 = jnp.sum(dkv2, axis=0)
    key_grad = jnp.concatenate([s1[:HALF], s2[:HALF]], 0)
    value_grad = jnp.concatenate([s1[HALF:], s2[HALF:]], 0)
    return query_grad, key_grad, value_grad


def solution(mesh):
    fine = Mesh(mesh.devices.reshape(2, 4, 2, 2, DEPTH), AXES)
    rows = P(("xh", "y", "c", "xl", "z"), None)
    cols = P(("xl", "z", "xh", "y", "c"), None)
    return jax.shard_map(
        on_device,
        mesh=fine,
        in_specs=(rows, cols, cols, rows, rows, P(None, ("xh", "y", "c", "xl", "z"))),
        out_specs=(rows, cols, cols),
        check_vma=False,
    )
```

time: 134 us -> 111 us (0.83)
  starting transfers between devices: 7.64 us -> 37 us
  blocking collectives: 23 us -> 0 us
  waiting for transfers between devices: 51.6 us -> 35.2 us
  between operations: 14.1 us -> 0.86 us
  local copies, waits for them, and re-layouts: 7.57 us -> 2.49 us
  Pallas kernels: 25.2 us -> 30.2 us
    ppermute x1 -> x22, waiting for transfers between devices: 2.65 us -> 27.9 us  [the longest x11 27.3 us: along(): return lax.ppermute(x, COLUMN, pairs)]
    all_to_all x1 -> x3, waiting for transfers between devices: 30.4 us -> 7.23 us  [the longest x1 4.23 us: on_device(): dkv2 = lax.all_to_all(dkv2, PLANE, 0, 0)]
    all_to_all x1 -> x0, blocking collectives: 23 us -> none  [on_device(): dq = jnp.sum(lax.all_to_all(dq, PLANE, 0, 0), axis=0)]
    reduce_scatter x1 -> x0, waiting for transfers between devices: 17.7 us -> none  [on_device(): dkv = lax.psum_scatter(dkv, 'z', scatter_dimension=0, tiled=True)]
    ppermute x1 -> x22, starting transfers between devices: 0.09 us -> 16.5 us  [the longest x11 12.8 us: along(): return lax.ppermute(x, COLUMN, pairs)]
    all_to_all x1 -> x3, starting transfers between devices: 7.48 us -> 20.6 us  [the longest x1 7.61 us: on_device(): kv = lax.all_to_all(kv, PLANE, 0, 0)]
    pallas_call x1 -> x3, Pallas kernels: 25.2 us -> 30.2 us  [the longest x2 27.7 us: tile_grads(): pl.pallas_call(tile_kernel, grid=(1,), in_specs=[pl.BlockSpec((PACK, D),...]
    concatenate x1 -> x0, local copies, waits for them, and re-layouts: 2.36 us -> none  [on_device(): jnp.concatenate([query, out_grad, row_lse, delta, jnp.zeros((6, D), F32)]...]
  transfers between devices with their start and end apart: 4 -> 25, of which waited for: 4 -> 13; matrix products, arithmetic and copies ran while one was open for 4% -> 3% of each run, Pallas kernels for 0% -> 13%
where the time goes in v2:
time: 111 us; the launch traced here: 110 us
  starting transfers between devices  37 us (33%)
  waiting for transfers between devices  35.2 us (32%)
  Pallas kernels  30.2 us (27%)
  other arithmetic  3.97 us (4%)
  local copies, waits for them, and re-layouts  2.49 us (2%)
    pallas_call x2, Pallas kernels, tile_grads(): pl.pallas_call(tile_kernel, grid=(1,), in_specs=[pl.BlockSpec((PACK, D),...  27.7 us
    ppermute x11, waiting for transfers between devices, along(): return lax.ppermute(x, COLUMN, pairs)  27.3 us
    ppermute x11, starting transfers between devices, along(): return lax.ppermute(x, COLUMN, pairs)  12.8 us
    all_to_all x1, starting transfers between devices, on_device(): kv = lax.all_to_all(kv, PLANE, 0, 0)  7.61 us
    all_to_all x1, starting transfers between devices, on_device(): dkv1 = lax.all_to_all(dkv1, PLANE, 0, 0)  7.07 us
    all_to_all x1, starting transfers between devices, on_device(): dkv2 = lax.all_to_all(dkv2, PLANE, 0, 0)  5.89 us
    all_to_all x1, waiting for transfers between devices, on_device(): dkv2 = lax.all_to_all(dkv2, PLANE, 0, 0)  4.23 us
    ppermute x11, starting transfers between devices, swap(): return lax.ppermute(x, 'c', SWAP)  3.7 us
  transfers between devices with their start and end apart: 25, of which 13 were waited for; matrix products, arithmetic and copies ran while one was open for 3% of the time, Pallas kernels for 13%

profile of v2, /device:TPU:2, one launch (start us, length us, event | category | flops | bytes accessed | tf_op | source)
XLA Modules:
  0.0 109.7 jit_solution(17756713279172359922)
XLA Ops:
  0.6 2.5 %shard_map.85 = (f32[264,128]{1,0:T(8,128)}, f32[16,256,128]{2,1,0:T(8,128)}) custom-call(f32[128,128]{1,0:T(8,128)} %q.1, f32[128,128]{1,0:T(8,128)} %k.1, f32[128,128]{1,0:T(8,128)} %v.1, f32[128,128]{1,0:T(8,128)} %o.1, f32[128,128]{1,0:T(8,128)} %g.1, f32[1,128]{1,0:T(1,128)} %lse.1), custom_call_target="tpu_custom_call" | custom-call | tf_op jit(solution)/shard_map/pallas_call | solution.py:66
  3.1 7.6 %all-to-all-start = ((f32[16,256,128]{2,1,0:T(8,128)}), f32[16,256,128]{2,1,0:T(8,128)}, u32[]{:S(2)}, u32[]{:S(2)}) async-start(f32[16,256,128]{2,1,0:T(8,128)} %get-tuple-element.19), calls=%async_computation | async-start | bytes 4194304 | tf_op jit(solution)/shard_map/all_to_all | solution.py:151
  10.8 0.1 collective-permute-start.4
  10.9 2.0 %collective-permute-start = (f32[264,128]{1,0:T(8,128)S(1)}, f32[264,128]{1,0:T(8,128)S(1)}, u32[]{:S(2)}, u32[]{:S(2)}) collective-permute-start(f32[264,128]{1,0:T(8,128)S(1)} %copy-done.1), channel_id=1, source_target_pairs={{0,1},{1,2},{2,3},{3,4},{4,5},{5,6},{6,7},{7,0},{16,23},{17,16},{1... | collective-permute-start | bytes 405512 | tf_op jit(solution)/shard_map/ppermute | solution.py:146
  12.9 0.0 collective-permute-done.4.refs_2_
  12.9 1.9 %collective-permute-start.6 = (f32[264,128]{1,0:T(8,128)S(1)}, f32[264,128]{1,0:T(8,128)S(1)}, u32[]{:S(2)}, u32[]{:S(2)}) collective-permute-start(f32[264,128]{1,0:T(8,128)S(1)} %collective-permute-done.4.refs_2_), channel_id=1, source_target_pairs={{0,1},{1,2},{2,3},{3,4},{4,5},{5,6},{6,7},{7,0},{16,23},{17,16},{1... | collective-permute-start | bytes 405512 | tf_op jit(solution)/shard_map/ppermute | solution.py:146
  14.8 5.0 %collective-permute-done.refs_7_ = f32[264,128]{1,0:T(8,128)S(1)} collective-permute-done((f32[264,128]{1,0:T(8,128)S(1)}, f32[264,128]{1,0:T(8,128)S(1)}, u32[]{:S(2)}, u32[]{:S(2)}) %collective-permute-start) | collective-permute-done | bytes 135200 | tf_op jit(solution)/shard_map/ppermute | solution.py:146
  19.8 0.0 collective-permute-start.1
  19.8 1.4 %collective-permute-done.6.refs_6_ = f32[264,128]{1,0:T(8,128)S(1)} collective-permute-done((f32[264,128]{1,0:T(8,128)S(1)}, f32[264,128]{1,0:T(8,128)S(1)}, u32[]{:S(2)}, u32[]{:S(2)}) %collective-permute-start.6) | collective-permute-done | bytes 135200 | tf_op jit(solution)/shard_map/ppermute | solution.py:146
  21.2 0.0 collective-permute-start.9
  21.2 4.8 %collective-permute-done.1.refs_11_ = f32[264,128]{1,0:T(8,128)S(1)} collective-permute-done((f32[264,128]{1,0:T(8,128)S(1)}, f32[264,128]{1,0:T(8,128)S(1)}, u32[]{:S(2)}, u32[]{:S(2)}) %collective-permute-start.1) | collective-permute-done | bytes 135200 | tf_op jit(solution)/shard_map/ppermute | solution.py:146
  26.0 0.0 collective-permute-start.2
  26.0 1.9 %collective-permute-start.8 = (f32[264,128]{1,0:T(8,128)S(1)}, f32[264,128]{1,0:T(8,128)S(1)}, u32[]{:S(2)}, u32[]{:S(2)}) collective-permute-start(f32[264,128]{1,0:T(8,128)S(1)} %collective-permute-done.refs_7_), channel_id=1, source_target_pairs={{0,16},{16,0},{1,17},{17,1},{2,18},{18,2},{3,19},{19,3},{4,20},{20... | collective-permute-start | bytes 405512 | tf_op jit(solution)/shard_map/ppermute | solution.py:140
  27.9 0.1 collective-permute-start.12
  28.0 4.2 %collective-permute-done.2.refs_15_ = f32[264,128]{1,0:T(8,128)S(1)} collective-permute-done((f32[264,128]{1,0:T(8,128)S(1)}, f32[264,128]{1,0:T(8,128)S(1)}, u32[]{:S(2)}, u32[]{:S(2)}) %collective-permute-start.2) | collective-permute-done | bytes 135200 | tf_op jit(solution)/shard_map/ppermute | solution.py:146
  32.2 1.1 %collective-permute-start.11 = (f32[264,128]{1,0:T(8,128)S(1)}, f32[264,128]{1,0:T(8,128)S(1)}, u32[]{:S(2)}, u32[]{:S(2)}) collective-permute-start(f32[264,128]{1,0:T(8,128)S(1)} %collective-permute-done.1.refs_11_), channel_id=1, source_target_pairs={{0,16},{16,0},{1,17},{17,1},{2,18},{18,2},{3,19},{19,3},{4,20},{20... | collective-permute-start | bytes 405512 | tf_op jit(solution)/shard_map/ppermute | solution.py:140
  33.4 0.1 collective-permute-start.10
  33.5 0.4 collective-permute-start.14
  33.9 0.3 collective-permute-done.12.refs_14_
  34.2 4.3 %collective-permute-done.3.refs_1_ = f32[264,128]{1,0:T(8,128)S(1)} collective-permute-done((f32[264,128]{1,0:T(8,128)S(1)}, f32[264,128]{1,0:T(8,128)S(1)}, u32[]{:S(2)}, u32[]{:S(2)}) %collective-permute-start.3) | collective-permute-done | bytes 135200 | tf_op jit(solution)/shard_map/ppermute | solution.py:146
  38.5 0.0 collective-permute-start.5
  38.5 0.7 copy-done.12
  39.2 0.1 copy-done.13
  39.2 0.0 copy-done.14
  39.3 0.6 copy-done.15
  39.9 0.0 collective-permute-done.5.refs_3_
  39.9 0.5 all-to-all-done.refs_16_
  40.5 13.8 %shard_map.86 = (f32[4,2,128,128]{3,2,1,0:T(8,128)S(1)}, f32[4,2,128,128]{3,2,1,0:T(8,128)S(1)}, f32[16,128,128]{2,1,0:T(8,128)}) custom-call(f32[264,128]{1,0:T(8,128)} %get-tuple-element.18.refs_0_, f32[264,128]{1,0:T(8,128)} %copy-done.11, f32[264,128]{1,0:T(8,128)} %copy-done.2, f32[264,128]{1,0:T(8,128)} %collective-permute-done.5.refs_3_, ...), custom_call_target="tpu_custom_call" | custom-call | flops 12000000000 | bytes 8388608 | tf_op jit(solution)/shard_map/pallas_call | solution.py:123
  54.3 7.1 %all-to-all-start.1 = ((f32[16,128,128]{2,1,0:T(8,128)}), f32[16,128,128]{2,1,0:T(8,128)S(1)}, u32[]{:S(2)}, u32[]{:S(2)}) async-start(f32[16,128,128]{2,1,0:T(8,128)} %get-tuple-element.24), calls=%async_computation.1 | async-start | bytes 2097152 | tf_op jit(solution)/shard_map/all_to_all | solution.py:163
  61.4 0.0 collective-permute-start.15
  61.4 13.8 %shard_map.87 = (f32[4,2,128,128]{3,2,1,0:T(8,128)S(1)}, f32[4,2,128,128]{3,2,1,0:T(8,128)S(1)}, f32[16,128,128]{2,1,0:T(8,128)}) custom-call(f32[264,128]{1,0:T(8,128)} %get-tuple-element.18.refs_0_, f32[264,128]{1,0:T(8,128)} %copy-done.11, f32[264,128]{1,0:T(8,128)} %copy-done.2, f32[264,128]{1,0:T(8,128)} %collective-permute-done.5.refs_3_, ...), custom_call_target="tpu_custom_call" | custom-call | flops 12000000000 | bytes 8388608 | tf_op jit(solution)/shard_map/pallas_call | solution.py:123
  75.3 2.5 %all-to-all-done.1 = f32[16,128,128]{2,1,0:T(8,128)S(1)} async-done(((f32[16,128,128]{2,1,0:T(8,128)}), f32[16,128,128]{2,1,0:T(8,128)S(1)}, u32[]{:S(2)}, u32[]{:S(2)}) %all-to-all-start.1) | async-done | bytes 1048608 | tf_op jit(solution)/shard_map/all_to_all | solution.py:163
  77.8 1.0 copy-done
  78.8 5.9 %all-to-all-start.2 = ((f32[16,128,128]{2,1,0:T(8,128)}), f32[16,128,128]{2,1,0:T(8,128)S(1)}, u32[]{:S(2)}, u32[]{:S(2)}) async-start(f32[16,128,128]{2,1,0:T(8,128)} %get-tuple-element.26), calls=%async_computation.2 | async-start | bytes 2097152 | tf_op jit(solution)/shard_map/all_to_all | solution.py:171
  84.7 1.3 %reduce_sum.18 = f32[128,128]{1,0:T(8,128)S(1)} reduce(f32[16,128,128]{2,1,0:T(8,128)} %copy-done, f32[]{:T(128)} %constant.0.clone.1), dimensions={0}, to_apply=%region_0.0 | reduce | flops 245760 | bytes 1114116 | tf_op jit(solution)/shard_map/reduce_sum | solution.py:174
  86.0 1.3 %add_add_fusion = f32[4,2,128,128]{3,2,1,0:T(8,128)S(1)} fusion(f32[4,2,128,128]{3,2,1,0:T(8,128)S(1)} %get-tuple-element.22, f32[4,2,128,128]{3,2,1,0:T(8,128)} %collective-permute-done.16, f32[4,2,128,128]{3,2,1,0:T(8,128)S(1)} %get-tuple-element.20, f32[4,2,128,128]{3,2,1,0:T(8,128)} %collective-permute-done.15), kind=kLoop, calls=%fused_computation | loop fusion | flops 393216 | bytes 2621440 | tf_op jit(solution)/shard_map/add | solution.py:166
  87.3 6.1 %collective-permute-start.20 = (f32[128,128]{1,0:T(8,128)S(1)}, f32[128,128]{1,0:T(8,128)S(1)}, u32[]{:S(2)}, u32[]{:S(2)}) collective-permute-start(f32[128,128]{1,0:T(8,128)S(1)} %slice_bitcast_fusion.3), channel_id=1, source_target_pairs={{0,4},{1,5},{2,6},{3,7},{4,0},{5,1},{6,2},{7,3},{16,20},{17,21},{1... | collective-permute-start | bytes 196616 | tf_op jit(solution)/shard_map/ppermute | solution.py:146
  93.4 2.0 %collective-permute-start.19 = (f32[2,128,128]{2,1,0:T(8,128)S(1)}, f32[2,128,128]{2,1,0:T(8,128)S(1)}, u32[]{:S(2)}, u32[]{:S(2)}) collective-permute-start(f32[2,128,128]{2,1,0:T(8,128)S(1)} %get-tuple-element.33), channel_id=1, source_target_pairs={{0,3},{1,4},{2,5},{3,6},{4,7},{5,0},{6,1},{7,2},{16,21},{17,22},{1... | collective-permute-start | bytes 393224 | tf_op jit(solution)/shard_map/ppermute | solution.py:146
  95.4 0.7 collective-permute-start.17
  96.1 4.2 %all-to-all-done.2 = f32[16,128,128]{2,1,0:T(8,128)S(1)} async-done(((f32[16,128,128]{2,1,0:T(8,128)}), f32[16,128,128]{2,1,0:T(8,128)S(1)}, u32[]{:S(2)}, u32[]{:S(2)}) %all-to-all-start.2) | async-done | bytes 1048608 | tf_op jit(solution)/shard_map/all_to_all | solution.py:171
  100.3 4.5 %collective-permute-done.19 = f32[2,128,128]{2,1,0:T(8,128)S(1)} collective-permute-done((f32[2,128,128]{2,1,0:T(8,128)S(1)}, f32[2,128,128]{2,1,0:T(8,128)S(1)}, u32[]{:S(2)}, u32[]{:S(2)}) %collective-permute-start.19) | collective-permute-done | bytes 131104 | tf_op jit(solution)/shard_map/ppermute | solution.py:146
  104.9 0.9 collective-permute-done.18
  105.8 1.8 %collective-permute-done.17 = f32[2,128,128]{2,1,0:T(8,128)S(1)} collective-permute-done((f32[2,128,128]{2,1,0:T(8,128)S(1)}, f32[2,128,128]{2,1,0:T(8,128)S(1)}, u32[]{:S(2)}, u32[]{:S(2)}) %collective-permute-start.17) | collective-permute-done | bytes 131104 | tf_op jit(solution)/shard_map/ppermute | solution.py:146
  107.6 0.1 reduce_sum.19
  107.7 0.1 collective-permute-start.21
  107.8 0.7 pad_maximum_fusion
  108.5 0.6 collective-permute-done.21
  109.0 0.7 fusion.2
  (47 shorter events, 0.1 us)
Async XLA Ops:
  3.1 7.6 %copy-start.1 = (f32[264,128]{1,0:T(8,128)S(1)}, f32[264,128]{1,0:T(8,128)}, u32[]{:S(2)}) copy-start(f32[264,128]{1,0:T(8,128)} %get-tuple-element.18.refs_0_) | copy-start | bytes 405508
  3.1 37.3 %all-to-all-start = ((f32[16,256,128]{2,1,0:T(8,128)}), f32[16,256,128]{2,1,0:T(8,128)}, u32[]{:S(2)}, u32[]{:S(2)}) async-start(f32[16,256,128]{2,1,0:T(8,128)} %get-tuple-element.19), calls=%async_computation | async-start | bytes 4194304 | tf_op jit(solution)/shard_map/all_to_all | solution.py:151
  10.8 2.1 %collective-permute-start.4 = (f32[264,128]{1,0:T(8,128)S(1)}, f32[264,128]{1,0:T(8,128)S(1)}, u32[]{:S(2)}, u32[]{:S(2)}) collective-permute-start(f32[264,128]{1,0:T(8,128)S(1)} %copy-done.1), channel_id=1, source_target_pairs={{0,16},{16,0},{1,17},{17,1},{2,18},{18,2},{3,19},{19,3},{4,20},{20... | collective-permute-start | bytes 405512 | tf_op jit(solution)/shard_map/ppermute | solution.py:140
  10.9 8.9 %collective-permute-start = (f32[264,128]{1,0:T(8,128)S(1)}, f32[264,128]{1,0:T(8,128)S(1)}, u32[]{:S(2)}, u32[]{:S(2)}) collective-permute-start(f32[264,128]{1,0:T(8,128)S(1)} %copy-done.1), channel_id=1, source_target_pairs={{0,1},{1,2},{2,3},{3,4},{4,5},{5,6},{6,7},{7,0},{16,23},{17,16},{1... | collective-permute-start | bytes 405512 | tf_op jit(solution)/shard_map/ppermute | solution.py:146
  12.9 27.6 %copy-start.2 = (f32[264,128]{1,0:T(8,128)}, f32[264,128]{1,0:T(8,128)S(1)}, u32[]{:S(2)}) copy-start(f32[264,128]{1,0:T(8,128)S(1)} %collective-permute-done.4.refs_2_) | copy-start | bytes 405508
  12.9 8.4 %collective-permute-start.6 = (f32[264,128]{1,0:T(8,128)S(1)}, f32[264,128]{1,0:T(8,128)S(1)}, u32[]{:S(2)}, u32[]{:S(2)}) collective-permute-start(f32[264,128]{1,0:T(8,128)S(1)} %collective-permute-done.4.refs_2_), channel_id=1, source_target_pairs={{0,1},{1,2},{2,3},{3,4},{4,5},{5,6},{6,7},{7,0},{16,23},{17,16},{1... | collective-permute-start | bytes 405512 | tf_op jit(solution)/shard_map/ppermute | solution.py:146
  19.8 20.7 %copy-start.3 = (f32[264,128]{1,0:T(8,128)}, f32[264,128]{1,0:T(8,128)S(1)}, u32[]{:S(2)}) copy-start(f32[264,128]{1,0:T(8,128)S(1)} %collective-permute-done.refs_7_) | copy-start | bytes 405508
  19.8 6.2 %collective-permute-start.1 = (f32[264,128]{1,0:T(8,128)S(1)}, f32[264,128]{1,0:T(8,128)S(1)}, u32[]{:S(2)}, u32[]{:S(2)}) collective-permute-start(f32[264,128]{1,0:T(8,128)S(1)} %collective-permute-done.refs_7_), channel_id=1, source_target_pairs={{0,1},{1,2},{2,3},{3,4},{4,5},{5,6},{6,7},{7,0},{16,23},{17,16},{1... | collective-permute-start | bytes 405512 | tf_op jit(solution)/shard_map/ppermute | solution.py:146
  21.2 19.2 %copy-start.4 = (f32[264,128]{1,0:T(8,128)}, f32[264,128]{1,0:T(8,128)S(1)}, u32[]{:S(2)}) copy-start(f32[264,128]{1,0:T(8,128)S(1)} %collective-permute-done.6.refs_6_) | copy-start | bytes 405508
  21.2 6.7 %collective-permute-start.9 = (f32[264,128]{1,0:T(8,128)S(1)}, f32[264,128]{1,0:T(8,128)S(1)}, u32[]{:S(2)}, u32[]{:S(2)}) collective-permute-start(f32[264,128]{1,0:T(8,128)S(1)} %collective-permute-done.6.refs_6_), channel_id=1, source_target_pairs={{0,1},{1,2},{2,3},{3,4},{4,5},{5,6},{6,7},{7,0},{16,23},{17,16},{1... | collective-permute-start | bytes 405512 | tf_op jit(solution)/shard_map/ppermute | solution.py:146
  26.0 14.4 %copy-start.5 = (f32[264,128]{1,0:T(8,128)}, f32[264,128]{1,0:T(8,128)S(1)}, u32[]{:S(2)}) copy-start(f32[264,128]{1,0:T(8,128)S(1)} %collective-permute-done.1.refs_11_) | copy-start | bytes 405508
  26.0 6.2 %collective-permute-start.2 = (f32[264,128]{1,0:T(8,128)S(1)}, f32[264,128]{1,0:T(8,128)S(1)}, u32[]{:S(2)}, u32[]{:S(2)}) collective-permute-start(f32[264,128]{1,0:T(8,128)S(1)} %collective-permute-done.1.refs_11_), channel_id=1, source_target_pairs={{0,1},{1,2},{2,3},{3,4},{4,5},{5,6},{6,7},{7,0},{16,23},{17,16},{1... | collective-permute-start | bytes 405512 | tf_op jit(solution)/shard_map/ppermute | solution.py:146
  26.0 7.3 %collective-permute-start.8 = (f32[264,128]{1,0:T(8,128)S(1)}, f32[264,128]{1,0:T(8,128)S(1)}, u32[]{:S(2)}, u32[]{:S(2)}) collective-permute-start(f32[264,128]{1,0:T(8,128)S(1)} %collective-permute-done.refs_7_), channel_id=1, source_target_pairs={{0,16},{16,0},{1,17},{17,1},{2,18},{18,2},{3,19},{19,3},{4,20},{20... | collective-permute-start | bytes 405512 | tf_op jit(solution)/shard_map/ppermute | solution.py:140
  27.9 5.6 %collective-permute-start.7 = (f32[264,128]{1,0:T(8,128)S(1)}, f32[264,128]{1,0:T(8,128)S(1)}, u32[]{:S(2)}, u32[]{:S(2)}) collective-permute-start(f32[264,128]{1,0:T(8,128)S(1)} %collective-permute-done.6.refs_6_), channel_id=1, source_target_pairs={{0,16},{16,0},{1,17},{17,1},{2,18},{18,2},{3,19},{19,3},{4,20},{20... | collective-permute-start | bytes 405512 | tf_op jit(solution)/shard_map/ppermute | solution.py:140
  27.9 12.6 %copy-start.6 = (f32[264,128]{1,0:T(8,128)}, f32[264,128]{1,0:T(8,128)S(1)}, u32[]{:S(2)}) copy-start(f32[264,128]{1,0:T(8,128)S(1)} %collective-permute-done.9.refs_10_) | copy-start | bytes 405508
  27.9 6.3 %collective-permute-start.12 = (f32[264,128]{1,0:T(8,128)S(1)}, f32[264,128]{1,0:T(8,128)S(1)}, u32[]{:S(2)}, u32[]{:S(2)}) collective-permute-start(f32[264,128]{1,0:T(8,128)S(1)} %collective-permute-done.9.refs_10_), channel_id=1, source_target_pairs={{0,1},{1,2},{2,3},{3,4},{4,5},{5,6},{6,7},{7,0},{16,23},{17,16},{1... | collective-permute-start | bytes 405512 | tf_op jit(solution)/shard_map/ppermute | solution.py:146
  32.2 8.2 %copy-start.7 = (f32[264,128]{1,0:T(8,128)}, f32[264,128]{1,0:T(8,128)S(1)}, u32[]{:S(2)}) copy-start(f32[264,128]{1,0:T(8,128)S(1)} %collective-permute-done.2.refs_15_) | copy-start | bytes 405508
  32.2 6.2 %collective-permute-start.3 = (f32[264,128]{1,0:T(8,128)S(1)}, f32[264,128]{1,0:T(8,128)S(1)}, u32[]{:S(2)}, u32[]{:S(2)}) collective-permute-start(f32[264,128]{1,0:T(8,128)S(1)} %collective-permute-done.2.refs_15_), channel_id=1, source_target_pairs={{0,1},{1,2},{2,3},{3,4},{4,5},{5,6},{6,7},{7,0},{16,23},{17,16},{1... | collective-permute-start | bytes 405512 | tf_op jit(solution)/shard_map/ppermute | solution.py:146
  32.2 6.2 %collective-permute-start.11 = (f32[264,128]{1,0:T(8,128)S(1)}, f32[264,128]{1,0:T(8,128)S(1)}, u32[]{:S(2)}, u32[]{:S(2)}) collective-permute-start(f32[264,128]{1,0:T(8,128)S(1)} %collective-permute-done.1.refs_11_), channel_id=1, source_target_pairs={{0,16},{16,0},{1,17},{17,1},{2,18},{18,2},{3,19},{19,3},{4,20},{20... | collective-permute-start | bytes 405512 | tf_op jit(solution)/shard_map/ppermute | solution.py:140
  33.4 7.1 %copy-start.8 = (f32[264,128]{1,0:T(8,128)}, f32[264,128]{1,0:T(8,128)S(1)}, u32[]{:S(2)}) copy-start(f32[264,128]{1,0:T(8,128)S(1)} %collective-permute-done.8.refs_5_) | copy-start | bytes 405508
  33.4 5.1 %collective-permute-start.10 = (f32[264,128]{1,0:T(8,128)S(1)}, f32[264,128]{1,0:T(8,128)S(1)}, u32[]{:S(2)}, u32[]{:S(2)}) collective-permute-start(f32[264,128]{1,0:T(8,128)S(1)} %collective-permute-done.9.refs_10_), channel_id=1, source_target_pairs={{0,16},{16,0},{1,17},{17,1},{2,18},{18,2},{3,19},{19,3},{4,20},{20... | collective-permute-start | bytes 405512 | tf_op jit(solution)/shard_map/ppermute | solution.py:140
  33.5 7.0 %copy-start.9 = (f32[264,128]{1,0:T(8,128)}, f32[264,128]{1,0:T(8,128)S(1)}, u32[]{:S(2)}) copy-start(f32[264,128]{1,0:T(8,128)S(1)} %collective-permute-done.7.refs_4_) | copy-start | bytes 405508
  33.5 5.0 %collective-permute-start.14 = (f32[264,128]{1,0:T(8,128)S(1)}, f32[264,128]{1,0:T(8,128)S(1)}, u32[]{:S(2)}, u32[]{:S(2)}) collective-permute-start(f32[264,128]{1,0:T(8,128)S(1)} %collective-permute-done.2.refs_15_), channel_id=1, source_target_pairs={{0,16},{16,0},{1,17},{17,1},{2,18},{18,2},{3,19},{19,3},{4,20},{20... | collective-permute-start | bytes 405512 | tf_op jit(solution)/shard_map/ppermute | solution.py:140
  34.2 6.3 %copy-start.10 = (f32[264,128]{1,0:T(8,128)}, f32[264,128]{1,0:T(8,128)S(1)}, u32[]{:S(2)}) copy-start(f32[264,128]{1,0:T(8,128)S(1)} %collective-permute-done.12.refs_14_) | copy-start | bytes 405508
  34.2 4.3 %collective-permute-start.13 = (f32[264,128]{1,0:T(8,128)S(1)}, f32[264,128]{1,0:T(8,128)S(1)}, u32[]{:S(2)}, u32[]{:S(2)}) collective-permute-start(f32[264,128]{1,0:T(8,128)S(1)} %collective-permute-done.12.refs_14_), channel_id=1, source_target_pairs={{0,16},{16,0},{1,17},{17,1},{2,18},{18,2},{3,19},{19,3},{4,20},{20... | collective-permute-start | bytes 405512 | tf_op jit(solution)/shard_map/ppermute | solution.py:140
  38.5 2.0 %copy-start.11 = (f32[264,128]{1,0:T(8,128)}, f32[264,128]{1,0:T(8,128)S(1)}, u32[]{:S(2)}) copy-start(f32[264,128]{1,0:T(8,128)S(1)} %collective-permute-done.3.refs_1_) | copy-start | bytes 405508
  38.5 1.5 %collective-permute-start.5 = (f32[264,128]{1,0:T(8,128)S(1)}, f32[264,128]{1,0:T(8,128)}, u32[]{:S(2)}, u32[]{:S(2)}) collective-permute-start(f32[264,128]{1,0:T(8,128)S(1)} %collective-permute-done.3.refs_1_), channel_id=1, source_target_pairs={{0,16},{16,0},{1,17},{17,1},{2,18},{18,2},{3,19},{19,3},{4,20},{20... | collective-permute-start | bytes 405512 | tf_op jit(solution)/shard_map/ppermute | solution.py:140
  38.5 0.7 copy-start.12
  38.5 0.8 copy-start.13
  38.5 0.8 copy-start.14
  39.3 0.7 copy-start.15
  54.3 23.4 %all-to-all-start.1 = ((f32[16,128,128]{2,1,0:T(8,128)}), f32[16,128,128]{2,1,0:T(8,128)S(1)}, u32[]{:S(2)}, u32[]{:S(2)}) async-start(f32[16,128,128]{2,1,0:T(8,128)} %get-tuple-element.24), calls=%async_computation.1 | async-start | bytes 2097152 | tf_op jit(solution)/shard_map/all_to_all | solution.py:163
  61.4 24.5 %collective-permute-start.15 = (f32[4,2,128,128]{3,2,1,0:T(8,128)S(1)}, f32[4,2,128,128]{3,2,1,0:T(8,128)}, u32[]{:S(2)}, u32[]{:S(2)}) collective-permute-start(f32[4,2,128,128]{3,2,1,0:T(8,128)S(1)} %get-tuple-element.21), channel_id=1, source_target_pairs={{0,16},{16,0},{1,17},{17,1},{2,18},{18,2},{3,19},{19,3},{4,20},{20... | collective-permute-start | bytes 1572872 | tf_op jit(solution)/shard_map/ppermute | solution.py:140
  77.8 1.0 copy-start
  77.8 8.2 %collective-permute-start.16 = (f32[4,2,128,128]{3,2,1,0:T(8,128)S(1)}, f32[4,2,128,128]{3,2,1,0:T(8,128)}, u32[]{:S(2)}, u32[]{:S(2)}) collective-permute-start(f32[4,2,128,128]{3,2,1,0:T(8,128)S(1)} %get-tuple-element.25), channel_id=1, source_target_pairs={{0,16},{16,0},{1,17},{17,1},{2,18},{18,2},{3,19},{19,3},{4,20},{20... | collective-permute-start | bytes 1572872 | tf_op jit(solution)/shard_map/ppermute | solution.py:140
  78.8 21.6 %all-to-all-start.2 = ((f32[16,128,128]{2,1,0:T(8,128)}), f32[16,128,128]{2,1,0:T(8,128)S(1)}, u32[]{:S(2)}, u32[]{:S(2)}) async-start(f32[16,128,128]{2,1,0:T(8,128)} %get-tuple-element.26), calls=%async_computation.2 | async-start | bytes 2097152 | tf_op jit(solution)/shard_map/all_to_all | solution.py:171
  87.3 13.0 %collective-permute-start.20 = (f32[128,128]{1,0:T(8,128)S(1)}, f32[128,128]{1,0:T(8,128)S(1)}, u32[]{:S(2)}, u32[]{:S(2)}) collective-permute-start(f32[128,128]{1,0:T(8,128)S(1)} %slice_bitcast_fusion.3), channel_id=1, source_target_pairs={{0,4},{1,5},{2,6},{3,7},{4,0},{5,1},{6,2},{7,3},{16,20},{17,21},{1... | collective-permute-start | bytes 196616 | tf_op jit(solution)/shard_map/ppermute | solution.py:146
  93.4 11.4 %collective-permute-start.19 = (f32[2,128,128]{2,1,0:T(8,128)S(1)}, f32[2,128,128]{2,1,0:T(8,128)S(1)}, u32[]{:S(2)}, u32[]{:S(2)}) collective-permute-start(f32[2,128,128]{2,1,0:T(8,128)S(1)} %get-tuple-element.33), channel_id=1, source_target_pairs={{0,3},{1,4},{2,5},{3,6},{4,7},{5,0},{6,1},{7,2},{16,21},{17,22},{1... | collective-permute-start | bytes 393224 | tf_op jit(solution)/shard_map/ppermute | solution.py:146
  95.4 10.4 %collective-permute-start.18 = (f32[2,128,128]{2,1,0:T(8,128)S(1)}, f32[2,128,128]{2,1,0:T(8,128)S(1)}, u32[]{:S(2)}, u32[]{:S(2)}) collective-permute-start(f32[2,128,128]{2,1,0:T(8,128)S(1)} %get-tuple-element.34), channel_id=1, source_target_pairs={{0,2},{1,3},{2,4},{3,5},{4,6},{5,7},{6,0},{7,1},{16,22},{17,23},{1... | collective-permute-start | bytes 393224 | tf_op jit(solution)/shard_map/ppermute | solution.py:146
  95.4 12.2 %collective-permute-start.17 = (f32[2,128,128]{2,1,0:T(8,128)S(1)}, f32[2,128,128]{2,1,0:T(8,128)S(1)}, u32[]{:S(2)}, u32[]{:S(2)}) collective-permute-start(f32[2,128,128]{2,1,0:T(8,128)S(1)} %get-tuple-element.35), channel_id=1, source_target_pairs={{0,1},{1,2},{2,3},{3,4},{4,5},{5,6},{6,7},{7,0},{16,23},{17,16},{1... | collective-permute-start | bytes 393224 | tf_op jit(solution)/shard_map/ppermute | solution.py:146
  107.7 1.3 %collective-permute-start.21 = (f32[128,128]{1,0:T(8,128)S(1)}, f32[128,128]{1,0:T(8,128)S(1)}, u32[]{:S(2)}, u32[]{:S(2)}) collective-permute-start(f32[128,128]{1,0:T(8,128)S(1)} %add_bitcast_fusion), channel_id=1, source_target_pairs={{0,16},{16,0},{1,17},{17,1},{2,18},{18,2},{3,19},{19,3},{4,20},{20... | collective-permute-start | bytes 196616 | tf_op jit(solution)/shard_map/ppermute | solution.py:140

commit v3 on v2

v3 whole, which is shorter than its diff:
```python
import math

import jax
import jax.numpy as jnp
from jax import lax
from jax.experimental import pallas as pl
from jax.experimental.pallas import tpu as pltpu
from jax.sharding import Mesh, PartitionSpec as P

D = 128
SCALE = 1.0 / math.sqrt(D)
LOG2E = math.log2(math.e)
LN2 = math.log(2.0)
BF16 = jnp.bfloat16
F32 = jnp.float32

AXES = ("xh", "y", "c", "xl", "z")
PLANE = ("xh", "y", "xl")
COLUMN = ("c", "z")
DEPTH = 8
ROWS = 128
BLOCKS = 16
TOKENS = ROWS * BLOCKS
PACK = 2 * ROWS + 8
CHUNKS = 4
TQ = TOKENS // CHUNKS
TK = TOKENS // 2

SWAP = [(0, 1), (1, 0)]


def shape(*dims, dtype=F32):
    return jax.ShapeDtypeStruct(dims, dtype)


def split(x):
    high = x.astype(BF16)
    return high, (x - high.astype(F32)).astype(BF16)


def split3(x):
    a = x.astype(BF16)
    rest = x - a.astype(F32)
    b = rest.astype(BF16)
    return a, b, (rest - b.astype(F32)).astype(BF16)


def dot(a, b):
    return jnp.dot(a, b, preferred_element_type=F32)


def pack_kernel(k, v, q, o, g, lse, own, copies):
    own[:ROWS] = q[...]
    own[ROWS : 2 * ROWS] = g[...]
    delta = jnp.sum((g[...] * o[...]).T, axis=0, keepdims=True)
    own[2 * ROWS :] = jnp.concatenate([lse[...], delta, jnp.zeros((6, D), F32)], 0)
    for b in range(BLOCKS):
        copies[b, :ROWS] = k[...]
        copies[b, ROWS:] = v[...]


def pack(query, keys, values, attn_out, out_grad, row_lse):
    return pl.pallas_call(pack_kernel, out_shape=[shape(PACK, D), shape(BLOCKS, 2 * ROWS, D)])(
        keys, values, query, attn_out, out_grad, row_lse
    )


def load_block(x_ref, base, factor, row_at, row_factor, at, turned, wide):
    x = x_ref[base : base + ROWS, :] * factor
    high, low = split(x)
    wide[at, :D] = high
    wide[at, D : 2 * D] = high
    wide[at, 2 * D : 3 * D] = low
    high, low = split(x.T)
    turned[:D, at] = high
    turned[D:, at] = low
    a, b, c = split3(x_ref[row_at : row_at + 1, :] * -row_factor)
    sub = lax.broadcasted_iota(jnp.int32, (D, ROWS), 0)
    tail = jnp.where(sub == 0, a.astype(F32), jnp.where(sub == 1, b.astype(F32), jnp.where(sub == 2, c.astype(F32), 0.0)))
    wide[at, 3 * D :] = tail.T.astype(BF16)


def tile_kernel(*refs):
    packs, kv_ref, mine, theirs, dkv_ref = refs[:BLOCKS], *refs[BLOCKS : BLOCKS + 4]
    q_turned, g_turned, q_all, g_all, dq, local, sems = refs[BLOCKS + 4 :]
    step = pl.program_id(0)

    @pl.when(step == 0)
    def _():
        copies = [pltpu.make_async_copy(packs[b], local.at[b], sems.at[b]) for b in range(BLOCKS)]
        for copy in copies:
            copy.start()
        for b in range(BLOCKS):
            copies[b].wait()
            at = slice(b * ROWS, (b + 1) * ROWS)
            load_block(local.at[b], 0, SCALE * LOG2E, 2 * ROWS, LOG2E, at, q_turned, q_all)
            load_block(local.at[b], ROWS, 1.0, 2 * ROWS + 1, 1.0, at, g_turned, g_all)
        dq[...] = jnp.zeros_like(dq)

    ones = (lax.broadcasted_iota(jnp.int32, (D, TK), 0) < 3).astype(F32).astype(BF16)
    k = kv_ref[:, :ROWS, :].reshape(TK, D)
    v = kv_ref[:, ROWS:, :].reshape(TK, D)
    k_high, k_low = split(k.T)
    v_high, v_low = split(v.T)
    k_all = jnp.concatenate([k_high, k_low, k_high, ones], 0)
    v_all = jnp.concatenate([v_high, v_low, v_high, ones], 0)
    k_wide = jnp.concatenate(split(k), 1)
    dvt = jnp.zeros((D, TK), F32)
    dkt = jnp.zeros((D, TK), F32)
    for j in range(TOKENS // TQ):
        at = slice(j * TQ, (j + 1) * TQ)
        probs = jnp.exp2(dot(q_all[at, :], k_all))
        dprob = dot(g_all[at, :], v_all)
        high, low = split(probs)
        part = dot(g_turned[:, at], high)
        dvt += part[:D] + part[D:] + dot(g_turned[:D, at], low)
        high, low = split(probs * dprob)
        part = dot(q_turned[:, at], high)
        dkt += part[:D] + part[D:] + dot(q_turned[:D, at], low)
        part = dot(high, k_wide) + dot(low, k_wide)
        dq[at, :] = dq[at, :] + (part[:, :D] + part[:, D:])
    dkv_ref[:, :ROWS, :] = (dkt * LN2).T.reshape(TK // ROWS, ROWS, D)
    dkv_ref[:, ROWS:, :] = dvt.T.reshape(TK // ROWS, ROWS, D)

    @pl.when(step == pl.num_programs(0) - 1)
    def _():
        for j in range(CHUNKS):
            for b in range(2):
                at = (4 * j + b) * ROWS
                mine[j, b] = dq[at : at + ROWS] * SCALE
                at += 2 * ROWS
                theirs[j, b] = dq[at : at + ROWS] * SCALE


def tile_grads(packs, kv):
    half = (CHUNKS, 2, ROWS, D)
    block = pl.BlockSpec((TK // ROWS, 2 * ROWS, D), lambda i: (i, 0, 0))
    return pl.pallas_call(
        tile_kernel,
        grid=(TOKENS // TK,),
        in_specs=[pl.BlockSpec(memory_space=pl.ANY)] * BLOCKS + [block],
        out_specs=[pl.BlockSpec(half, lambda i: (0, 0, 0, 0))] * 2 + [block],
        out_shape=[shape(*half), shape(*half), pltpu.HBM((BLOCKS, 2 * ROWS, D), F32)],
        scratch_shapes=[pltpu.VMEM((2 * D, TOKENS), BF16)] * 2
        + [pltpu.VMEM((TOKENS, 4 * D), BF16)] * 2
        + [pltpu.VMEM((TOKENS, D), F32), pltpu.VMEM((BLOCKS, PACK, D), F32), pltpu.SemaphoreType.DMA((BLOCKS,))],
        compiler_params=pltpu.CompilerParams(vmem_limit_bytes=36 * 1024 * 1024),
        cost_estimate=pl.CostEstimate(flops=24_000_000_000, bytes_accessed=8 << 20, transcendentals=TOKENS * TOKENS),
    )(*packs, kv)


def swap(x):
    return lax.ppermute(x, "c", SWAP)


def along(x, step):
    pairs = [(z, (z + step) % DEPTH) for z in range(DEPTH)]
    pairs += [(DEPTH + z, DEPTH + (z - step) % DEPTH) for z in range(DEPTH)]
    return lax.ppermute(x, COLUMN, pairs)


def on_device(query, keys, values, attn_out, out_grad, row_lse):
    own, kv = pack(query, keys, values, attn_out, out_grad, row_lse)
    other = swap(own)
    kv = lax.all_to_all(kv, PLANE, 0, 0)
    a, b = own, other
    packs = []
    for j in range(1, CHUNKS):
        a, b = along(a, 1), along(b, 1)
        packs += [swap(b), swap(a), b, a]
    far = along(a, 1)
    packs = [own, far, other, swap(far)] + packs
    packs = [pltpu.with_memory_space_constraint(x, pltpu.HBM) for x in packs]
    mine, theirs, dkv = tile_grads(packs, kv)
    dq = mine + swap(theirs)
    dkv = lax.all_to_all(dkv, PLANE, 0, 0)
    r1 = along(dq[1], 1)
    r2 = along(dq[2], 2)
    r3 = along(dq[3], 3)
    r4 = along(dq[0, 1], 4)
    query_grad = (dq[0, 0] + r4) + (r1[0] + r2[0] + r3[0]) + swap(r1[1] + r2[1] + r3[1])
    query_grad, dkv = lax.optimization_barrier((query_grad, dkv))
    dkv = jnp.sum(dkv, axis=0)
    return query_grad, dkv[:ROWS], dkv[ROWS:]


def solution(mesh):
    fine = Mesh(mesh.devices.reshape(2, 4, 2, 2, DEPTH), AXES)
    rows = P(("xh", "y", "c", "xl", "z"), None)
    cols = P(("xl", "z", "xh", "y", "c"), None)
    return jax.shard_map(
        on_device,
        mesh=fine,
        in_specs=(rows, cols, cols, rows, rows, P(None, ("xh", "y", "c", "xl", "z"))),
        out_specs=(rows, cols, cols),
        check_vma=False,
    )
```

time: 111 us -> 105 us (0.946)
  waiting for transfers between devices: 35.2 us -> 40.4 us
  starting transfers between devices: 37 us -> 33.3 us
  other arithmetic: 3.97 us -> 0.85 us
  Pallas kernels: 30.2 us -> 27.2 us
    all_to_all x2 -> x1, starting transfers between devices: 13 us -> 7.06 us  [on_device(): dkv = lax.all_to_all(dkv, PLANE, 0, 0)]
    pallas_call x2 -> x1, Pallas kernels: 27.7 us -> 24.7 us  [tile_grads(): pl.pallas_call(tile_kernel, grid=(TOKENS // TK,), in_specs=[pl.BlockSpec(...]
    all_to_all x2 -> x1, waiting for transfers between devices: 6.74 us -> 9.42 us  [on_device(): dkv = lax.all_to_all(dkv, PLANE, 0, 0)]
    ppermute x11, waiting for transfers between devices: 27.3 us -> 28.8 us  [along(): return lax.ppermute(x, COLUMN, pairs)]
    ppermute x11 -> x10, waiting for transfers between devices: 0.62 us -> 1.92 us  [swap(): return lax.ppermute(x, 'c', SWAP)]
    reduce_sum x2 -> x1, other arithmetic: 1.34 us -> 0.1 us  [on_device(): dkv = jnp.sum(dkv, axis=0)]
    add x1, other arithmetic: 1.31 us -> 0.08 us  [on_device(): dq = mine + swap(theirs)]
    ppermute x11 -> x10, starting transfers between devices: 3.7 us -> 4.77 us  [swap(): return lax.ppermute(x, 'c', SWAP)]
  transfers between devices with their start and end apart: 25 -> 23, of which waited for: 13 -> 12; matrix products, arithmetic and copies ran while one was open for 3% -> 1% of each run, Pallas kernels for 13% -> 0%
where the time goes in v3:
time: 105 us
  waiting for transfers between devices  40.4 us (38%)
  starting transfers between devices  33.3 us (32%)
  Pallas kernels  27.2 us (26%)
  local copies, waits for them, and re-layouts  2.15 us (2%)
    ppermute x11, waiting for transfers between devices, along(): return lax.ppermute(x, COLUMN, pairs)  28.8 us
    pallas_call x1, Pallas kernels, tile_grads(): pl.pallas_call(tile_kernel, grid=(TOKENS // TK,), in_specs=[pl.BlockSpec(...  24.7 us
    ppermute x11, starting transfers between devices, along(): return lax.ppermute(x, COLUMN, pairs)  13.9 us
    all_to_all x1, waiting for transfers between devices, on_device(): dkv = lax.all_to_all(dkv, PLANE, 0, 0)  9.42 us
    all_to_all x1, starting transfers between devices, on_device(): kv = lax.all_to_all(kv, PLANE, 0, 0)  7.61 us
    all_to_all x1, starting transfers between devices, on_device(): dkv = lax.all_to_all(dkv, PLANE, 0, 0)  7.06 us
    ppermute x10, starting transfers between devices, swap(): return lax.ppermute(x, 'c', SWAP)  4.77 us
    pallas_call x1, Pallas kernels, pack(): pl.pallas_call(pack_kernel, out_shape=[shape(PACK, D), shape(BLOCKS, 2 *...  2.51 us
  transfers between devices with their start and end apart: 23, of which 12 were waited for; matrix products, arithmetic and copies ran while one was open for 1% of the time, Pallas kernels for 0%

profile of v3, /device:TPU:2, one launch (start us, length us, event | category | flops | bytes accessed | tf_op | source)
XLA Modules:
  0.0 104.8 jit_solution(2556087201269900238)
XLA Ops:
  0.6 2.5 %shard_map.85 = (f32[264,128]{1,0:T(8,128)}, f32[16,256,128]{2,1,0:T(8,128)}) custom-call(f32[128,128]{1,0:T(8,128)} %k.1, f32[128,128]{1,0:T(8,128)} %v.1, f32[128,128]{1,0:T(8,128)} %q.1, f32[128,128]{1,0:T(8,128)} %o.1, f32[128,128]{1,0:T(8,128)} %g.1, f32[1,128]{1,0:T(1,128)} %lse.1), custom_call_target="tpu_custom_call" | custom-call | tf_op jit(solution)/shard_map/pallas_call | solution.py:63
  3.1 7.6 %all-to-all-start = ((f32[16,256,128]{2,1,0:T(8,128)}), f32[16,256,128]{2,1,0:T(8,128)S(1)}, u32[]{:S(2)}, u32[]{:S(2)}) async-start(f32[16,256,128]{2,1,0:T(8,128)} %get-tuple-element.11), calls=%async_computation | async-start | bytes 4194304 | tf_op jit(solution)/shard_map/all_to_all | solution.py:165
  10.8 0.1 collective-permute-start.4
  10.9 2.0 %collective-permute-start = (f32[264,128]{1,0:T(8,128)S(1)}, f32[264,128]{1,0:T(8,128)S(1)}, u32[]{:S(2)}, u32[]{:S(2)}) collective-permute-start(f32[264,128]{1,0:T(8,128)S(1)} %copy-done), channel_id=1, source_target_pairs={{0,1},{1,2},{2,3},{3,4},{4,5},{5,6},{6,7},{7,0},{16,23},{17,16},{1... | collective-permute-start | bytes 405512 | tf_op jit(solution)/shard_map/ppermute | solution.py:159
  12.9 0.0 collective-permute-done.4.refs_2_
  12.9 1.9 %collective-permute-start.6 = (f32[264,128]{1,0:T(8,128)S(1)}, f32[264,128]{1,0:T(8,128)S(1)}, u32[]{:S(2)}, u32[]{:S(2)}) collective-permute-start(f32[264,128]{1,0:T(8,128)S(1)} %collective-permute-done.4.refs_2_), channel_id=1, source_target_pairs={{0,1},{1,2},{2,3},{3,4},{4,5},{5,6},{6,7},{7,0},{16,23},{17,16},{1... | collective-permute-start | bytes 405512 | tf_op jit(solution)/shard_map/ppermute | solution.py:159
  14.8 5.0 %collective-permute-done.refs_7_ = f32[264,128]{1,0:T(8,128)S(1)} collective-permute-done((f32[264,128]{1,0:T(8,128)S(1)}, f32[264,128]{1,0:T(8,128)S(1)}, u32[]{:S(2)}, u32[]{:S(2)}) %collective-permute-start) | collective-permute-done | bytes 135200 | tf_op jit(solution)/shard_map/ppermute | solution.py:159
  19.8 0.0 collective-permute-start.1
  19.8 1.4 %collective-permute-done.6.refs_6_ = f32[264,128]{1,0:T(8,128)S(1)} collective-permute-done((f32[264,128]{1,0:T(8,128)S(1)}, f32[264,128]{1,0:T(8,128)S(1)}, u32[]{:S(2)}, u32[]{:S(2)}) %collective-permute-start.6) | collective-permute-done | bytes 135200 | tf_op jit(solution)/shard_map/ppermute | solution.py:159
  21.2 0.0 collective-permute-start.9
  21.2 4.8 %collective-permute-done.1.refs_11_ = f32[264,128]{1,0:T(8,128)S(1)} collective-permute-done((f32[264,128]{1,0:T(8,128)S(1)}, f32[264,128]{1,0:T(8,128)S(1)}, u32[]{:S(2)}, u32[]{:S(2)}) %collective-permute-start.1) | collective-permute-done | bytes 135200 | tf_op jit(solution)/shard_map/ppermute | solution.py:159
  26.0 0.0 collective-permute-start.2
  26.0 1.7 %collective-permute-start.8 = (f32[264,128]{1,0:T(8,128)S(1)}, f32[264,128]{1,0:T(8,128)S(1)}, u32[]{:S(2)}, u32[]{:S(2)}) collective-permute-start(f32[264,128]{1,0:T(8,128)S(1)} %collective-permute-done.refs_7_), channel_id=1, source_target_pairs={{0,16},{16,0},{1,17},{17,1},{2,18},{18,2},{3,19},{19,3},{4,20},{20... | collective-permute-start | bytes 405512 | tf_op jit(solution)/shard_map/ppermute | solution.py:153
  27.7 0.0 collective-permute-done.9.refs_10_
  27.7 0.1 collective-permute-start.12
  27.8 4.5 %collective-permute-done.2.refs_15_ = f32[264,128]{1,0:T(8,128)S(1)} collective-permute-done((f32[264,128]{1,0:T(8,128)S(1)}, f32[264,128]{1,0:T(8,128)S(1)}, u32[]{:S(2)}, u32[]{:S(2)}) %collective-permute-start.2) | collective-permute-done | bytes 135200 | tf_op jit(solution)/shard_map/ppermute | solution.py:159
  32.2 0.8 collective-permute-start.11
  33.0 0.1 collective-permute-start.10
  33.1 0.0 collective-permute-done.7.refs_4_
  33.1 0.4 collective-permute-start.14
  33.6 0.4 collective-permute-done.12.refs_14_
  34.0 4.5 %collective-permute-done.3.refs_1_ = f32[264,128]{1,0:T(8,128)S(1)} collective-permute-done((f32[264,128]{1,0:T(8,128)S(1)}, f32[264,128]{1,0:T(8,128)S(1)}, u32[]{:S(2)}, u32[]{:S(2)}) %collective-permute-start.3) | collective-permute-done | bytes 135200 | tf_op jit(solution)/shard_map/ppermute | solution.py:159
  38.5 0.0 collective-permute-start.5
  38.5 0.0 collective-permute-done.14.refs_13_
  38.5 0.0 collective-permute-done.13.refs_12_
  38.5 0.6 copy-done.11
  39.2 0.1 copy-done.12
  39.2 0.1 copy-done.13
  39.3 0.6 copy-done.14
  39.9 0.0 collective-permute-done.5.refs_3_
  40.0 0.3 all-to-all-done.refs_16_
  40.3 24.7 %shard_map.86 = (f32[4,2,128,128]{3,2,1,0:T(8,128)S(1)}, f32[4,2,128,128]{3,2,1,0:T(8,128)S(1)}, f32[16,256,128]{2,1,0:T(8,128)}) custom-call(f32[264,128]{1,0:T(8,128)} %get-tuple-element.10.refs_0_, f32[264,128]{1,0:T(8,128)} %copy-done.10, f32[264,128]{1,0:T(8,128)} %copy-done.1, f32[264,128]{1,0:T(8,128)} %collective-permute-done.5.refs_3_, ...), custom_call_target="tpu_custom_call" | custom-call | flops 24000000000 | bytes 8388608 | tf_op jit(solution)/shard_map/pallas_call | solution.py:138
  65.1 7.1 %all-to-all-start.1 = ((f32[16,256,128]{2,1,0:T(8,128)}), f32[16,256,128]{2,1,0:T(8,128)S(1)}, u32[]{:S(2)}, u32[]{:S(2)}) async-start(f32[16,256,128]{2,1,0:T(8,128)} %get-tuple-element.14), calls=%async_computation.1 | async-start | bytes 4194304 | tf_op jit(solution)/shard_map/all_to_all | solution.py:176
  72.1 0.0 collective-permute-start.15
  72.2 1.9 %collective-permute-done.15 = f32[4,2,128,128]{3,2,1,0:T(8,128)S(1)} collective-permute-done((f32[4,2,128,128]{3,2,1,0:T(8,128)S(1)}, f32[4,2,128,128]{3,2,1,0:T(8,128)S(1)}, u32[]{:S(2)}, u32[]{:S(2)}) %collective-permute-start.15) | collective-permute-done | bytes 524320 | tf_op jit(solution)/shard_map/ppermute | solution.py:153
  74.1 0.1 add.32
  74.2 2.0 %collective-permute-start.17 = (f32[2,128,128]{2,1,0:T(8,128)S(1)}, f32[2,128,128]{2,1,0:T(8,128)S(1)}, u32[]{:S(2)}, u32[]{:S(2)}) collective-permute-start(f32[2,128,128]{2,1,0:T(8,128)S(1)} %get-tuple-element.17), channel_id=1, source_target_pairs={{0,1},{1,2},{2,3},{3,4},{4,5},{5,6},{6,7},{7,0},{16,23},{17,16},{1... | collective-permute-start | bytes 393224 | tf_op jit(solution)/shard_map/ppermute | solution.py:159
  76.2 5.8 %collective-permute-start.19 = (f32[2,128,128]{2,1,0:T(8,128)S(1)}, f32[2,128,128]{2,1,0:T(8,128)S(1)}, u32[]{:S(2)}, u32[]{:S(2)}) collective-permute-start(f32[2,128,128]{2,1,0:T(8,128)S(1)} %get-tuple-element.18), channel_id=1, source_target_pairs={{0,3},{1,4},{2,5},{3,6},{4,7},{5,0},{6,1},{7,2},{16,21},{17,22},{1... | collective-permute-start | bytes 393224 | tf_op jit(solution)/shard_map/ppermute | solution.py:159
  82.0 1.5 %collective-permute-start.18 = (f32[2,128,128]{2,1,0:T(8,128)S(1)}, f32[2,128,128]{2,1,0:T(8,128)S(1)}, u32[]{:S(2)}, u32[]{:S(2)}) collective-permute-start(f32[2,128,128]{2,1,0:T(8,128)S(1)} %get-tuple-element.19), channel_id=1, source_target_pairs={{0,2},{1,3},{2,4},{3,5},{4,6},{5,7},{6,0},{7,1},{16,22},{17,23},{1... | collective-permute-start | bytes 393224 | tf_op jit(solution)/shard_map/ppermute | solution.py:159
  83.5 0.5 collective-permute-start.16
  84.0 7.0 %collective-permute-done.19 = f32[2,128,128]{2,1,0:T(8,128)S(1)} collective-permute-done((f32[2,128,128]{2,1,0:T(8,128)S(1)}, f32[2,128,128]{2,1,0:T(8,128)S(1)}, u32[]{:S(2)}, u32[]{:S(2)}) %collective-permute-start.19) | collective-permute-done | bytes 131104 | tf_op jit(solution)/shard_map/ppermute | solution.py:159
  91.0 0.3 collective-permute-done.18
  91.3 1.7 %collective-permute-start.20 = (f32[128,128]{1,0:T(8,128)S(1)}, f32[128,128]{1,0:T(8,128)S(1)}, u32[]{:S(2)}, u32[]{:S(2)}) collective-permute-start(f32[128,128]{1,0:T(8,128)S(1)} %fusion), channel_id=1, source_target_pairs={{0,16},{16,0},{1,17},{17,1},{2,18},{18,2},{3,19},{19,3},{4,20},{20... | collective-permute-start | bytes 196616 | tf_op jit(solution)/shard_map/ppermute | solution.py:153
  93.0 0.9 collective-permute-done.16
  93.9 0.7 fusion.3
  94.6 9.4 %all-to-all-done.1 = f32[16,256,128]{2,1,0:T(8,128)S(1)} async-done(((f32[16,256,128]{2,1,0:T(8,128)}), f32[16,256,128]{2,1,0:T(8,128)S(1)}, u32[]{:S(2)}, u32[]{:S(2)}) %all-to-all-start.1) | async-done | bytes 2097184 | tf_op jit(solution)/shard_map/all_to_all | solution.py:176
  104.0 0.1 reduce_sum.9
  104.1 0.7 fusion.5
  (37 shorter events, 0.1 us)
Async XLA Ops:
  3.1 7.6 %copy-start = (f32[264,128]{1,0:T(8,128)S(1)}, f32[264,128]{1,0:T(8,128)}, u32[]{:S(2)}) copy-start(f32[264,128]{1,0:T(8,128)} %get-tuple-element.10.refs_0_) | copy-start | bytes 405508
  3.1 37.2 %all-to-all-start = ((f32[16,256,128]{2,1,0:T(8,128)}), f32[16,256,128]{2,1,0:T(8,128)S(1)}, u32[]{:S(2)}, u32[]{:S(2)}) async-start(f32[16,256,128]{2,1,0:T(8,128)} %get-tuple-element.11), calls=%async_computation | async-start | bytes 4194304 | tf_op jit(solution)/shard_map/all_to_all | solution.py:165
  10.8 2.1 %collective-permute-start.4 = (f32[264,128]{1,0:T(8,128)S(1)}, f32[264,128]{1,0:T(8,128)S(1)}, u32[]{:S(2)}, u32[]{:S(2)}) collective-permute-start(f32[264,128]{1,0:T(8,128)S(1)} %copy-done), channel_id=1, source_target_pairs={{0,16},{16,0},{1,17},{17,1},{2,18},{18,2},{3,19},{19,3},{4,20},{20... | collective-permute-start | bytes 405512 | tf_op jit(solution)/shard_map/ppermute | solution.py:153
  10.9 8.9 %collective-permute-start = (f32[264,128]{1,0:T(8,128)S(1)}, f32[264,128]{1,0:T(8,128)S(1)}, u32[]{:S(2)}, u32[]{:S(2)}) collective-permute-start(f32[264,128]{1,0:T(8,128)S(1)} %copy-done), channel_id=1, source_target_pairs={{0,1},{1,2},{2,3},{3,4},{4,5},{5,6},{6,7},{7,0},{16,23},{17,16},{1... | collective-permute-start | bytes 405512 | tf_op jit(solution)/shard_map/ppermute | solution.py:159
  12.9 27.5 %copy-start.1 = (f32[264,128]{1,0:T(8,128)}, f32[264,128]{1,0:T(8,128)S(1)}, u32[]{:S(2)}) copy-start(f32[264,128]{1,0:T(8,128)S(1)} %collective-permute-done.4.refs_2_) | copy-start | bytes 405508
  12.9 8.4 %collective-permute-start.6 = (f32[264,128]{1,0:T(8,128)S(1)}, f32[264,128]{1,0:T(8,128)S(1)}, u32[]{:S(2)}, u32[]{:S(2)}) collective-permute-start(f32[264,128]{1,0:T(8,128)S(1)} %collective-permute-done.4.refs_2_), channel_id=1, source_target_pairs={{0,1},{1,2},{2,3},{3,4},{4,5},{5,6},{6,7},{7,0},{16,23},{17,16},{1... | collective-permute-start | bytes 405512 | tf_op jit(solution)/shard_map/ppermute | solution.py:159
  19.8 20.5 %copy-start.2 = (f32[264,128]{1,0:T(8,128)}, f32[264,128]{1,0:T(8,128)S(1)}, u32[]{:S(2)}) copy-start(f32[264,128]{1,0:T(8,128)S(1)} %collective-permute-done.refs_7_) | copy-start | bytes 405508
  19.8 6.2 %collective-permute-start.1 = (f32[264,128]{1,0:T(8,128)S(1)}, f32[264,128]{1,0:T(8,128)S(1)}, u32[]{:S(2)}, u32[]{:S(2)}) collective-permute-start(f32[264,128]{1,0:T(8,128)S(1)} %collective-permute-done.refs_7_), channel_id=1, source_target_pairs={{0,1},{1,2},{2,3},{3,4},{4,5},{5,6},{6,7},{7,0},{16,23},{17,16},{1... | collective-permute-start | bytes 405512 | tf_op jit(solution)/shard_map/ppermute | solution.py:159
  21.2 18.7 %copy-start.3 = (f32[264,128]{1,0:T(8,128)}, f32[264,128]{1,0:T(8,128)S(1)}, u32[]{:S(2)}) copy-start(f32[264,128]{1,0:T(8,128)S(1)} %collective-permute-done.6.refs_6_) | copy-start | bytes 405508
  21.2 6.4 %collective-permute-start.9 = (f32[264,128]{1,0:T(8,128)S(1)}, f32[264,128]{1,0:T(8,128)S(1)}, u32[]{:S(2)}, u32[]{:S(2)}) collective-permute-start(f32[264,128]{1,0:T(8,128)S(1)} %collective-permute-done.6.refs_6_), channel_id=1, source_target_pairs={{0,1},{1,2},{2,3},{3,4},{4,5},{5,6},{6,7},{7,0},{16,23},{17,16},{1... | collective-permute-start | bytes 405512 | tf_op jit(solution)/shard_map/ppermute | solution.py:159
  26.0 14.3 %copy-start.4 = (f32[264,128]{1,0:T(8,128)}, f32[264,128]{1,0:T(8,128)S(1)}, u32[]{:S(2)}) copy-start(f32[264,128]{1,0:T(8,128)S(1)} %collective-permute-done.1.refs_11_) | copy-start | bytes 405508
  26.0 6.2 %collective-permute-start.2 = (f32[264,128]{1,0:T(8,128)S(1)}, f32[264,128]{1,0:T(8,128)S(1)}, u32[]{:S(2)}, u32[]{:S(2)}) collective-permute-start(f32[264,128]{1,0:T(8,128)S(1)} %collective-permute-done.1.refs_11_), channel_id=1, source_target_pairs={{0,1},{1,2},{2,3},{3,4},{4,5},{5,6},{6,7},{7,0},{16,23},{17,16},{1... | collective-permute-start | bytes 405512 | tf_op jit(solution)/shard_map/ppermute | solution.py:159
  26.0 7.0 %collective-permute-start.8 = (f32[264,128]{1,0:T(8,128)S(1)}, f32[264,128]{1,0:T(8,128)S(1)}, u32[]{:S(2)}, u32[]{:S(2)}) collective-permute-start(f32[264,128]{1,0:T(8,128)S(1)} %collective-permute-done.refs_7_), channel_id=1, source_target_pairs={{0,16},{16,0},{1,17},{17,1},{2,18},{18,2},{3,19},{19,3},{4,20},{20... | collective-permute-start | bytes 405512 | tf_op jit(solution)/shard_map/ppermute | solution.py:153
  27.7 5.5 %collective-permute-start.7 = (f32[264,128]{1,0:T(8,128)S(1)}, f32[264,128]{1,0:T(8,128)S(1)}, u32[]{:S(2)}, u32[]{:S(2)}) collective-permute-start(f32[264,128]{1,0:T(8,128)S(1)} %collective-permute-done.6.refs_6_), channel_id=1, source_target_pairs={{0,16},{16,0},{1,17},{17,1},{2,18},{18,2},{3,19},{19,3},{4,20},{20... | collective-permute-start | bytes 405512 | tf_op jit(solution)/shard_map/ppermute | solution.py:153
  27.7 12.3 %copy-start.5 = (f32[264,128]{1,0:T(8,128)}, f32[264,128]{1,0:T(8,128)S(1)}, u32[]{:S(2)}) copy-start(f32[264,128]{1,0:T(8,128)S(1)} %collective-permute-done.9.refs_10_) | copy-start | bytes 405508
  27.7 6.3 %collective-permute-start.12 = (f32[264,128]{1,0:T(8,128)S(1)}, f32[264,128]{1,0:T(8,128)S(1)}, u32[]{:S(2)}, u32[]{:S(2)}) collective-permute-start(f32[264,128]{1,0:T(8,128)S(1)} %collective-permute-done.9.refs_10_), channel_id=1, source_target_pairs={{0,1},{1,2},{2,3},{3,4},{4,5},{5,6},{6,7},{7,0},{16,23},{17,16},{1... | collective-permute-start | bytes 405512 | tf_op jit(solution)/shard_map/ppermute | solution.py:159
  32.2 7.7 %copy-start.6 = (f32[264,128]{1,0:T(8,128)}, f32[264,128]{1,0:T(8,128)S(1)}, u32[]{:S(2)}) copy-start(f32[264,128]{1,0:T(8,128)S(1)} %collective-permute-done.2.refs_15_) | copy-start | bytes 405508
  32.2 6.2 %collective-permute-start.3 = (f32[264,128]{1,0:T(8,128)S(1)}, f32[264,128]{1,0:T(8,128)S(1)}, u32[]{:S(2)}, u32[]{:S(2)}) collective-permute-start(f32[264,128]{1,0:T(8,128)S(1)} %collective-permute-done.2.refs_15_), channel_id=1, source_target_pairs={{0,1},{1,2},{2,3},{3,4},{4,5},{5,6},{6,7},{7,0},{16,23},{17,16},{1... | collective-permute-start | bytes 405512 | tf_op jit(solution)/shard_map/ppermute | solution.py:159
  32.2 6.2 %collective-permute-start.11 = (f32[264,128]{1,0:T(8,128)S(1)}, f32[264,128]{1,0:T(8,128)S(1)}, u32[]{:S(2)}, u32[]{:S(2)}) collective-permute-start(f32[264,128]{1,0:T(8,128)S(1)} %collective-permute-done.1.refs_11_), channel_id=1, source_target_pairs={{0,16},{16,0},{1,17},{17,1},{2,18},{18,2},{3,19},{19,3},{4,20},{20... | collective-permute-start | bytes 405512 | tf_op jit(solution)/shard_map/ppermute | solution.py:153
  33.0 6.9 %copy-start.7 = (f32[264,128]{1,0:T(8,128)}, f32[264,128]{1,0:T(8,128)S(1)}, u32[]{:S(2)}) copy-start(f32[264,128]{1,0:T(8,128)S(1)} %collective-permute-done.8.refs_5_) | copy-start | bytes 405508
  33.0 5.4 %collective-permute-start.10 = (f32[264,128]{1,0:T(8,128)S(1)}, f32[264,128]{1,0:T(8,128)S(1)}, u32[]{:S(2)}, u32[]{:S(2)}) collective-permute-start(f32[264,128]{1,0:T(8,128)S(1)} %collective-permute-done.9.refs_10_), channel_id=1, source_target_pairs={{0,16},{16,0},{1,17},{17,1},{2,18},{18,2},{3,19},{19,3},{4,20},{20... | collective-permute-start | bytes 405512 | tf_op jit(solution)/shard_map/ppermute | solution.py:153
  33.1 6.8 %copy-start.8 = (f32[264,128]{1,0:T(8,128)}, f32[264,128]{1,0:T(8,128)S(1)}, u32[]{:S(2)}) copy-start(f32[264,128]{1,0:T(8,128)S(1)} %collective-permute-done.7.refs_4_) | copy-start | bytes 405508
  33.1 5.4 %collective-permute-start.14 = (f32[264,128]{1,0:T(8,128)S(1)}, f32[264,128]{1,0:T(8,128)S(1)}, u32[]{:S(2)}, u32[]{:S(2)}) collective-permute-start(f32[264,128]{1,0:T(8,128)S(1)} %collective-permute-done.2.refs_15_), channel_id=1, source_target_pairs={{0,16},{16,0},{1,17},{17,1},{2,18},{18,2},{3,19},{19,3},{4,20},{20... | collective-permute-start | bytes 405512 | tf_op jit(solution)/shard_map/ppermute | solution.py:153
  34.0 6.0 %copy-start.9 = (f32[264,128]{1,0:T(8,128)}, f32[264,128]{1,0:T(8,128)S(1)}, u32[]{:S(2)}) copy-start(f32[264,128]{1,0:T(8,128)S(1)} %collective-permute-done.12.refs_14_) | copy-start | bytes 405508
  34.0 4.5 %collective-permute-start.13 = (f32[264,128]{1,0:T(8,128)S(1)}, f32[264,128]{1,0:T(8,128)S(1)}, u32[]{:S(2)}, u32[]{:S(2)}) collective-permute-start(f32[264,128]{1,0:T(8,128)S(1)} %collective-permute-done.12.refs_14_), channel_id=1, source_target_pairs={{0,16},{16,0},{1,17},{17,1},{2,18},{18,2},{3,19},{19,3},{4,20},{20... | collective-permute-start | bytes 405512 | tf_op jit(solution)/shard_map/ppermute | solution.py:153
  38.5 1.5 %copy-start.10 = (f32[264,128]{1,0:T(8,128)}, f32[264,128]{1,0:T(8,128)S(1)}, u32[]{:S(2)}) copy-start(f32[264,128]{1,0:T(8,128)S(1)} %collective-permute-done.3.refs_1_) | copy-start | bytes 405508
  38.5 1.5 %collective-permute-start.5 = (f32[264,128]{1,0:T(8,128)S(1)}, f32[264,128]{1,0:T(8,128)}, u32[]{:S(2)}, u32[]{:S(2)}) collective-permute-start(f32[264,128]{1,0:T(8,128)S(1)} %collective-permute-done.3.refs_1_), channel_id=1, source_target_pairs={{0,16},{16,0},{1,17},{17,1},{2,18},{18,2},{3,19},{19,3},{4,20},{20... | collective-permute-start | bytes 405512 | tf_op jit(solution)/shard_map/ppermute | solution.py:153
  38.5 0.7 copy-start.11
  38.5 0.7 copy-start.12
  38.5 0.8 copy-start.13
  39.3 0.7 copy-start.14
  65.1 38.9 %all-to-all-start.1 = ((f32[16,256,128]{2,1,0:T(8,128)}), f32[16,256,128]{2,1,0:T(8,128)S(1)}, u32[]{:S(2)}, u32[]{:S(2)}) async-start(f32[16,256,128]{2,1,0:T(8,128)} %get-tuple-element.14), calls=%async_computation.1 | async-start | bytes 4194304 | tf_op jit(solution)/shard_map/all_to_all | solution.py:176
  72.1 1.9 %collective-permute-start.15 = (f32[4,2,128,128]{3,2,1,0:T(8,128)S(1)}, f32[4,2,128,128]{3,2,1,0:T(8,128)S(1)}, u32[]{:S(2)}, u32[]{:S(2)}) collective-permute-start(f32[4,2,128,128]{3,2,1,0:T(8,128)S(1)} %get-tuple-element.13), channel_id=1, source_target_pairs={{0,16},{16,0},{1,17},{17,1},{2,18},{18,2},{3,19},{19,3},{4,20},{20... | collective-permute-start | bytes 1572872 | tf_op jit(solution)/shard_map/ppermute | solution.py:153
  74.2 9.9 %collective-permute-start.17 = (f32[2,128,128]{2,1,0:T(8,128)S(1)}, f32[2,128,128]{2,1,0:T(8,128)S(1)}, u32[]{:S(2)}, u32[]{:S(2)}) collective-permute-start(f32[2,128,128]{2,1,0:T(8,128)S(1)} %get-tuple-element.17), channel_id=1, source_target_pairs={{0,1},{1,2},{2,3},{3,4},{4,5},{5,6},{6,7},{7,0},{16,23},{17,16},{1... | collective-permute-start | bytes 393224 | tf_op jit(solution)/shard_map/ppermute | solution.py:159
  76.2 14.9 %collective-permute-start.19 = (f32[2,128,128]{2,1,0:T(8,128)S(1)}, f32[2,128,128]{2,1,0:T(8,128)S(1)}, u32[]{:S(2)}, u32[]{:S(2)}) collective-permute-start(f32[2,128,128]{2,1,0:T(8,128)S(1)} %get-tuple-element.18), channel_id=1, source_target_pairs={{0,3},{1,4},{2,5},{3,6},{4,7},{5,0},{6,1},{7,2},{16,21},{17,22},{1... | collective-permute-start | bytes 393224 | tf_op jit(solution)/shard_map/ppermute | solution.py:159
  82.0 9.3 %collective-permute-start.18 = (f32[2,128,128]{2,1,0:T(8,128)S(1)}, f32[2,128,128]{2,1,0:T(8,128)S(1)}, u32[]{:S(2)}, u32[]{:S(2)}) collective-permute-start(f32[2,128,128]{2,1,0:T(8,128)S(1)} %get-tuple-element.19), channel_id=1, source_target_pairs={{0,2},{1,3},{2,4},{3,5},{4,6},{5,7},{6,0},{7,1},{16,22},{17,23},{1... | collective-permute-start | bytes 393224 | tf_op jit(solution)/shard_map/ppermute | solution.py:159
  83.5 10.4 %collective-permute-start.16 = (f32[128,128]{1,0:T(8,128)S(1)}, f32[128,128]{1,0:T(8,128)S(1)}, u32[]{:S(2)}, u32[]{:S(2)}) collective-permute-start(f32[128,128]{1,0:T(8,128)S(1)} %slice_bitcast_fusion.3), channel_id=1, source_target_pairs={{0,4},{1,5},{2,6},{3,7},{4,0},{5,1},{6,2},{7,3},{16,20},{17,21},{1... | collective-permute-start | bytes 196616 | tf_op jit(solution)/shard_map/ppermute | solution.py:159
  91.3 2.6 %collective-permute-start.20 = (f32[128,128]{1,0:T(8,128)S(1)}, f32[128,128]{1,0:T(8,128)S(1)}, u32[]{:S(2)}, u32[]{:S(2)}) collective-permute-start(f32[128,128]{1,0:T(8,128)S(1)} %fusion), channel_id=1, source_target_pairs={{0,16},{16,0},{1,17},{17,1},{2,18},{18,2},{3,19},{19,3},{4,20},{20... | collective-permute-start | bytes 196616 | tf_op jit(solution)/shard_map/ppermute | solution.py:153

commit v4 on v3

--- a/solution.py
+++ b/solution.py
@@ -82,19 +82,15 @@
 
 def tile_kernel(*refs):
     packs, kv_ref, mine, theirs, dkv_ref = refs[:BLOCKS], *refs[BLOCKS : BLOCKS + 4]
-    q_turned, g_turned, q_all, g_all, dq, local, sems = refs[BLOCKS + 4 :]
+    q_turned, g_turned, q_all, g_all, dq = refs[BLOCKS + 4 :]
     step = pl.program_id(0)
 
     @pl.when(step == 0)
     def _():
-        copies = [pltpu.make_async_copy(packs[b], local.at[b], sems.at[b]) for b in range(BLOCKS)]
-        for copy in copies:
-            copy.start()
         for b in range(BLOCKS):
-            copies[b].wait()
             at = slice(b * ROWS, (b + 1) * ROWS)
-            load_block(local.at[b], 0, SCALE * LOG2E, 2 * ROWS, LOG2E, at, q_turned, q_all)
-            load_block(local.at[b], ROWS, 1.0, 2 * ROWS + 1, 1.0, at, g_turned, g_all)
+            load_block(packs[b], 0, SCALE * LOG2E, 2 * ROWS, LOG2E, at, q_turned, q_all)
+            load_block(packs[b], ROWS, 1.0, 2 * ROWS + 1, 1.0, at, g_turned, g_all)
         dq[...] = jnp.zeros_like(dq)
 
     ones = (lax.broadcasted_iota(jnp.int32, (D, TK), 0) < 3).astype(F32).astype(BF16)
@@ -138,12 +134,12 @@
     return pl.pallas_call(
         tile_kernel,
         grid=(TOKENS // TK,),
-        in_specs=[pl.BlockSpec(memory_space=pl.ANY)] * BLOCKS + [block],
+        in_specs=[pl.BlockSpec((PACK, D), lambda i: (0, 0))] * BLOCKS + [block],
         out_specs=[pl.BlockSpec(half, lambda i: (0, 0, 0, 0))] * 2 + [block],
         out_shape=[shape(*half), shape(*half), pltpu.HBM((BLOCKS, 2 * ROWS, D), F32)],
         scratch_shapes=[pltpu.VMEM((2 * D, TOKENS), BF16)] * 2
         + [pltpu.VMEM((TOKENS, 4 * D), BF16)] * 2
-        + [pltpu.VMEM((TOKENS, D), F32), pltpu.VMEM((BLOCKS, PACK, D), F32), pltpu.SemaphoreType.DMA((BLOCKS,))],
+        + [pltpu.VMEM((TOKENS, D), F32)],
         compiler_params=pltpu.CompilerParams(vmem_limit_bytes=36 * 1024 * 1024),
         cost_estimate=pl.CostEstimate(flops=24_000_000_000, bytes_accessed=8 << 20, transcendentals=TOKENS * TOKENS),
     )(*packs, kv)
@@ -169,8 +165,9 @@
         a, b = along(a, 1), along(b, 1)
         packs += [swap(b), swap(a), b, a]
     far = along(a, 1)
-    packs = [own, far, other, swap(far)] + packs
-    packs = [pltpu.with_memory_space_constraint(x, pltpu.HBM) for x in packs]
+    far, *packs = lax.optimization_barrier((far, *packs))
+    packs = [pltpu.with_memory_space_constraint(x, pltpu.HBM) for x in [own, other] + packs]
+    packs = [packs[0], far, packs[1], swap(far)] + packs[2:]
     mine, theirs, dkv = tile_grads(packs, kv)
     dq = mine + swap(theirs)
     dkv = lax.all_to_all(dkv, PLANE, 0, 0)
@@ -180,8 +177,7 @@
     r4 = along(dq[0, 1], 4)
     query_grad = (dq[0, 0] + r4) + (r1[0] + r2[0] + r3[0]) + swap(r1[1] + r2[1] + r3[1])
     query_grad, dkv = lax.optimization_barrier((query_grad, dkv))
-    dkv = jnp.sum(dkv, axis=0)
-    return query_grad, dkv[:ROWS], dkv[ROWS:]
+    return query_grad, jnp.sum(dkv[:, :ROWS], axis=0), jnp.sum(dkv[:, ROWS:], axis=0)
 
 
 def solution(mesh):

time: 105 us -> 103 us (0.981)
  waiting for transfers between devices: 40.4 us -> 36.7 us
  starting transfers between devices: 33.3 us -> 36.9 us
  local copies, waits for them, and re-layouts: 2.15 us -> 0.43 us
    ppermute x10, starting transfers between devices: 4.77 us -> 8.14 us  [swap(): return lax.ppermute(x, 'c', SWAP)]
    ppermute x11, waiting for transfers between devices: 28.8 us -> 25.7 us  [along(): return lax.ppermute(x, COLUMN, pairs)]
    all_to_all x1, waiting for transfers between devices: 9.42 us -> 8 us  [on_device(): dkv = lax.all_to_all(dkv, PLANE, 0, 0)]
    unnamed x30 -> x28, local copies, waits for them, and re-layouts: 1.46 us -> 0.39 us
  transfers between devices with their start and end apart: 23 -> 23, of which waited for: 12 -> 13; matrix products, arithmetic and copies ran while one was open for 1% -> 1% of each run, Pallas kernels for 0% -> 0%
where the time goes in v4:
time: 103 us
  starting transfers between devices  36.9 us (36%)
  waiting for transfers between devices  36.7 us (36%)
  Pallas kernels  26.5 us (26%)
  other arithmetic  1.47 us (1%)
    ppermute x11, waiting for transfers between devices, along(): return lax.ppermute(x, COLUMN, pairs)  25.7 us
    pallas_call x1, Pallas kernels, tile_grads(): pl.pallas_call(tile_kernel, grid=(TOKENS // TK,), in_specs=[pl.BlockSpec(...  24 us
    ppermute x11, starting transfers between devices, along(): return lax.ppermute(x, COLUMN, pairs)  13.9 us
    ppermute x10, starting transfers between devices, swap(): return lax.ppermute(x, 'c', SWAP)  8.14 us
    all_to_all x1, waiting for transfers between devices, on_device(): dkv = lax.all_to_all(dkv, PLANE, 0, 0)  8 us
    all_to_all x1, starting transfers between devices, on_device(): kv = lax.all_to_all(kv, PLANE, 0, 0)  7.61 us
    all_to_all x1, starting transfers between devices, on_device(): dkv = lax.all_to_all(dkv, PLANE, 0, 0)  7.18 us
    ppermute x10, waiting for transfers between devices, swap(): return lax.ppermute(x, 'c', SWAP)  2.9 us
  transfers between devices with their start and end apart: 23, of which 13 were waited for; matrix products, arithmetic and copies ran while one was open for 1% of the time, Pallas kernels for 0%

profile of v4, /device:TPU:2, one launch (start us, length us, event | category | flops | bytes accessed | tf_op | source)
XLA Modules:
  0.0 102.7 jit_solution(15351935945397007030)
XLA Ops:
  0.6 2.5 %shard_map.85 = (f32[264,128]{1,0:T(8,128)}, f32[16,256,128]{2,1,0:T(8,128)}) custom-call(f32[128,128]{1,0:T(8,128)} %k.1, f32[128,128]{1,0:T(8,128)} %v.1, f32[128,128]{1,0:T(8,128)} %q.1, f32[128,128]{1,0:T(8,128)} %o.1, f32[128,128]{1,0:T(8,128)} %g.1, f32[1,128]{1,0:T(1,128)} %lse.1), custom_call_target="tpu_custom_call" | custom-call | tf_op jit(solution)/shard_map/pallas_call | solution.py:63
  3.1 7.6 %all-to-all-start = ((f32[16,256,128]{2,1,0:T(8,128)}), f32[16,256,128]{2,1,0:T(8,128)S(1)}, u32[]{:S(2)}, u32[]{:S(2)}) async-start(f32[16,256,128]{2,1,0:T(8,128)} %get-tuple-element.37), calls=%async_computation | async-start | bytes 4194304 | tf_op jit(solution)/shard_map/all_to_all | solution.py:161
  10.8 0.1 collective-permute-start.4
  10.9 2.0 %collective-permute-start = (f32[264,128]{1,0:T(8,128)S(1)}, f32[264,128]{1,0:T(8,128)S(1)}, u32[]{:S(2)}, u32[]{:S(2)}) collective-permute-start(f32[264,128]{1,0:T(8,128)S(1)} %copy-done), channel_id=1, source_target_pairs={{0,1},{1,2},{2,3},{3,4},{4,5},{5,6},{6,7},{7,0},{16,23},{17,16},{1... | collective-permute-start | bytes 405512 | tf_op jit(solution)/shard_map/ppermute | solution.py:155
  12.9 0.0 collective-permute-done.4.refs_2_
  12.9 1.9 %collective-permute-start.5 = (f32[264,128]{1,0:T(8,128)S(1)}, f32[264,128]{1,0:T(8,128)S(1)}, u32[]{:S(2)}, u32[]{:S(2)}) collective-permute-start(f32[264,128]{1,0:T(8,128)S(1)} %collective-permute-done.4.refs_2_), channel_id=1, source_target_pairs={{0,1},{1,2},{2,3},{3,4},{4,5},{5,6},{6,7},{7,0},{16,23},{17,16},{1... | collective-permute-start | bytes 405512 | tf_op jit(solution)/shard_map/ppermute | solution.py:155
  14.8 5.0 %collective-permute-done.refs_7_ = f32[264,128]{1,0:T(8,128)S(1)} collective-permute-done((f32[264,128]{1,0:T(8,128)S(1)}, f32[264,128]{1,0:T(8,128)S(1)}, u32[]{:S(2)}, u32[]{:S(2)}) %collective-permute-start) | collective-permute-done | bytes 135200 | tf_op jit(solution)/shard_map/ppermute | solution.py:155
  19.8 0.0 collective-permute-start.1
  19.8 1.4 %collective-permute-done.5.refs_6_ = f32[264,128]{1,0:T(8,128)S(1)} collective-permute-done((f32[264,128]{1,0:T(8,128)S(1)}, f32[264,128]{1,0:T(8,128)S(1)}, u32[]{:S(2)}, u32[]{:S(2)}) %collective-permute-start.5) | collective-permute-done | bytes 135200 | tf_op jit(solution)/shard_map/ppermute | solution.py:155
  21.2 0.0 collective-permute-start.8
  21.2 2.5 %collective-permute-start.7 = (f32[264,128]{1,0:T(8,128)S(1)}, f32[264,128]{1,0:T(8,128)S(1)}, u32[]{:S(2)}, u32[]{:S(2)}) collective-permute-start(f32[264,128]{1,0:T(8,128)S(1)} %collective-permute-done.refs_7_), channel_id=1, source_target_pairs={{0,16},{16,0},{1,17},{17,1},{2,18},{18,2},{3,19},{19,3},{4,20},{20... | collective-permute-start | bytes 405512 | tf_op jit(solution)/shard_map/ppermute | solution.py:149
  23.8 2.3 %collective-permute-done.1.refs_11_ = f32[264,128]{1,0:T(8,128)S(1)} collective-permute-done((f32[264,128]{1,0:T(8,128)S(1)}, f32[264,128]{1,0:T(8,128)S(1)}, u32[]{:S(2)}, u32[]{:S(2)}) %collective-permute-start.1) | collective-permute-done | bytes 135200 | tf_op jit(solution)/shard_map/ppermute | solution.py:155
  26.0 0.0 collective-permute-start.2
  26.0 1.7 %collective-permute-start.6 = (f32[264,128]{1,0:T(8,128)S(1)}, f32[264,128]{1,0:T(8,128)S(1)}, u32[]{:S(2)}, u32[]{:S(2)}) collective-permute-start(f32[264,128]{1,0:T(8,128)S(1)} %collective-permute-done.5.refs_6_), channel_id=1, source_target_pairs={{0,16},{16,0},{1,17},{17,1},{2,18},{18,2},{3,19},{19,3},{4,20},{20... | collective-permute-start | bytes 405512 | tf_op jit(solution)/shard_map/ppermute | solution.py:149
  27.7 0.0 collective-permute-done.8.refs_10_
  27.7 0.0 collective-permute-start.11
  27.7 1.8 %collective-permute-start.10 = (f32[264,128]{1,0:T(8,128)S(1)}, f32[264,128]{1,0:T(8,128)S(1)}, u32[]{:S(2)}, u32[]{:S(2)}) collective-permute-start(f32[264,128]{1,0:T(8,128)S(1)} %collective-permute-done.1.refs_11_), channel_id=1, source_target_pairs={{0,16},{16,0},{1,17},{17,1},{2,18},{18,2},{3,19},{19,3},{4,20},{20... | collective-permute-start | bytes 405512 | tf_op jit(solution)/shard_map/ppermute | solution.py:149
  29.5 0.0 collective-permute-done.7.refs_5_
  29.5 0.1 collective-permute-start.9
  29.6 2.6 %collective-permute-done.2.refs_15_ = f32[264,128]{1,0:T(8,128)S(1)} collective-permute-done((f32[264,128]{1,0:T(8,128)S(1)}, f32[264,128]{1,0:T(8,128)S(1)}, u32[]{:S(2)}, u32[]{:S(2)}) %collective-permute-start.2) | collective-permute-done | bytes 135200 | tf_op jit(solution)/shard_map/ppermute | solution.py:155
  32.2 0.0 collective-permute-start.13
  32.2 0.0 collective-permute-done.6.refs_4_
  32.3 0.1 collective-permute-start.3
  32.4 1.5 %collective-permute-done.11.refs_14_ = f32[264,128]{1,0:T(8,128)S(1)} collective-permute-done((f32[264,128]{1,0:T(8,128)S(1)}, f32[264,128]{1,0:T(8,128)S(1)}, u32[]{:S(2)}, u32[]{:S(2)}) %collective-permute-start.11) | collective-permute-done | bytes 135200 | tf_op jit(solution)/shard_map/ppermute | solution.py:155
  33.9 0.0 collective-permute-start.12
  33.9 0.0 collective-permute-done.9.refs_8_
  34.0 4.6 %collective-permute-done.3.refs_1_ = f32[264,128]{1,0:T(8,128)S(1)} collective-permute-done((f32[264,128]{1,0:T(8,128)S(1)}, f32[264,128]{1,0:T(8,128)S(1)}, u32[]{:S(2)}, u32[]{:S(2)}) %collective-permute-start.3) | collective-permute-done | bytes 135200 | tf_op jit(solution)/shard_map/ppermute | solution.py:155
  38.6 0.0 collective-permute-done.12.refs_12_
  38.6 0.3 collective-permute-start.14
  38.9 0.3 copy-done.13
  39.2 1.0 collective-permute-done.14.refs_3_
  40.2 0.1 all-to-all-done.refs_16_
  40.3 24.0 %shard_map.86 = (f32[4,2,128,128]{3,2,1,0:T(8,128)S(1)}, f32[4,2,128,128]{3,2,1,0:T(8,128)S(1)}, f32[16,256,128]{2,1,0:T(8,128)}) custom-call(f32[264,128]{1,0:T(8,128)} %get-tuple-element.23.refs_0_, f32[264,128]{1,0:T(8,128)S(1)} %collective-permute-done.3.refs_1_, f32[264,128]{1,0:T(8,128)} %copy-done.1, f32[264,128]{1,0:T(8,128)S(1)} %collective-permute-done.14.refs_3_, ...), custom_call_target="tpu_custom_call" | custom-call | flops 24000000000 | bytes 8388608 | tf_op jit(solution)/shard_map/pallas_call | solution.py:134
  64.3 7.2 %all-to-all-start.1 = ((f32[16,256,128]{2,1,0:T(8,128)}), f32[16,256,128]{2,1,0:T(8,128)S(1)}, u32[]{:S(2)}, u32[]{:S(2)}) async-start(f32[16,256,128]{2,1,0:T(8,128)} %get-tuple-element.40), calls=%async_computation.1 | async-start | bytes 4194304 | tf_op jit(solution)/shard_map/all_to_all | solution.py:173
  71.5 0.0 collective-permute-start.15
  71.5 1.9 %collective-permute-done.15 = f32[4,2,128,128]{3,2,1,0:T(8,128)S(1)} collective-permute-done((f32[4,2,128,128]{3,2,1,0:T(8,128)S(1)}, f32[4,2,128,128]{3,2,1,0:T(8,128)S(1)}, u32[]{:S(2)}, u32[]{:S(2)}) %collective-permute-start.15) | collective-permute-done | bytes 524320 | tf_op jit(solution)/shard_map/ppermute | solution.py:149
  73.4 0.1 add.32
  73.5 2.1 %collective-permute-start.17 = (f32[2,128,128]{2,1,0:T(8,128)S(1)}, f32[2,128,128]{2,1,0:T(8,128)S(1)}, u32[]{:S(2)}, u32[]{:S(2)}) collective-permute-start(f32[2,128,128]{2,1,0:T(8,128)S(1)} %get-tuple-element.45), channel_id=1, source_target_pairs={{0,1},{1,2},{2,3},{3,4},{4,5},{5,6},{6,7},{7,0},{16,23},{17,16},{1... | collective-permute-start | bytes 393224 | tf_op jit(solution)/shard_map/ppermute | solution.py:155
  75.6 5.8 %collective-permute-start.19 = (f32[2,128,128]{2,1,0:T(8,128)S(1)}, f32[2,128,128]{2,1,0:T(8,128)S(1)}, u32[]{:S(2)}, u32[]{:S(2)}) collective-permute-start(f32[2,128,128]{2,1,0:T(8,128)S(1)} %get-tuple-element.46), channel_id=1, source_target_pairs={{0,3},{1,4},{2,5},{3,6},{4,7},{5,0},{6,1},{7,2},{16,21},{17,22},{1... | collective-permute-start | bytes 393224 | tf_op jit(solution)/shard_map/ppermute | solution.py:155
  81.4 1.5 %collective-permute-start.18 = (f32[2,128,128]{2,1,0:T(8,128)S(1)}, f32[2,128,128]{2,1,0:T(8,128)S(1)}, u32[]{:S(2)}, u32[]{:S(2)}) collective-permute-start(f32[2,128,128]{2,1,0:T(8,128)S(1)} %get-tuple-element.47), channel_id=1, source_target_pairs={{0,2},{1,3},{2,4},{3,5},{4,6},{5,7},{6,0},{7,1},{16,22},{17,23},{1... | collective-permute-start | bytes 393224 | tf_op jit(solution)/shard_map/ppermute | solution.py:155
  82.9 0.5 collective-permute-start.16
  83.4 7.0 %collective-permute-done.19 = f32[2,128,128]{2,1,0:T(8,128)S(1)} collective-permute-done((f32[2,128,128]{2,1,0:T(8,128)S(1)}, f32[2,128,128]{2,1,0:T(8,128)S(1)}, u32[]{:S(2)}, u32[]{:S(2)}) %collective-permute-start.19) | collective-permute-done | bytes 131104 | tf_op jit(solution)/shard_map/ppermute | solution.py:155
  90.4 0.2 collective-permute-done.18
  90.7 1.7 %collective-permute-start.20 = (f32[128,128]{1,0:T(8,128)S(1)}, f32[128,128]{1,0:T(8,128)S(1)}, u32[]{:S(2)}, u32[]{:S(2)}) collective-permute-start(f32[128,128]{1,0:T(8,128)S(1)} %fusion), channel_id=1, source_target_pairs={{0,16},{16,0},{1,17},{17,1},{2,18},{18,2},{3,19},{19,3},{4,20},{20... | collective-permute-start | bytes 196616 | tf_op jit(solution)/shard_map/ppermute | solution.py:149
  92.4 0.9 collective-permute-done.16
  93.3 0.7 fusion.3
  94.0 8.0 %all-to-all-done.1 = f32[16,256,128]{2,1,0:T(8,128)S(1)} async-done(((f32[16,256,128]{2,1,0:T(8,128)}), f32[16,256,128]{2,1,0:T(8,128)S(1)}, u32[]{:S(2)}, u32[]{:S(2)}) %all-to-all-start.1) | async-done | bytes 2097184 | tf_op jit(solution)/shard_map/all_to_all | solution.py:173
  102.0 0.7 slice_reduce_fusion
  (34 shorter events, 0.1 us)
Async XLA Ops:
  3.1 7.6 %copy-start = (f32[264,128]{1,0:T(8,128)S(1)}, f32[264,128]{1,0:T(8,128)}, u32[]{:S(2)}) copy-start(f32[264,128]{1,0:T(8,128)} %get-tuple-element.23.refs_0_) | copy-start | bytes 405508
  3.1 37.2 %all-to-all-start = ((f32[16,256,128]{2,1,0:T(8,128)}), f32[16,256,128]{2,1,0:T(8,128)S(1)}, u32[]{:S(2)}, u32[]{:S(2)}) async-start(f32[16,256,128]{2,1,0:T(8,128)} %get-tuple-element.37), calls=%async_computation | async-start | bytes 4194304 | tf_op jit(solution)/shard_map/all_to_all | solution.py:161
  10.8 2.1 %collective-permute-start.4 = (f32[264,128]{1,0:T(8,128)S(1)}, f32[264,128]{1,0:T(8,128)S(1)}, u32[]{:S(2)}, u32[]{:S(2)}) collective-permute-start(f32[264,128]{1,0:T(8,128)S(1)} %copy-done), channel_id=1, source_target_pairs={{0,16},{16,0},{1,17},{17,1},{2,18},{18,2},{3,19},{19,3},{4,20},{20... | collective-permute-start | bytes 405512 | tf_op jit(solution)/shard_map/ppermute | solution.py:149
  10.9 8.9 %collective-permute-start = (f32[264,128]{1,0:T(8,128)S(1)}, f32[264,128]{1,0:T(8,128)S(1)}, u32[]{:S(2)}, u32[]{:S(2)}) collective-permute-start(f32[264,128]{1,0:T(8,128)S(1)} %copy-done), channel_id=1, source_target_pairs={{0,1},{1,2},{2,3},{3,4},{4,5},{5,6},{6,7},{7,0},{16,23},{17,16},{1... | collective-permute-start | bytes 405512 | tf_op jit(solution)/shard_map/ppermute | solution.py:155
  12.9 19.4 %copy-start.1 = (f32[264,128]{1,0:T(8,128)}, f32[264,128]{1,0:T(8,128)S(1)}, u32[]{:S(2)}) copy-start(f32[264,128]{1,0:T(8,128)S(1)} %collective-permute-done.4.refs_2_) | copy-start | bytes 405508
  12.9 8.4 %collective-permute-start.5 = (f32[264,128]{1,0:T(8,128)S(1)}, f32[264,128]{1,0:T(8,128)S(1)}, u32[]{:S(2)}, u32[]{:S(2)}) collective-permute-start(f32[264,128]{1,0:T(8,128)S(1)} %collective-permute-done.4.refs_2_), channel_id=1, source_target_pairs={{0,1},{1,2},{2,3},{3,4},{4,5},{5,6},{6,7},{7,0},{16,23},{17,16},{1... | collective-permute-start | bytes 405512 | tf_op jit(solution)/shard_map/ppermute | solution.py:155
  19.8 20.4 %copy-start.2 = (f32[264,128]{1,0:T(8,128)}, f32[264,128]{1,0:T(8,128)S(1)}, u32[]{:S(2)}) copy-start(f32[264,128]{1,0:T(8,128)S(1)} %collective-permute-done.refs_7_) | copy-start | bytes 405508
  19.8 6.2 %collective-permute-start.1 = (f32[264,128]{1,0:T(8,128)S(1)}, f32[264,128]{1,0:T(8,128)S(1)}, u32[]{:S(2)}, u32[]{:S(2)}) collective-permute-start(f32[264,128]{1,0:T(8,128)S(1)} %collective-permute-done.refs_7_), channel_id=1, source_target_pairs={{0,1},{1,2},{2,3},{3,4},{4,5},{5,6},{6,7},{7,0},{16,23},{17,16},{1... | collective-permute-start | bytes 405512 | tf_op jit(solution)/shard_map/ppermute | solution.py:155
  21.2 19.0 %copy-start.3 = (f32[264,128]{1,0:T(8,128)}, f32[264,128]{1,0:T(8,128)S(1)}, u32[]{:S(2)}) copy-start(f32[264,128]{1,0:T(8,128)S(1)} %collective-permute-done.5.refs_6_) | copy-start | bytes 405508
  21.2 6.4 %collective-permute-start.8 = (f32[264,128]{1,0:T(8,128)S(1)}, f32[264,128]{1,0:T(8,128)S(1)}, u32[]{:S(2)}, u32[]{:S(2)}) collective-permute-start(f32[264,128]{1,0:T(8,128)S(1)} %collective-permute-done.5.refs_6_), channel_id=1, source_target_pairs={{0,1},{1,2},{2,3},{3,4},{4,5},{5,6},{6,7},{7,0},{16,23},{17,16},{1... | collective-permute-start | bytes 405512 | tf_op jit(solution)/shard_map/ppermute | solution.py:155
  21.2 8.2 %collective-permute-start.7 = (f32[264,128]{1,0:T(8,128)S(1)}, f32[264,128]{1,0:T(8,128)S(1)}, u32[]{:S(2)}, u32[]{:S(2)}) collective-permute-start(f32[264,128]{1,0:T(8,128)S(1)} %collective-permute-done.refs_7_), channel_id=1, source_target_pairs={{0,16},{16,0},{1,17},{17,1},{2,18},{18,2},{3,19},{19,3},{4,20},{20... | collective-permute-start | bytes 405512 | tf_op jit(solution)/shard_map/ppermute | solution.py:149
  26.0 14.3 %copy-start.4 = (f32[264,128]{1,0:T(8,128)}, f32[264,128]{1,0:T(8,128)S(1)}, u32[]{:S(2)}) copy-start(f32[264,128]{1,0:T(8,128)S(1)} %collective-permute-done.1.refs_11_) | copy-start | bytes 405508
  26.0 6.2 %collective-permute-start.2 = (f32[264,128]{1,0:T(8,128)S(1)}, f32[264,128]{1,0:T(8,128)S(1)}, u32[]{:S(2)}, u32[]{:S(2)}) collective-permute-start(f32[264,128]{1,0:T(8,128)S(1)} %collective-permute-done.1.refs_11_), channel_id=1, source_target_pairs={{0,1},{1,2},{2,3},{3,4},{4,5},{5,6},{6,7},{7,0},{16,23},{17,16},{1... | collective-permute-start | bytes 405512 | tf_op jit(solution)/shard_map/ppermute | solution.py:155
  26.0 6.2 %collective-permute-start.6 = (f32[264,128]{1,0:T(8,128)S(1)}, f32[264,128]{1,0:T(8,128)S(1)}, u32[]{:S(2)}, u32[]{:S(2)}) collective-permute-start(f32[264,128]{1,0:T(8,128)S(1)} %collective-permute-done.5.refs_6_), channel_id=1, source_target_pairs={{0,16},{16,0},{1,17},{17,1},{2,18},{18,2},{3,19},{19,3},{4,20},{20... | collective-permute-start | bytes 405512 | tf_op jit(solution)/shard_map/ppermute | solution.py:149
  27.7 12.5 %copy-start.5 = (f32[264,128]{1,0:T(8,128)}, f32[264,128]{1,0:T(8,128)S(1)}, u32[]{:S(2)}) copy-start(f32[264,128]{1,0:T(8,128)S(1)} %collective-permute-done.8.refs_10_) | copy-start | bytes 405508
  27.7 6.2 %collective-permute-start.11 = (f32[264,128]{1,0:T(8,128)S(1)}, f32[264,128]{1,0:T(8,128)S(1)}, u32[]{:S(2)}, u32[]{:S(2)}) collective-permute-start(f32[264,128]{1,0:T(8,128)S(1)} %collective-permute-done.8.refs_10_), channel_id=1, source_target_pairs={{0,1},{1,2},{2,3},{3,4},{4,5},{5,6},{6,7},{7,0},{16,23},{17,16},{1... | collective-permute-start | bytes 405512 | tf_op jit(solution)/shard_map/ppermute | solution.py:155
  27.7 6.2 %collective-permute-start.10 = (f32[264,128]{1,0:T(8,128)S(1)}, f32[264,128]{1,0:T(8,128)S(1)}, u32[]{:S(2)}, u32[]{:S(2)}) collective-permute-start(f32[264,128]{1,0:T(8,128)S(1)} %collective-permute-done.1.refs_11_), channel_id=1, source_target_pairs={{0,16},{16,0},{1,17},{17,1},{2,18},{18,2},{3,19},{19,3},{4,20},{20... | collective-permute-start | bytes 405512 | tf_op jit(solution)/shard_map/ppermute | solution.py:149
  29.5 10.7 %copy-start.6 = (f32[264,128]{1,0:T(8,128)}, f32[264,128]{1,0:T(8,128)S(1)}, u32[]{:S(2)}) copy-start(f32[264,128]{1,0:T(8,128)S(1)} %collective-permute-done.7.refs_5_) | copy-start | bytes 405508
  29.5 4.4 %collective-permute-start.9 = (f32[264,128]{1,0:T(8,128)S(1)}, f32[264,128]{1,0:T(8,128)S(1)}, u32[]{:S(2)}, u32[]{:S(2)}) collective-permute-start(f32[264,128]{1,0:T(8,128)S(1)} %collective-permute-done.8.refs_10_), channel_id=1, source_target_pairs={{0,16},{16,0},{1,17},{17,1},{2,18},{18,2},{3,19},{19,3},{4,20},{20... | collective-permute-start | bytes 405512 | tf_op jit(solution)/shard_map/ppermute | solution.py:149
  32.2 8.0 %copy-start.7 = (f32[264,128]{1,0:T(8,128)}, f32[264,128]{1,0:T(8,128)S(1)}, u32[]{:S(2)}) copy-start(f32[264,128]{1,0:T(8,128)S(1)} %collective-permute-done.2.refs_15_) | copy-start | bytes 405508
  32.2 1.7 %collective-permute-start.13 = (f32[264,128]{1,0:T(8,128)S(1)}, f32[264,128]{1,0:T(8,128)S(1)}, u32[]{:S(2)}, u32[]{:S(2)}) collective-permute-start(f32[264,128]{1,0:T(8,128)S(1)} %collective-permute-done.2.refs_15_), channel_id=1, source_target_pairs={{0,16},{16,0},{1,17},{17,1},{2,18},{18,2},{3,19},{19,3},{4,20},{20... | collective-permute-start | bytes 405512 | tf_op jit(solution)/shard_map/ppermute | solution.py:149
  32.3 8.0 %copy-start.8 = (f32[264,128]{1,0:T(8,128)}, f32[264,128]{1,0:T(8,128)S(1)}, u32[]{:S(2)}) copy-start(f32[264,128]{1,0:T(8,128)S(1)} %collective-permute-done.6.refs_4_) | copy-start | bytes 405508
  32.3 6.3 %collective-permute-start.3 = (f32[264,128]{1,0:T(8,128)S(1)}, f32[264,128]{1,0:T(8,128)S(1)}, u32[]{:S(2)}, u32[]{:S(2)}) collective-permute-start(f32[264,128]{1,0:T(8,128)S(1)} %collective-permute-done.2.refs_15_), channel_id=1, source_target_pairs={{0,1},{1,2},{2,3},{3,4},{4,5},{5,6},{6,7},{7,0},{16,23},{17,16},{1... | collective-permute-start | bytes 405512 | tf_op jit(solution)/shard_map/ppermute | solution.py:155
  33.9 6.3 %copy-start.9 = (f32[264,128]{1,0:T(8,128)}, f32[264,128]{1,0:T(8,128)S(1)}, u32[]{:S(2)}) copy-start(f32[264,128]{1,0:T(8,128)S(1)} %collective-permute-done.11.refs_14_) | copy-start | bytes 405508
  33.9 4.7 %collective-permute-start.12 = (f32[264,128]{1,0:T(8,128)S(1)}, f32[264,128]{1,0:T(8,128)S(1)}, u32[]{:S(2)}, u32[]{:S(2)}) collective-permute-start(f32[264,128]{1,0:T(8,128)S(1)} %collective-permute-done.11.refs_14_), channel_id=1, source_target_pairs={{0,16},{16,0},{1,17},{17,1},{2,18},{18,2},{3,19},{19,3},{4,20},{20... | collective-permute-start | bytes 405512 | tf_op jit(solution)/shard_map/ppermute | solution.py:149
  33.9 4.7 %copy-start.10 = (f32[264,128]{1,0:T(8,128)}, f32[264,128]{1,0:T(8,128)S(1)}, u32[]{:S(2)}) copy-start(f32[264,128]{1,0:T(8,128)S(1)} %collective-permute-done.10.refs_9_) | copy-start | bytes 405508
  33.9 4.9 %copy-start.11 = (f32[264,128]{1,0:T(8,128)}, f32[264,128]{1,0:T(8,128)S(1)}, u32[]{:S(2)}) copy-start(f32[264,128]{1,0:T(8,128)S(1)} %collective-permute-done.9.refs_8_) | copy-start | bytes 405508
  34.0 4.9 %copy-start.12 = (f32[264,128]{1,0:T(8,128)}, f32[264,128]{1,0:T(8,128)S(1)}, u32[]{:S(2)}) copy-start(f32[264,128]{1,0:T(8,128)S(1)} %collective-permute-done.13.refs_13_) | copy-start | bytes 405508
  38.6 0.6 copy-start.13
  38.6 1.6 %collective-permute-start.14 = (f32[264,128]{1,0:T(8,128)S(1)}, f32[264,128]{1,0:T(8,128)S(1)}, u32[]{:S(2)}, u32[]{:S(2)}) collective-permute-start(f32[264,128]{1,0:T(8,128)S(1)} %collective-permute-done.3.refs_1_), channel_id=1, source_target_pairs={{0,16},{16,0},{1,17},{17,1},{2,18},{18,2},{3,19},{19,3},{4,20},{20... | collective-permute-start | bytes 405512 | tf_op jit(solution)/shard_map/ppermute | solution.py:149
  64.3 37.7 %all-to-all-start.1 = ((f32[16,256,128]{2,1,0:T(8,128)}), f32[16,256,128]{2,1,0:T(8,128)S(1)}, u32[]{:S(2)}, u32[]{:S(2)}) async-start(f32[16,256,128]{2,1,0:T(8,128)} %get-tuple-element.40), calls=%async_computation.1 | async-start | bytes 4194304 | tf_op jit(solution)/shard_map/all_to_all | solution.py:173
  71.5 1.9 %collective-permute-start.15 = (f32[4,2,128,128]{3,2,1,0:T(8,128)S(1)}, f32[4,2,128,128]{3,2,1,0:T(8,128)S(1)}, u32[]{:S(2)}, u32[]{:S(2)}) collective-permute-start(f32[4,2,128,128]{3,2,1,0:T(8,128)S(1)} %get-tuple-element.39), channel_id=1, source_target_pairs={{0,16},{16,0},{1,17},{17,1},{2,18},{18,2},{3,19},{19,3},{4,20},{20... | collective-permute-start | bytes 1572872 | tf_op jit(solution)/shard_map/ppermute | solution.py:149
  73.5 9.9 %collective-permute-start.17 = (f32[2,128,128]{2,1,0:T(8,128)S(1)}, f32[2,128,128]{2,1,0:T(8,128)S(1)}, u32[]{:S(2)}, u32[]{:S(2)}) collective-permute-start(f32[2,128,128]{2,1,0:T(8,128)S(1)} %get-tuple-element.45), channel_id=1, source_target_pairs={{0,1},{1,2},{2,3},{3,4},{4,5},{5,6},{6,7},{7,0},{16,23},{17,16},{1... | collective-permute-start | bytes 393224 | tf_op jit(solution)/shard_map/ppermute | solution.py:155
  75.6 14.9 %collective-permute-start.19 = (f32[2,128,128]{2,1,0:T(8,128)S(1)}, f32[2,128,128]{2,1,0:T(8,128)S(1)}, u32[]{:S(2)}, u32[]{:S(2)}) collective-permute-start(f32[2,128,128]{2,1,0:T(8,128)S(1)} %get-tuple-element.46), channel_id=1, source_target_pairs={{0,3},{1,4},{2,5},{3,6},{4,7},{5,0},{6,1},{7,2},{16,21},{17,22},{1... | collective-permute-start | bytes 393224 | tf_op jit(solution)/shard_map/ppermute | solution.py:155
  81.4 9.3 %collective-permute-start.18 = (f32[2,128,128]{2,1,0:T(8,128)S(1)}, f32[2,128,128]{2,1,0:T(8,128)S(1)}, u32[]{:S(2)}, u32[]{:S(2)}) collective-permute-start(f32[2,128,128]{2,1,0:T(8,128)S(1)} %get-tuple-element.47), channel_id=1, source_target_pairs={{0,2},{1,3},{2,4},{3,5},{4,6},{5,7},{6,0},{7,1},{16,22},{17,23},{1... | collective-permute-start | bytes 393224 | tf_op jit(solution)/shard_map/ppermute | solution.py:155
  82.9 10.5 %collective-permute-start.16 = (f32[128,128]{1,0:T(8,128)S(1)}, f32[128,128]{1,0:T(8,128)S(1)}, u32[]{:S(2)}, u32[]{:S(2)}) collective-permute-start(f32[128,128]{1,0:T(8,128)S(1)} %slice_bitcast_fusion.3), channel_id=1, source_target_pairs={{0,4},{1,5},{2,6},{3,7},{4,0},{5,1},{6,2},{7,3},{16,20},{17,21},{1... | collective-permute-start | bytes 196616 | tf_op jit(solution)/shard_map/ppermute | solution.py:155
  90.7 2.6 %collective-permute-start.20 = (f32[128,128]{1,0:T(8,128)S(1)}, f32[128,128]{1,0:T(8,128)S(1)}, u32[]{:S(2)}, u32[]{:S(2)}) collective-permute-start(f32[128,128]{1,0:T(8,128)S(1)} %fusion), channel_id=1, source_target_pairs={{0,16},{16,0},{1,17},{17,1},{2,18},{18,2},{3,19},{19,3},{4,20},{20... | collective-permute-start | bytes 196616 | tf_op jit(solution)/shard_map/ppermute | solution.py:149

commit v5 on v4

--- a/solution.py
+++ b/solution.py
@@ -15,7 +15,7 @@
 F32 = jnp.float32
 
 AXES = ("xh", "y", "c", "xl", "z")
-PLANE = ("xh", "y", "xl")
+PLANE = ("xl", "xh", "y")
 COLUMN = ("c", "z")
 DEPTH = 8
 ROWS = 128
@@ -155,19 +155,25 @@
     return lax.ppermute(x, COLUMN, pairs)
 
 
+def across(x):
+    pairs = [(DEPTH + z, (z + 1) % DEPTH) for z in range(DEPTH)]
+    pairs += [(z, DEPTH + (z - 1) % DEPTH) for z in range(DEPTH)]
+    return lax.ppermute(x, COLUMN, pairs)
+
+
 def on_device(query, keys, values, attn_out, out_grad, row_lse):
     own, kv = pack(query, keys, values, attn_out, out_grad, row_lse)
+    kv = lax.all_to_all(kv, PLANE, 0, 0)
     other = swap(own)
-    kv = lax.all_to_all(kv, PLANE, 0, 0)
-    a, b = own, other
-    packs = []
-    for j in range(1, CHUNKS):
+    a, b = along(own, 1), across(own)
+    packs = [own, other, swap(b), swap(a), b, a]
+    for _ in range(2, CHUNKS):
         a, b = along(a, 1), along(b, 1)
         packs += [swap(b), swap(a), b, a]
     far = along(a, 1)
-    far, *packs = lax.optimization_barrier((far, *packs))
-    packs = [pltpu.with_memory_space_constraint(x, pltpu.HBM) for x in [own, other] + packs]
-    packs = [packs[0], far, packs[1], swap(far)] + packs[2:]
+    far_other = along(b, 1)
+    packs = [pltpu.with_memory_space_constraint(x, pltpu.HBM) for x in packs]
+    packs = [packs[0], far, packs[1], far_other] + packs[2:]
     mine, theirs, dkv = tile_grads(packs, kv)
     dq = mine + swap(theirs)
     dkv = lax.all_to_all(dkv, PLANE, 0, 0)

time: 103 us -> 98.8 us (0.959); the launches traced: 103 us -> 97 us
  starting transfers between devices: 36.9 us -> 32.3 us
  waiting for transfers between devices: 36.7 us -> 35.1 us
    ppermute x11, starting transfers between devices: 13.9 us -> 7.43 us  [along(): return lax.ppermute(x, COLUMN, pairs)]
    ppermute x0 -> x1, starting transfers between devices: none -> 4.82 us  [across(): return lax.ppermute(x, COLUMN, pairs)]
    all_to_all x1, waiting for transfers between devices: 8 us -> 4.48 us  [on_device(): dkv = lax.all_to_all(dkv, PLANE, 0, 0)]
    ppermute x0 -> x1, waiting for transfers between devices: none -> 3.49 us  [across(): return lax.ppermute(x, COLUMN, pairs)]
    ppermute x10 -> x9, starting transfers between devices: 8.14 us -> 5.25 us  [swap(): return lax.ppermute(x, 'c', SWAP)]
    ppermute x10 -> x9, waiting for transfers between devices: 2.9 us -> 1.92 us  [swap(): return lax.ppermute(x, 'c', SWAP)]
  transfers between devices with their start and end apart: 23 -> 23, of which waited for: 13 -> 14; matrix products, arithmetic and copies ran while one was open for 1% -> 1% of each run, Pallas kernels for 0% -> 0%
where the time goes in v5:
time: 98.8 us; the launch traced here: 97 us
  waiting for transfers between devices  35.1 us (36%)
  starting transfers between devices  32.3 us (33%)
  Pallas kernels  26.5 us (27%)
  other arithmetic  1.47 us (1%)
    ppermute x11, waiting for transfers between devices, along(): return lax.ppermute(x, COLUMN, pairs)  25.2 us
    pallas_call x1, Pallas kernels, tile_grads(): pl.pallas_call(tile_kernel, grid=(TOKENS // TK,), in_specs=[pl.BlockSpec(...  24 us
    all_to_all x1, starting transfers between devices, on_device(): kv = lax.all_to_all(kv, PLANE, 0, 0)  7.61 us
    ppermute x11, starting transfers between devices, along(): return lax.ppermute(x, COLUMN, pairs)  7.43 us
    all_to_all x1, starting transfers between devices, on_device(): dkv = lax.all_to_all(dkv, PLANE, 0, 0)  7.22 us
    ppermute x9, starting transfers between devices, swap(): return lax.ppermute(x, 'c', SWAP)  5.25 us
    ppermute x1, starting transfers between devices, across(): return lax.ppermute(x, COLUMN, pairs)  4.82 us
    all_to_all x1, waiting for transfers between devices, on_device(): dkv = lax.all_to_all(dkv, PLANE, 0, 0)  4.48 us
  transfers between devices with their start and end apart: 23, of which 14 were waited for; matrix products, arithmetic and copies ran while one was open for 1% of the time, Pallas kernels for 0%

profile of v5, /device:TPU:2, one launch (start us, length us, event | category | flops | bytes accessed | tf_op | source)
XLA Modules:
  0.0 97.0 jit_solution(2399059861665873098)
XLA Ops:
  0.6 2.5 %shard_map.85 = (f32[264,128]{1,0:T(8,128)}, f32[16,256,128]{2,1,0:T(8,128)}) custom-call(f32[128,128]{1,0:T(8,128)} %k.1, f32[128,128]{1,0:T(8,128)} %v.1, f32[128,128]{1,0:T(8,128)} %q.1, f32[128,128]{1,0:T(8,128)} %o.1, f32[128,128]{1,0:T(8,128)} %g.1, f32[1,128]{1,0:T(1,128)} %lse.1), custom_call_target="tpu_custom_call" | custom-call | tf_op jit(solution)/shard_map/pallas_call | solution.py:63
  3.1 7.6 %all-to-all-start = ((f32[16,256,128]{2,1,0:T(8,128)}), f32[16,256,128]{2,1,0:T(8,128)S(1)}, u32[]{:S(2)}, u32[]{:S(2)}) async-start(f32[16,256,128]{2,1,0:T(8,128)} %get-tuple-element.11), calls=%async_computation | async-start | bytes 4194304 | tf_op jit(solution)/shard_map/all_to_all | solution.py:166
  10.8 4.8 %collective-permute-start.5 = (f32[264,128]{1,0:T(8,128)S(1)}, f32[264,128]{1,0:T(8,128)S(1)}, u32[]{:S(2)}, u32[]{:S(2)}) collective-permute-start(f32[264,128]{1,0:T(8,128)S(1)} %copy-done), channel_id=1, source_target_pairs={{16,1},{17,2},{18,3},{19,4},{20,5},{21,6},{22,7},{23,0},{0,23},{1,... | collective-permute-start | bytes 405512 | tf_op jit(solution)/shard_map/ppermute | solution.py:161
  15.6 0.0 collective-permute-start
  15.6 3.5 %collective-permute-done.5.refs_6_ = f32[264,128]{1,0:T(8,128)S(1)} collective-permute-done((f32[264,128]{1,0:T(8,128)S(1)}, f32[264,128]{1,0:T(8,128)S(1)}, u32[]{:S(2)}, u32[]{:S(2)}) %collective-permute-start.5) | collective-permute-done | bytes 135200 | tf_op jit(solution)/shard_map/ppermute | solution.py:161
  19.1 0.0 collective-permute-start.6
  19.1 2.7 %collective-permute-done.refs_7_ = f32[264,128]{1,0:T(8,128)S(1)} collective-permute-done((f32[264,128]{1,0:T(8,128)S(1)}, f32[264,128]{1,0:T(8,128)S(1)}, u32[]{:S(2)}, u32[]{:S(2)}) %collective-permute-start) | collective-permute-done | bytes 135200 | tf_op jit(solution)/shard_map/ppermute | solution.py:155
  21.8 0.9 collective-permute-start.4
  22.7 0.1 collective-permute-start.9
  22.8 2.5 %collective-permute-done.6.refs_10_ = f32[264,128]{1,0:T(8,128)S(1)} collective-permute-done((f32[264,128]{1,0:T(8,128)S(1)}, f32[264,128]{1,0:T(8,128)S(1)}, u32[]{:S(2)}, u32[]{:S(2)}) %collective-permute-start.6) | collective-permute-done | bytes 135200 | tf_op jit(solution)/shard_map/ppermute | solution.py:155
  25.3 0.0 collective-permute-start.7
  25.3 2.7 %collective-permute-start.10 = (f32[264,128]{1,0:T(8,128)S(1)}, f32[264,128]{1,0:T(8,128)S(1)}, u32[]{:S(2)}, u32[]{:S(2)}) collective-permute-start(f32[264,128]{1,0:T(8,128)S(1)} %collective-permute-done.refs_7_), channel_id=1, source_target_pairs={{0,16},{16,0},{1,17},{17,1},{2,18},{18,2},{3,19},{19,3},{4,20},{20... | collective-permute-start | bytes 405512 | tf_op jit(solution)/shard_map/ppermute | solution.py:149
  28.0 0.1 collective-permute-done.1.refs_11_
  28.0 0.0 collective-permute-done.4.refs_2_
  28.1 1.4 %collective-permute-start.11 = (f32[264,128]{1,0:T(8,128)S(1)}, f32[264,128]{1,0:T(8,128)S(1)}, u32[]{:S(2)}, u32[]{:S(2)}) collective-permute-start(f32[264,128]{1,0:T(8,128)S(1)} %collective-permute-done.6.refs_10_), channel_id=1, source_target_pairs={{0,16},{16,0},{1,17},{17,1},{2,18},{18,2},{3,19},{19,3},{4,20},{20... | collective-permute-start | bytes 405512 | tf_op jit(solution)/shard_map/ppermute | solution.py:149
  29.4 0.1 collective-permute-start.12
  29.5 2.0 %collective-permute-done.7.refs_14_ = f32[264,128]{1,0:T(8,128)S(1)} collective-permute-done((f32[264,128]{1,0:T(8,128)S(1)}, f32[264,128]{1,0:T(8,128)S(1)}, u32[]{:S(2)}, u32[]{:S(2)}) %collective-permute-start.7) | collective-permute-done | bytes 135200 | tf_op jit(solution)/shard_map/ppermute | solution.py:155
  31.5 0.0 collective-permute-start.13
  31.5 0.0 collective-permute-done.10.refs_5_
  31.6 0.1 collective-permute-start.8
  31.7 2.6 %collective-permute-done.2.refs_15_ = f32[264,128]{1,0:T(8,128)S(1)} collective-permute-done((f32[264,128]{1,0:T(8,128)S(1)}, f32[264,128]{1,0:T(8,128)S(1)}, u32[]{:S(2)}, u32[]{:S(2)}) %collective-permute-start.2) | collective-permute-done | bytes 135200 | tf_op jit(solution)/shard_map/ppermute | solution.py:155
  34.3 0.0 collective-permute-start.14
  34.3 0.0 collective-permute-done.11.refs_8_
  34.3 0.3 collective-permute-start.3
  34.6 0.0 collective-permute-done.12.refs_9_
  34.6 0.0 collective-permute-done.13.refs_12_
  34.6 3.3 %collective-permute-done.8.refs_3_ = f32[264,128]{1,0:T(8,128)S(1)} collective-permute-done((f32[264,128]{1,0:T(8,128)S(1)}, f32[264,128]{1,0:T(8,128)S(1)}, u32[]{:S(2)}, u32[]{:S(2)}) %collective-permute-start.8) | collective-permute-done | bytes 135200 | tf_op jit(solution)/shard_map/ppermute | solution.py:155
  37.9 0.0 collective-permute-done.14.refs_13_
  37.9 0.6 copy-done.13
  38.5 2.2 %collective-permute-done.3.refs_1_ = f32[264,128]{1,0:T(8,128)S(1)} collective-permute-done((f32[264,128]{1,0:T(8,128)S(1)}, f32[264,128]{1,0:T(8,128)S(1)}, u32[]{:S(2)}, u32[]{:S(2)}) %collective-permute-start.3) | collective-permute-done | bytes 135200 | tf_op jit(solution)/shard_map/ppermute | solution.py:155
  40.8 24.0 %shard_map.86 = (f32[4,2,128,128]{3,2,1,0:T(8,128)S(1)}, f32[4,2,128,128]{3,2,1,0:T(8,128)S(1)}, f32[16,256,128]{2,1,0:T(8,128)}) custom-call(f32[264,128]{1,0:T(8,128)} %get-tuple-element.10.refs_0_, f32[264,128]{1,0:T(8,128)S(1)} %collective-permute-done.3.refs_1_, f32[264,128]{1,0:T(8,128)} %copy-done.5, f32[264,128]{1,0:T(8,128)S(1)} %collective-permute-done.8.refs_3_, ...), custom_call_target="tpu_custom_call" | custom-call | flops 24000000000 | bytes 8388608 | tf_op jit(solution)/shard_map/pallas_call | solution.py:134
  64.8 7.2 %all-to-all-start.1 = ((f32[16,256,128]{2,1,0:T(8,128)}), f32[16,256,128]{2,1,0:T(8,128)S(1)}, u32[]{:S(2)}, u32[]{:S(2)}) async-start(f32[16,256,128]{2,1,0:T(8,128)} %get-tuple-element.14), calls=%async_computation.1 | async-start | bytes 4194304 | tf_op jit(solution)/shard_map/all_to_all | solution.py:179
  72.0 0.0 collective-permute-start.15
  72.0 1.9 %collective-permute-done.15 = f32[4,2,128,128]{3,2,1,0:T(8,128)S(1)} collective-permute-done((f32[4,2,128,128]{3,2,1,0:T(8,128)S(1)}, f32[4,2,128,128]{3,2,1,0:T(8,128)S(1)}, u32[]{:S(2)}, u32[]{:S(2)}) %collective-permute-start.15) | collective-permute-done | bytes 524320 | tf_op jit(solution)/shard_map/ppermute | solution.py:149
  73.9 0.1 add.32
  74.0 0.3 collective-permute-start.17
  74.3 4.7 %collective-permute-start.19 = (f32[2,128,128]{2,1,0:T(8,128)S(1)}, f32[2,128,128]{2,1,0:T(8,128)S(1)}, u32[]{:S(2)}, u32[]{:S(2)}) collective-permute-start(f32[2,128,128]{2,1,0:T(8,128)S(1)} %get-tuple-element.20), channel_id=1, source_target_pairs={{0,3},{1,4},{2,5},{3,6},{4,7},{5,0},{6,1},{7,2},{16,21},{17,22},{1... | collective-permute-start | bytes 393224 | tf_op jit(solution)/shard_map/ppermute | solution.py:155
  79.1 0.0 collective-permute-start.18
  79.1 2.1 %collective-permute-start.16 = (f32[128,128]{1,0:T(8,128)S(1)}, f32[128,128]{1,0:T(8,128)S(1)}, u32[]{:S(2)}, u32[]{:S(2)}) collective-permute-start(f32[128,128]{1,0:T(8,128)S(1)} %slice_bitcast_fusion.3), channel_id=1, source_target_pairs={{0,4},{1,5},{2,6},{3,7},{4,0},{5,1},{6,2},{7,3},{16,20},{17,21},{1... | collective-permute-start | bytes 196616 | tf_op jit(solution)/shard_map/ppermute | solution.py:155
  81.1 1.6 %collective-permute-done.17 = f32[2,128,128]{2,1,0:T(8,128)S(1)} collective-permute-done((f32[2,128,128]{2,1,0:T(8,128)S(1)}, f32[2,128,128]{2,1,0:T(8,128)S(1)}, u32[]{:S(2)}, u32[]{:S(2)}) %collective-permute-start.17) | collective-permute-done | bytes 131104 | tf_op jit(solution)/shard_map/ppermute | solution.py:155
  82.7 1.1 %collective-permute-done.19 = f32[2,128,128]{2,1,0:T(8,128)S(1)} collective-permute-done((f32[2,128,128]{2,1,0:T(8,128)S(1)}, f32[2,128,128]{2,1,0:T(8,128)S(1)}, u32[]{:S(2)}, u32[]{:S(2)}) %collective-permute-start.19) | collective-permute-done | bytes 131104 | tf_op jit(solution)/shard_map/ppermute | solution.py:155
  83.8 4.9 %collective-permute-done.18 = f32[2,128,128]{2,1,0:T(8,128)S(1)} collective-permute-done((f32[2,128,128]{2,1,0:T(8,128)S(1)}, f32[2,128,128]{2,1,0:T(8,128)S(1)}, u32[]{:S(2)}, u32[]{:S(2)}) %collective-permute-start.18) | collective-permute-done | bytes 131104 | tf_op jit(solution)/shard_map/ppermute | solution.py:155
  88.7 0.1 collective-permute-start.20
  88.8 2.2 %collective-permute-done.16 = f32[128,128]{1,0:T(8,128)S(1)} collective-permute-done((f32[128,128]{1,0:T(8,128)S(1)}, f32[128,128]{1,0:T(8,128)S(1)}, u32[]{:S(2)}, u32[]{:S(2)}) %collective-permute-start.16) | collective-permute-done | bytes 65568 | tf_op jit(solution)/shard_map/ppermute | solution.py:155
  91.1 0.0 collective-permute-done.20
  91.1 0.7 fusion.3
  91.7 4.5 %all-to-all-done.1 = f32[16,256,128]{2,1,0:T(8,128)S(1)} async-done(((f32[16,256,128]{2,1,0:T(8,128)}), f32[16,256,128]{2,1,0:T(8,128)S(1)}, u32[]{:S(2)}, u32[]{:S(2)}) %all-to-all-start.1) | async-done | bytes 2097184 | tf_op jit(solution)/shard_map/all_to_all | solution.py:179
  96.2 0.7 slice_reduce_fusion
  (34 shorter events, 0.1 us)
Async XLA Ops:
  3.1 7.6 %copy-start = (f32[264,128]{1,0:T(8,128)S(1)}, f32[264,128]{1,0:T(8,128)}, u32[]{:S(2)}) copy-start(f32[264,128]{1,0:T(8,128)} %get-tuple-element.10.refs_0_) | copy-start | bytes 405508
  3.1 37.7 %all-to-all-start = ((f32[16,256,128]{2,1,0:T(8,128)}), f32[16,256,128]{2,1,0:T(8,128)S(1)}, u32[]{:S(2)}, u32[]{:S(2)}) async-start(f32[16,256,128]{2,1,0:T(8,128)} %get-tuple-element.11), calls=%async_computation | async-start | bytes 4194304 | tf_op jit(solution)/shard_map/all_to_all | solution.py:166
  10.8 8.3 %collective-permute-start.5 = (f32[264,128]{1,0:T(8,128)S(1)}, f32[264,128]{1,0:T(8,128)S(1)}, u32[]{:S(2)}, u32[]{:S(2)}) collective-permute-start(f32[264,128]{1,0:T(8,128)S(1)} %copy-done), channel_id=1, source_target_pairs={{16,1},{17,2},{18,3},{19,4},{20,5},{21,6},{22,7},{23,0},{0,23},{1,... | collective-permute-start | bytes 405512 | tf_op jit(solution)/shard_map/ppermute | solution.py:161
  15.6 6.2 %collective-permute-start = (f32[264,128]{1,0:T(8,128)S(1)}, f32[264,128]{1,0:T(8,128)S(1)}, u32[]{:S(2)}, u32[]{:S(2)}) collective-permute-start(f32[264,128]{1,0:T(8,128)S(1)} %copy-done), channel_id=1, source_target_pairs={{0,1},{1,2},{2,3},{3,4},{4,5},{5,6},{6,7},{7,0},{16,23},{17,16},{1... | collective-permute-start | bytes 405512 | tf_op jit(solution)/shard_map/ppermute | solution.py:155
  19.1 12.5 %copy-start.1 = (f32[264,128]{1,0:T(8,128)}, f32[264,128]{1,0:T(8,128)S(1)}, u32[]{:S(2)}) copy-start(f32[264,128]{1,0:T(8,128)S(1)} %collective-permute-done.5.refs_6_) | copy-start | bytes 405508
  19.1 6.2 %collective-permute-start.6 = (f32[264,128]{1,0:T(8,128)S(1)}, f32[264,128]{1,0:T(8,128)S(1)}, u32[]{:S(2)}, u32[]{:S(2)}) collective-permute-start(f32[264,128]{1,0:T(8,128)S(1)} %collective-permute-done.5.refs_6_), channel_id=1, source_target_pairs={{0,1},{1,2},{2,3},{3,4},{4,5},{5,6},{6,7},{7,0},{16,23},{17,16},{1... | collective-permute-start | bytes 405512 | tf_op jit(solution)/shard_map/ppermute | solution.py:155
  21.8 19.0 %copy-start.2 = (f32[264,128]{1,0:T(8,128)}, f32[264,128]{1,0:T(8,128)S(1)}, u32[]{:S(2)}) copy-start(f32[264,128]{1,0:T(8,128)S(1)} %collective-permute-done.refs_7_) | copy-start | bytes 405508
  21.8 6.2 %collective-permute-start.1 = (f32[264,128]{1,0:T(8,128)S(1)}, f32[264,128]{1,0:T(8,128)S(1)}, u32[]{:S(2)}, u32[]{:S(2)}) collective-permute-start(f32[264,128]{1,0:T(8,128)S(1)} %collective-permute-done.refs_7_), channel_id=1, source_target_pairs={{0,1},{1,2},{2,3},{3,4},{4,5},{5,6},{6,7},{7,0},{16,23},{17,16},{1... | collective-permute-start | bytes 405512 | tf_op jit(solution)/shard_map/ppermute | solution.py:155
  21.8 6.2 %collective-permute-start.4 = (f32[264,128]{1,0:T(8,128)S(1)}, f32[264,128]{1,0:T(8,128)S(1)}, u32[]{:S(2)}, u32[]{:S(2)}) collective-permute-start(f32[264,128]{1,0:T(8,128)S(1)} %copy-done), channel_id=1, source_target_pairs={{0,16},{16,0},{1,17},{17,1},{2,18},{18,2},{3,19},{19,3},{4,20},{20... | collective-permute-start | bytes 405512 | tf_op jit(solution)/shard_map/ppermute | solution.py:149
  22.7 6.7 %collective-permute-start.9 = (f32[264,128]{1,0:T(8,128)S(1)}, f32[264,128]{1,0:T(8,128)S(1)}, u32[]{:S(2)}, u32[]{:S(2)}) collective-permute-start(f32[264,128]{1,0:T(8,128)S(1)} %collective-permute-done.5.refs_6_), channel_id=1, source_target_pairs={{0,16},{16,0},{1,17},{17,1},{2,18},{18,2},{3,19},{19,3},{4,20},{20... | collective-permute-start | bytes 405512 | tf_op jit(solution)/shard_map/ppermute | solution.py:149
  25.3 15.5 %copy-start.3 = (f32[264,128]{1,0:T(8,128)}, f32[264,128]{1,0:T(8,128)S(1)}, u32[]{:S(2)}) copy-start(f32[264,128]{1,0:T(8,128)S(1)} %collective-permute-done.6.refs_10_) | copy-start | bytes 405508
  25.3 6.2 %collective-permute-start.7 = (f32[264,128]{1,0:T(8,128)S(1)}, f32[264,128]{1,0:T(8,128)S(1)}, u32[]{:S(2)}, u32[]{:S(2)}) collective-permute-start(f32[264,128]{1,0:T(8,128)S(1)} %collective-permute-done.6.refs_10_), channel_id=1, source_target_pairs={{0,1},{1,2},{2,3},{3,4},{4,5},{5,6},{6,7},{7,0},{16,23},{17,16},{1... | collective-permute-start | bytes 405512 | tf_op jit(solution)/shard_map/ppermute | solution.py:155
  25.3 6.2 %collective-permute-start.10 = (f32[264,128]{1,0:T(8,128)S(1)}, f32[264,128]{1,0:T(8,128)S(1)}, u32[]{:S(2)}, u32[]{:S(2)}) collective-permute-start(f32[264,128]{1,0:T(8,128)S(1)} %collective-permute-done.refs_7_), channel_id=1, source_target_pairs={{0,16},{16,0},{1,17},{17,1},{2,18},{18,2},{3,19},{19,3},{4,20},{20... | collective-permute-start | bytes 405512 | tf_op jit(solution)/shard_map/ppermute | solution.py:149
  28.0 12.7 %copy-start.4 = (f32[264,128]{1,0:T(8,128)}, f32[264,128]{1,0:T(8,128)S(1)}, u32[]{:S(2)}) copy-start(f32[264,128]{1,0:T(8,128)S(1)} %collective-permute-done.1.refs_11_) | copy-start | bytes 405508
  28.0 6.2 %collective-permute-start.2 = (f32[264,128]{1,0:T(8,128)S(1)}, f32[264,128]{1,0:T(8,128)S(1)}, u32[]{:S(2)}, u32[]{:S(2)}) collective-permute-start(f32[264,128]{1,0:T(8,128)S(1)} %collective-permute-done.1.refs_11_), channel_id=1, source_target_pairs={{0,1},{1,2},{2,3},{3,4},{4,5},{5,6},{6,7},{7,0},{16,23},{17,16},{1... | collective-permute-start | bytes 405512 | tf_op jit(solution)/shard_map/ppermute | solution.py:155
  28.0 12.7 %copy-start.5 = (f32[264,128]{1,0:T(8,128)}, f32[264,128]{1,0:T(8,128)S(1)}, u32[]{:S(2)}) copy-start(f32[264,128]{1,0:T(8,128)S(1)} %collective-permute-done.4.refs_2_) | copy-start | bytes 405508
  28.1 6.2 %collective-permute-start.11 = (f32[264,128]{1,0:T(8,128)S(1)}, f32[264,128]{1,0:T(8,128)S(1)}, u32[]{:S(2)}, u32[]{:S(2)}) collective-permute-start(f32[264,128]{1,0:T(8,128)S(1)} %collective-permute-done.6.refs_10_), channel_id=1, source_target_pairs={{0,16},{16,0},{1,17},{17,1},{2,18},{18,2},{3,19},{19,3},{4,20},{20... | collective-permute-start | bytes 405512 | tf_op jit(solution)/shard_map/ppermute | solution.py:149
  29.4 11.3 %copy-start.6 = (f32[264,128]{1,0:T(8,128)}, f32[264,128]{1,0:T(8,128)S(1)}, u32[]{:S(2)}) copy-start(f32[264,128]{1,0:T(8,128)S(1)} %collective-permute-done.9.refs_4_) | copy-start | bytes 405508
  29.4 5.1 %collective-permute-start.12 = (f32[264,128]{1,0:T(8,128)S(1)}, f32[264,128]{1,0:T(8,128)S(1)}, u32[]{:S(2)}, u32[]{:S(2)}) collective-permute-start(f32[264,128]{1,0:T(8,128)S(1)} %collective-permute-done.1.refs_11_), channel_id=1, source_target_pairs={{0,16},{16,0},{1,17},{17,1},{2,18},{18,2},{3,19},{19,3},{4,20},{20... | collective-permute-start | bytes 405512 | tf_op jit(solution)/shard_map/ppermute | solution.py:149
  31.5 9.3 %copy-start.7 = (f32[264,128]{1,0:T(8,128)}, f32[264,128]{1,0:T(8,128)S(1)}, u32[]{:S(2)}) copy-start(f32[264,128]{1,0:T(8,128)S(1)} %collective-permute-done.7.refs_14_) | copy-start | bytes 405508
  31.5 3.0 %collective-permute-start.13 = (f32[264,128]{1,0:T(8,128)S(1)}, f32[264,128]{1,0:T(8,128)S(1)}, u32[]{:S(2)}, u32[]{:S(2)}) collective-permute-start(f32[264,128]{1,0:T(8,128)S(1)} %collective-permute-done.7.refs_14_), channel_id=1, source_target_pairs={{0,16},{16,0},{1,17},{17,1},{2,18},{18,2},{3,19},{19,3},{4,20},{20... | collective-permute-start | bytes 405512 | tf_op jit(solution)/shard_map/ppermute | solution.py:149
  31.6 9.3 %copy-start.8 = (f32[264,128]{1,0:T(8,128)}, f32[264,128]{1,0:T(8,128)S(1)}, u32[]{:S(2)}) copy-start(f32[264,128]{1,0:T(8,128)S(1)} %collective-permute-done.10.refs_5_) | copy-start | bytes 405508
  31.6 6.3 %collective-permute-start.8 = (f32[264,128]{1,0:T(8,128)S(1)}, f32[264,128]{1,0:T(8,128)S(1)}, u32[]{:S(2)}, u32[]{:S(2)}) collective-permute-start(f32[264,128]{1,0:T(8,128)S(1)} %collective-permute-done.7.refs_14_), channel_id=1, source_target_pairs={{0,1},{1,2},{2,3},{3,4},{4,5},{5,6},{6,7},{7,0},{16,23},{17,16},{1... | collective-permute-start | bytes 405512 | tf_op jit(solution)/shard_map/ppermute | solution.py:155
  34.3 3.6 %copy-start.9 = (f32[264,128]{1,0:T(8,128)}, f32[264,128]{1,0:T(8,128)S(1)}, u32[]{:S(2)}) copy-start(f32[264,128]{1,0:T(8,128)S(1)} %collective-permute-done.2.refs_15_) | copy-start | bytes 405508
  34.3 3.6 %collective-permute-start.14 = (f32[264,128]{1,0:T(8,128)S(1)}, f32[264,128]{1,0:T(8,128)S(1)}, u32[]{:S(2)}, u32[]{:S(2)}) collective-permute-start(f32[264,128]{1,0:T(8,128)S(1)} %collective-permute-done.2.refs_15_), channel_id=1, source_target_pairs={{0,16},{16,0},{1,17},{17,1},{2,18},{18,2},{3,19},{19,3},{4,20},{20... | collective-permute-start | bytes 405512 | tf_op jit(solution)/shard_map/ppermute | solution.py:149
  34.3 6.6 %copy-start.10 = (f32[264,128]{1,0:T(8,128)}, f32[264,128]{1,0:T(8,128)S(1)}, u32[]{:S(2)}) copy-start(f32[264,128]{1,0:T(8,128)S(1)} %collective-permute-done.11.refs_8_) | copy-start | bytes 405508
  34.3 6.5 %collective-permute-start.3 = (f32[264,128]{1,0:T(8,128)S(1)}, f32[264,128]{1,0:T(8,128)S(1)}, u32[]{:S(2)}, u32[]{:S(2)}) collective-permute-start(f32[264,128]{1,0:T(8,128)S(1)} %collective-permute-done.2.refs_15_), channel_id=1, source_target_pairs={{0,1},{1,2},{2,3},{3,4},{4,5},{5,6},{6,7},{7,0},{16,23},{17,16},{1... | collective-permute-start | bytes 405512 | tf_op jit(solution)/shard_map/ppermute | solution.py:155
  34.6 3.3 %copy-start.11 = (f32[264,128]{1,0:T(8,128)}, f32[264,128]{1,0:T(8,128)S(1)}, u32[]{:S(2)}) copy-start(f32[264,128]{1,0:T(8,128)S(1)} %collective-permute-done.12.refs_9_) | copy-start | bytes 405508
  34.6 3.3 %copy-start.12 = (f32[264,128]{1,0:T(8,128)}, f32[264,128]{1,0:T(8,128)S(1)}, u32[]{:S(2)}) copy-start(f32[264,128]{1,0:T(8,128)S(1)} %collective-permute-done.13.refs_12_) | copy-start | bytes 405508
  37.9 0.6 copy-start.13
  64.8 31.4 %all-to-all-start.1 = ((f32[16,256,128]{2,1,0:T(8,128)}), f32[16,256,128]{2,1,0:T(8,128)S(1)}, u32[]{:S(2)}, u32[]{:S(2)}) async-start(f32[16,256,128]{2,1,0:T(8,128)} %get-tuple-element.14), calls=%async_computation.1 | async-start | bytes 4194304 | tf_op jit(solution)/shard_map/all_to_all | solution.py:179
  72.0 1.9 %collective-permute-start.15 = (f32[4,2,128,128]{3,2,1,0:T(8,128)S(1)}, f32[4,2,128,128]{3,2,1,0:T(8,128)S(1)}, u32[]{:S(2)}, u32[]{:S(2)}) collective-permute-start(f32[4,2,128,128]{3,2,1,0:T(8,128)S(1)} %get-tuple-element.13), channel_id=1, source_target_pairs={{0,16},{16,0},{1,17},{17,1},{2,18},{18,2},{3,19},{19,3},{4,20},{20... | collective-permute-start | bytes 1572872 | tf_op jit(solution)/shard_map/ppermute | solution.py:149
  74.0 8.7 %collective-permute-start.17 = (f32[2,128,128]{2,1,0:T(8,128)S(1)}, f32[2,128,128]{2,1,0:T(8,128)S(1)}, u32[]{:S(2)}, u32[]{:S(2)}) collective-permute-start(f32[2,128,128]{2,1,0:T(8,128)S(1)} %get-tuple-element.19), channel_id=1, source_target_pairs={{0,1},{1,2},{2,3},{3,4},{4,5},{5,6},{6,7},{7,0},{16,23},{17,16},{1... | collective-permute-start | bytes 393224 | tf_op jit(solution)/shard_map/ppermute | solution.py:155
  74.3 9.4 %collective-permute-start.19 = (f32[2,128,128]{2,1,0:T(8,128)S(1)}, f32[2,128,128]{2,1,0:T(8,128)S(1)}, u32[]{:S(2)}, u32[]{:S(2)}) collective-permute-start(f32[2,128,128]{2,1,0:T(8,128)S(1)} %get-tuple-element.20), channel_id=1, source_target_pairs={{0,3},{1,4},{2,5},{3,6},{4,7},{5,0},{6,1},{7,2},{16,21},{17,22},{1... | collective-permute-start | bytes 393224 | tf_op jit(solution)/shard_map/ppermute | solution.py:155
  79.1 9.7 %collective-permute-start.18 = (f32[2,128,128]{2,1,0:T(8,128)S(1)}, f32[2,128,128]{2,1,0:T(8,128)S(1)}, u32[]{:S(2)}, u32[]{:S(2)}) collective-permute-start(f32[2,128,128]{2,1,0:T(8,128)S(1)} %get-tuple-element.21), channel_id=1, source_target_pairs={{0,2},{1,3},{2,4},{3,5},{4,6},{5,7},{6,0},{7,1},{16,22},{17,23},{1... | collective-permute-start | bytes 393224 | tf_op jit(solution)/shard_map/ppermute | solution.py:155
  79.1 12.0 %collective-permute-start.16 = (f32[128,128]{1,0:T(8,128)S(1)}, f32[128,128]{1,0:T(8,128)S(1)}, u32[]{:S(2)}, u32[]{:S(2)}) collective-permute-start(f32[128,128]{1,0:T(8,128)S(1)} %slice_bitcast_fusion.3), channel_id=1, source_target_pairs={{0,4},{1,5},{2,6},{3,7},{4,0},{5,1},{6,2},{7,3},{16,20},{17,21},{1... | collective-permute-start | bytes 196616 | tf_op jit(solution)/shard_map/ppermute | solution.py:155
  88.7 2.4 %collective-permute-start.20 = (f32[128,128]{1,0:T(8,128)S(1)}, f32[128,128]{1,0:T(8,128)S(1)}, u32[]{:S(2)}, u32[]{:S(2)}) collective-permute-start(f32[128,128]{1,0:T(8,128)S(1)} %fusion), channel_id=1, source_target_pairs={{0,16},{16,0},{1,17},{17,1},{2,18},{18,2},{3,19},{19,3},{4,20},{20... | collective-permute-start | bytes 196616 | tf_op jit(solution)/shard_map/ppermute | solution.py:149

commit v6 on v5

--- a/solution.py
+++ b/solution.py
@@ -24,7 +24,7 @@
 PACK = 2 * ROWS + 8
 CHUNKS = 4
 TQ = TOKENS // CHUNKS
-TK = TOKENS // 2
+TK = TOKENS
 
 SWAP = [(0, 1), (1, 0)]
 
@@ -140,7 +140,7 @@
         scratch_shapes=[pltpu.VMEM((2 * D, TOKENS), BF16)] * 2
         + [pltpu.VMEM((TOKENS, 4 * D), BF16)] * 2
         + [pltpu.VMEM((TOKENS, D), F32)],
-        compiler_params=pltpu.CompilerParams(vmem_limit_bytes=36 * 1024 * 1024),
+        compiler_params=pltpu.CompilerParams(vmem_limit_bytes=48 * 1024 * 1024),
         cost_estimate=pl.CostEstimate(flops=24_000_000_000, bytes_accessed=8 << 20, transcendentals=TOKENS * TOKENS),
     )(*packs, kv)
 

time: 98.8 us -> 98.2 us (level)
  no operation moved by 1% of the time
where the time goes in v6:
time: 98.2 us; the launch traced here: 96.4 us
  waiting for transfers between devices  35.3 us (36%)
  starting transfers between devices  32.1 us (33%)
  Pallas kernels  25.9 us (26%)
  other arithmetic  1.47 us (1%)
    ppermute x11, waiting for transfers between devices, along(): return lax.ppermute(x, COLUMN, pairs)  25.2 us
    pallas_call x1, Pallas kernels, tile_grads(): pl.pallas_call(tile_kernel, grid=(TOKENS // TK,), in_specs=[pl.BlockSpec(...  23.4 us
    all_to_all x1, starting transfers between devices, on_device(): kv = lax.all_to_all(kv, PLANE, 0, 0)  7.61 us
    all_to_all x1, starting transfers between devices, on_device(): dkv = lax.all_to_all(dkv, PLANE, 0, 0)  7.22 us
    ppermute x11, starting transfers between devices, along(): return lax.ppermute(x, COLUMN, pairs)  7.21 us
    ppermute x9, starting transfers between devices, swap(): return lax.ppermute(x, 'c', SWAP)  5.25 us
    ppermute x1, starting transfers between devices, across(): return lax.ppermute(x, COLUMN, pairs)  4.82 us
    all_to_all x1, waiting for transfers between devices, on_device(): dkv = lax.all_to_all(dkv, PLANE, 0, 0)  4.7 us
  transfers between devices with their start and end apart: 23, of which 14 were waited for; matrix products, arithmetic and copies ran while one was open for 1% of the time, Pallas kernels for 0%

profile of v6, /device:TPU:2, one launch (start us, length us, event | category | flops | bytes accessed | tf_op | source)
XLA Modules:
  0.0 96.4 jit_solution(37462550907374442)
XLA Ops:
  0.6 2.5 %shard_map.85 = (f32[264,128]{1,0:T(8,128)}, f32[16,256,128]{2,1,0:T(8,128)}) custom-call(f32[128,128]{1,0:T(8,128)} %k.1, f32[128,128]{1,0:T(8,128)} %v.1, f32[128,128]{1,0:T(8,128)} %q.1, f32[128,128]{1,0:T(8,128)} %o.1, f32[128,128]{1,0:T(8,128)} %g.1, f32[1,128]{1,0:T(1,128)} %lse.1), custom_call_target="tpu_custom_call" | custom-call | tf_op jit(solution)/shard_map/pallas_call | solution.py:63
  3.1 7.6 %all-to-all-start = ((f32[16,256,128]{2,1,0:T(8,128)}), f32[16,256,128]{2,1,0:T(8,128)S(1)}, u32[]{:S(2)}, u32[]{:S(2)}) async-start(f32[16,256,128]{2,1,0:T(8,128)} %get-tuple-element.11), calls=%async_computation | async-start | bytes 4194304 | tf_op jit(solution)/shard_map/all_to_all | solution.py:166
  10.8 4.8 %collective-permute-start.5 = (f32[264,128]{1,0:T(8,128)S(1)}, f32[264,128]{1,0:T(8,128)S(1)}, u32[]{:S(2)}, u32[]{:S(2)}) collective-permute-start(f32[264,128]{1,0:T(8,128)S(1)} %copy-done), channel_id=1, source_target_pairs={{16,1},{17,2},{18,3},{19,4},{20,5},{21,6},{22,7},{23,0},{0,23},{1,... | collective-permute-start | bytes 405512 | tf_op jit(solution)/shard_map/ppermute | solution.py:161
  15.6 0.0 collective-permute-start
  15.6 3.5 %collective-permute-done.5.refs_6_ = f32[264,128]{1,0:T(8,128)S(1)} collective-permute-done((f32[264,128]{1,0:T(8,128)S(1)}, f32[264,128]{1,0:T(8,128)S(1)}, u32[]{:S(2)}, u32[]{:S(2)}) %collective-permute-start.5) | collective-permute-done | bytes 135200 | tf_op jit(solution)/shard_map/ppermute | solution.py:161
  19.1 0.0 collective-permute-start.6
  19.1 2.7 %collective-permute-done.refs_7_ = f32[264,128]{1,0:T(8,128)S(1)} collective-permute-done((f32[264,128]{1,0:T(8,128)S(1)}, f32[264,128]{1,0:T(8,128)S(1)}, u32[]{:S(2)}, u32[]{:S(2)}) %collective-permute-start) | collective-permute-done | bytes 135200 | tf_op jit(solution)/shard_map/ppermute | solution.py:155
  21.8 0.9 collective-permute-start.4
  22.7 0.1 collective-permute-start.9
  22.8 2.5 %collective-permute-done.6.refs_10_ = f32[264,128]{1,0:T(8,128)S(1)} collective-permute-done((f32[264,128]{1,0:T(8,128)S(1)}, f32[264,128]{1,0:T(8,128)S(1)}, u32[]{:S(2)}, u32[]{:S(2)}) %collective-permute-start.6) | collective-permute-done | bytes 135200 | tf_op jit(solution)/shard_map/ppermute | solution.py:155
  25.3 0.0 collective-permute-start.7
  25.3 2.7 %collective-permute-start.10 = (f32[264,128]{1,0:T(8,128)S(1)}, f32[264,128]{1,0:T(8,128)S(1)}, u32[]{:S(2)}, u32[]{:S(2)}) collective-permute-start(f32[264,128]{1,0:T(8,128)S(1)} %collective-permute-done.refs_7_), channel_id=1, source_target_pairs={{0,16},{16,0},{1,17},{17,1},{2,18},{18,2},{3,19},{19,3},{4,20},{20... | collective-permute-start | bytes 405512 | tf_op jit(solution)/shard_map/ppermute | solution.py:149
  28.0 0.1 collective-permute-done.1.refs_11_
  28.0 0.0 collective-permute-done.4.refs_2_
  28.1 1.4 %collective-permute-start.11 = (f32[264,128]{1,0:T(8,128)S(1)}, f32[264,128]{1,0:T(8,128)S(1)}, u32[]{:S(2)}, u32[]{:S(2)}) collective-permute-start(f32[264,128]{1,0:T(8,128)S(1)} %collective-permute-done.6.refs_10_), channel_id=1, source_target_pairs={{0,16},{16,0},{1,17},{17,1},{2,18},{18,2},{3,19},{19,3},{4,20},{20... | collective-permute-start | bytes 405512 | tf_op jit(solution)/shard_map/ppermute | solution.py:149
  29.4 0.1 collective-permute-start.12
  29.5 2.0 %collective-permute-done.7.refs_14_ = f32[264,128]{1,0:T(8,128)S(1)} collective-permute-done((f32[264,128]{1,0:T(8,128)S(1)}, f32[264,128]{1,0:T(8,128)S(1)}, u32[]{:S(2)}, u32[]{:S(2)}) %collective-permute-start.7) | collective-permute-done | bytes 135200 | tf_op jit(solution)/shard_map/ppermute | solution.py:155
  31.5 0.0 collective-permute-start.13
  31.5 0.0 collective-permute-done.10.refs_5_
  31.6 0.1 collective-permute-start.8
  31.7 2.6 %collective-permute-done.2.refs_15_ = f32[264,128]{1,0:T(8,128)S(1)} collective-permute-done((f32[264,128]{1,0:T(8,128)S(1)}, f32[264,128]{1,0:T(8,128)S(1)}, u32[]{:S(2)}, u32[]{:S(2)}) %collective-permute-start.2) | collective-permute-done | bytes 135200 | tf_op jit(solution)/shard_map/ppermute | solution.py:155
  34.3 0.0 collective-permute-start.14
  34.3 0.0 collective-permute-done.11.refs_8_
  34.3 0.3 collective-permute-start.3
  34.6 0.0 collective-permute-done.12.refs_9_
  34.6 0.0 collective-permute-done.13.refs_12_
  34.6 3.3 %collective-permute-done.8.refs_3_ = f32[264,128]{1,0:T(8,128)S(1)} collective-permute-done((f32[264,128]{1,0:T(8,128)S(1)}, f32[264,128]{1,0:T(8,128)S(1)}, u32[]{:S(2)}, u32[]{:S(2)}) %collective-permute-start.8) | collective-permute-done | bytes 135200 | tf_op jit(solution)/shard_map/ppermute | solution.py:155
  37.9 0.0 collective-permute-done.14.refs_13_
  37.9 0.6 copy-done.13
  38.5 2.2 %collective-permute-done.3.refs_1_ = f32[264,128]{1,0:T(8,128)S(1)} collective-permute-done((f32[264,128]{1,0:T(8,128)S(1)}, f32[264,128]{1,0:T(8,128)S(1)}, u32[]{:S(2)}, u32[]{:S(2)}) %collective-permute-start.3) | collective-permute-done | bytes 135200 | tf_op jit(solution)/shard_map/ppermute | solution.py:155
  40.8 23.4 %shard_map.86 = (f32[4,2,128,128]{3,2,1,0:T(8,128)S(1)}, f32[4,2,128,128]{3,2,1,0:T(8,128)S(1)}, f32[16,256,128]{2,1,0:T(8,128)}) custom-call(f32[264,128]{1,0:T(8,128)} %get-tuple-element.10.refs_0_, f32[264,128]{1,0:T(8,128)S(1)} %collective-permute-done.3.refs_1_, f32[264,128]{1,0:T(8,128)} %copy-done.5, f32[264,128]{1,0:T(8,128)S(1)} %collective-permute-done.8.refs_3_, ...), custom_call_target="tpu_custom_call" | custom-call | flops 24000000000 | bytes 8388608 | tf_op jit(solution)/shard_map/pallas_call | solution.py:134
  64.2 7.2 %all-to-all-start.1 = ((f32[16,256,128]{2,1,0:T(8,128)}), f32[16,256,128]{2,1,0:T(8,128)S(1)}, u32[]{:S(2)}, u32[]{:S(2)}) async-start(f32[16,256,128]{2,1,0:T(8,128)} %get-tuple-element.14), calls=%async_computation.1 | async-start | bytes 4194304 | tf_op jit(solution)/shard_map/all_to_all | solution.py:179
  71.5 0.0 collective-permute-start.15
  71.5 1.9 %collective-permute-done.15 = f32[4,2,128,128]{3,2,1,0:T(8,128)S(1)} collective-permute-done((f32[4,2,128,128]{3,2,1,0:T(8,128)S(1)}, f32[4,2,128,128]{3,2,1,0:T(8,128)S(1)}, u32[]{:S(2)}, u32[]{:S(2)}) %collective-permute-start.15) | collective-permute-done | bytes 524320 | tf_op jit(solution)/shard_map/ppermute | solution.py:149
  73.4 0.1 add.32
  73.5 0.1 collective-permute-start.17
  73.6 4.7 %collective-permute-start.19 = (f32[2,128,128]{2,1,0:T(8,128)S(1)}, f32[2,128,128]{2,1,0:T(8,128)S(1)}, u32[]{:S(2)}, u32[]{:S(2)}) collective-permute-start(f32[2,128,128]{2,1,0:T(8,128)S(1)} %get-tuple-element.20), channel_id=1, source_target_pairs={{0,3},{1,4},{2,5},{3,6},{4,7},{5,0},{6,1},{7,2},{16,21},{17,22},{1... | collective-permute-start | bytes 393224 | tf_op jit(solution)/shard_map/ppermute | solution.py:155
  78.3 0.0 collective-permute-start.18
  78.3 2.1 %collective-permute-start.16 = (f32[128,128]{1,0:T(8,128)S(1)}, f32[128,128]{1,0:T(8,128)S(1)}, u32[]{:S(2)}, u32[]{:S(2)}) collective-permute-start(f32[128,128]{1,0:T(8,128)S(1)} %slice_bitcast_fusion.3), channel_id=1, source_target_pairs={{0,4},{1,5},{2,6},{3,7},{4,0},{5,1},{6,2},{7,3},{16,20},{17,21},{1... | collective-permute-start | bytes 196616 | tf_op jit(solution)/shard_map/ppermute | solution.py:155
  80.3 1.6 %collective-permute-done.17 = f32[2,128,128]{2,1,0:T(8,128)S(1)} collective-permute-done((f32[2,128,128]{2,1,0:T(8,128)S(1)}, f32[2,128,128]{2,1,0:T(8,128)S(1)}, u32[]{:S(2)}, u32[]{:S(2)}) %collective-permute-start.17) | collective-permute-done | bytes 131104 | tf_op jit(solution)/shard_map/ppermute | solution.py:155
  81.9 1.1 %collective-permute-done.19 = f32[2,128,128]{2,1,0:T(8,128)S(1)} collective-permute-done((f32[2,128,128]{2,1,0:T(8,128)S(1)}, f32[2,128,128]{2,1,0:T(8,128)S(1)}, u32[]{:S(2)}, u32[]{:S(2)}) %collective-permute-start.19) | collective-permute-done | bytes 131104 | tf_op jit(solution)/shard_map/ppermute | solution.py:155
  83.0 4.9 %collective-permute-done.18 = f32[2,128,128]{2,1,0:T(8,128)S(1)} collective-permute-done((f32[2,128,128]{2,1,0:T(8,128)S(1)}, f32[2,128,128]{2,1,0:T(8,128)S(1)}, u32[]{:S(2)}, u32[]{:S(2)}) %collective-permute-start.18) | collective-permute-done | bytes 131104 | tf_op jit(solution)/shard_map/ppermute | solution.py:155
  88.0 0.1 collective-permute-start.20
  88.1 2.2 %collective-permute-done.16 = f32[128,128]{1,0:T(8,128)S(1)} collective-permute-done((f32[128,128]{1,0:T(8,128)S(1)}, f32[128,128]{1,0:T(8,128)S(1)}, u32[]{:S(2)}, u32[]{:S(2)}) %collective-permute-start.16) | collective-permute-done | bytes 65568 | tf_op jit(solution)/shard_map/ppermute | solution.py:155
  90.3 0.0 collective-permute-done.20
  90.3 0.7 fusion.3
  91.0 4.7 %all-to-all-done.1 = f32[16,256,128]{2,1,0:T(8,128)S(1)} async-done(((f32[16,256,128]{2,1,0:T(8,128)}), f32[16,256,128]{2,1,0:T(8,128)S(1)}, u32[]{:S(2)}, u32[]{:S(2)}) %all-to-all-start.1) | async-done | bytes 2097184 | tf_op jit(solution)/shard_map/all_to_all | solution.py:179
  95.7 0.7 slice_reduce_fusion
  (34 shorter events, 0.1 us)
Async XLA Ops:
  3.1 7.6 %copy-start = (f32[264,128]{1,0:T(8,128)S(1)}, f32[264,128]{1,0:T(8,128)}, u32[]{:S(2)}) copy-start(f32[264,128]{1,0:T(8,128)} %get-tuple-element.10.refs_0_) | copy-start | bytes 405508
  3.1 37.7 %all-to-all-start = ((f32[16,256,128]{2,1,0:T(8,128)}), f32[16,256,128]{2,1,0:T(8,128)S(1)}, u32[]{:S(2)}, u32[]{:S(2)}) async-start(f32[16,256,128]{2,1,0:T(8,128)} %get-tuple-element.11), calls=%async_computation | async-start | bytes 4194304 | tf_op jit(solution)/shard_map/all_to_all | solution.py:166
  10.8 8.3 %collective-permute-start.5 = (f32[264,128]{1,0:T(8,128)S(1)}, f32[264,128]{1,0:T(8,128)S(1)}, u32[]{:S(2)}, u32[]{:S(2)}) collective-permute-start(f32[264,128]{1,0:T(8,128)S(1)} %copy-done), channel_id=1, source_target_pairs={{16,1},{17,2},{18,3},{19,4},{20,5},{21,6},{22,7},{23,0},{0,23},{1,... | collective-permute-start | bytes 405512 | tf_op jit(solution)/shard_map/ppermute | solution.py:161
  15.6 6.2 %collective-permute-start = (f32[264,128]{1,0:T(8,128)S(1)}, f32[264,128]{1,0:T(8,128)S(1)}, u32[]{:S(2)}, u32[]{:S(2)}) collective-permute-start(f32[264,128]{1,0:T(8,128)S(1)} %copy-done), channel_id=1, source_target_pairs={{0,1},{1,2},{2,3},{3,4},{4,5},{5,6},{6,7},{7,0},{16,23},{17,16},{1... | collective-permute-start | bytes 405512 | tf_op jit(solution)/shard_map/ppermute | solution.py:155
  19.1 12.5 %copy-start.1 = (f32[264,128]{1,0:T(8,128)}, f32[264,128]{1,0:T(8,128)S(1)}, u32[]{:S(2)}) copy-start(f32[264,128]{1,0:T(8,128)S(1)} %collective-permute-done.5.refs_6_) | copy-start | bytes 405508
  19.1 6.2 %collective-permute-start.6 = (f32[264,128]{1,0:T(8,128)S(1)}, f32[264,128]{1,0:T(8,128)S(1)}, u32[]{:S(2)}, u32[]{:S(2)}) collective-permute-start(f32[264,128]{1,0:T(8,128)S(1)} %collective-permute-done.5.refs_6_), channel_id=1, source_target_pairs={{0,1},{1,2},{2,3},{3,4},{4,5},{5,6},{6,7},{7,0},{16,23},{17,16},{1... | collective-permute-start | bytes 405512 | tf_op jit(solution)/shard_map/ppermute | solution.py:155
  21.8 19.0 %copy-start.2 = (f32[264,128]{1,0:T(8,128)}, f32[264,128]{1,0:T(8,128)S(1)}, u32[]{:S(2)}) copy-start(f32[264,128]{1,0:T(8,128)S(1)} %collective-permute-done.refs_7_) | copy-start | bytes 405508
  21.8 6.2 %collective-permute-start.1 = (f32[264,128]{1,0:T(8,128)S(1)}, f32[264,128]{1,0:T(8,128)S(1)}, u32[]{:S(2)}, u32[]{:S(2)}) collective-permute-start(f32[264,128]{1,0:T(8,128)S(1)} %collective-permute-done.refs_7_), channel_id=1, source_target_pairs={{0,1},{1,2},{2,3},{3,4},{4,5},{5,6},{6,7},{7,0},{16,23},{17,16},{1... | collective-permute-start | bytes 405512 | tf_op jit(solution)/shard_map/ppermute | solution.py:155
  21.8 6.2 %collective-permute-start.4 = (f32[264,128]{1,0:T(8,128)S(1)}, f32[264,128]{1,0:T(8,128)S(1)}, u32[]{:S(2)}, u32[]{:S(2)}) collective-permute-start(f32[264,128]{1,0:T(8,128)S(1)} %copy-done), channel_id=1, source_target_pairs={{0,16},{16,0},{1,17},{17,1},{2,18},{18,2},{3,19},{19,3},{4,20},{20... | collective-permute-start | bytes 405512 | tf_op jit(solution)/shard_map/ppermute | solution.py:149
  22.7 6.7 %collective-permute-start.9 = (f32[264,128]{1,0:T(8,128)S(1)}, f32[264,128]{1,0:T(8,128)S(1)}, u32[]{:S(2)}, u32[]{:S(2)}) collective-permute-start(f32[264,128]{1,0:T(8,128)S(1)} %collective-permute-done.5.refs_6_), channel_id=1, source_target_pairs={{0,16},{16,0},{1,17},{17,1},{2,18},{18,2},{3,19},{19,3},{4,20},{20... | collective-permute-start | bytes 405512 | tf_op jit(solution)/shard_map/ppermute | solution.py:149
  25.3 15.5 %copy-start.3 = (f32[264,128]{1,0:T(8,128)}, f32[264,128]{1,0:T(8,128)S(1)}, u32[]{:S(2)}) copy-start(f32[264,128]{1,0:T(8,128)S(1)} %collective-permute-done.6.refs_10_) | copy-start | bytes 405508
  25.3 6.2 %collective-permute-start.7 = (f32[264,128]{1,0:T(8,128)S(1)}, f32[264,128]{1,0:T(8,128)S(1)}, u32[]{:S(2)}, u32[]{:S(2)}) collective-permute-start(f32[264,128]{1,0:T(8,128)S(1)} %collective-permute-done.6.refs_10_), channel_id=1, source_target_pairs={{0,1},{1,2},{2,3},{3,4},{4,5},{5,6},{6,7},{7,0},{16,23},{17,16},{1... | collective-permute-start | bytes 405512 | tf_op jit(solution)/shard_map/ppermute | solution.py:155
  25.3 6.2 %collective-permute-start.10 = (f32[264,128]{1,0:T(8,128)S(1)}, f32[264,128]{1,0:T(8,128)S(1)}, u32[]{:S(2)}, u32[]{:S(2)}) collective-permute-start(f32[264,128]{1,0:T(8,128)S(1)} %collective-permute-done.refs_7_), channel_id=1, source_target_pairs={{0,16},{16,0},{1,17},{17,1},{2,18},{18,2},{3,19},{19,3},{4,20},{20... | collective-permute-start | bytes 405512 | tf_op jit(solution)/shard_map/ppermute | solution.py:149
  28.0 12.7 %copy-start.4 = (f32[264,128]{1,0:T(8,128)}, f32[264,128]{1,0:T(8,128)S(1)}, u32[]{:S(2)}) copy-start(f32[264,128]{1,0:T(8,128)S(1)} %collective-permute-done.1.refs_11_) | copy-start | bytes 405508
  28.0 6.2 %collective-permute-start.2 = (f32[264,128]{1,0:T(8,128)S(1)}, f32[264,128]{1,0:T(8,128)S(1)}, u32[]{:S(2)}, u32[]{:S(2)}) collective-permute-start(f32[264,128]{1,0:T(8,128)S(1)} %collective-permute-done.1.refs_11_), channel_id=1, source_target_pairs={{0,1},{1,2},{2,3},{3,4},{4,5},{5,6},{6,7},{7,0},{16,23},{17,16},{1... | collective-permute-start | bytes 405512 | tf_op jit(solution)/shard_map/ppermute | solution.py:155
  28.0 12.7 %copy-start.5 = (f32[264,128]{1,0:T(8,128)}, f32[264,128]{1,0:T(8,128)S(1)}, u32[]{:S(2)}) copy-start(f32[264,128]{1,0:T(8,128)S(1)} %collective-permute-done.4.refs_2_) | copy-start | bytes 405508
  28.1 6.2 %collective-permute-start.11 = (f32[264,128]{1,0:T(8,128)S(1)}, f32[264,128]{1,0:T(8,128)S(1)}, u32[]{:S(2)}, u32[]{:S(2)}) collective-permute-start(f32[264,128]{1,0:T(8,128)S(1)} %collective-permute-done.6.refs_10_), channel_id=1, source_target_pairs={{0,16},{16,0},{1,17},{17,1},{2,18},{18,2},{3,19},{19,3},{4,20},{20... | collective-permute-start | bytes 405512 | tf_op jit(solution)/shard_map/ppermute | solution.py:149
  29.4 11.3 %copy-start.6 = (f32[264,128]{1,0:T(8,128)}, f32[264,128]{1,0:T(8,128)S(1)}, u32[]{:S(2)}) copy-start(f32[264,128]{1,0:T(8,128)S(1)} %collective-permute-done.9.refs_4_) | copy-start | bytes 405508
  29.4 5.1 %collective-permute-start.12 = (f32[264,128]{1,0:T(8,128)S(1)}, f32[264,128]{1,0:T(8,128)S(1)}, u32[]{:S(2)}, u32[]{:S(2)}) collective-permute-start(f32[264,128]{1,0:T(8,128)S(1)} %collective-permute-done.1.refs_11_), channel_id=1, source_target_pairs={{0,16},{16,0},{1,17},{17,1},{2,18},{18,2},{3,19},{19,3},{4,20},{20... | collective-permute-start | bytes 405512 | tf_op jit(solution)/shard_map/ppermute | solution.py:149
  31.5 9.3 %copy-start.7 = (f32[264,128]{1,0:T(8,128)}, f32[264,128]{1,0:T(8,128)S(1)}, u32[]{:S(2)}) copy-start(f32[264,128]{1,0:T(8,128)S(1)} %collective-permute-done.7.refs_14_) | copy-start | bytes 405508
  31.5 3.0 %collective-permute-start.13 = (f32[264,128]{1,0:T(8,128)S(1)}, f32[264,128]{1,0:T(8,128)S(1)}, u32[]{:S(2)}, u32[]{:S(2)}) collective-permute-start(f32[264,128]{1,0:T(8,128)S(1)} %collective-permute-done.7.refs_14_), channel_id=1, source_target_pairs={{0,16},{16,0},{1,17},{17,1},{2,18},{18,2},{3,19},{19,3},{4,20},{20... | collective-permute-start | bytes 405512 | tf_op jit(solution)/shard_map/ppermute | solution.py:149
  31.6 9.3 %copy-start.8 = (f32[264,128]{1,0:T(8,128)}, f32[264,128]{1,0:T(8,128)S(1)}, u32[]{:S(2)}) copy-start(f32[264,128]{1,0:T(8,128)S(1)} %collective-permute-done.10.refs_5_) | copy-start | bytes 405508
  31.6 6.3 %collective-permute-start.8 = (f32[264,128]{1,0:T(8,128)S(1)}, f32[264,128]{1,0:T(8,128)S(1)}, u32[]{:S(2)}, u32[]{:S(2)}) collective-permute-start(f32[264,128]{1,0:T(8,128)S(1)} %collective-permute-done.7.refs_14_), channel_id=1, source_target_pairs={{0,1},{1,2},{2,3},{3,4},{4,5},{5,6},{6,7},{7,0},{16,23},{17,16},{1... | collective-permute-start | bytes 405512 | tf_op jit(solution)/shard_map/ppermute | solution.py:155
  34.3 3.6 %copy-start.9 = (f32[264,128]{1,0:T(8,128)}, f32[264,128]{1,0:T(8,128)S(1)}, u32[]{:S(2)}) copy-start(f32[264,128]{1,0:T(8,128)S(1)} %collective-permute-done.2.refs_15_) | copy-start | bytes 405508
  34.3 3.6 %collective-permute-start.14 = (f32[264,128]{1,0:T(8,128)S(1)}, f32[264,128]{1,0:T(8,128)S(1)}, u32[]{:S(2)}, u32[]{:S(2)}) collective-permute-start(f32[264,128]{1,0:T(8,128)S(1)} %collective-permute-done.2.refs_15_), channel_id=1, source_target_pairs={{0,16},{16,0},{1,17},{17,1},{2,18},{18,2},{3,19},{19,3},{4,20},{20... | collective-permute-start | bytes 405512 | tf_op jit(solution)/shard_map/ppermute | solution.py:149
  34.3 6.6 %copy-start.10 = (f32[264,128]{1,0:T(8,128)}, f32[264,128]{1,0:T(8,128)S(1)}, u32[]{:S(2)}) copy-start(f32[264,128]{1,0:T(8,128)S(1)} %collective-permute-done.11.refs_8_) | copy-start | bytes 405508
  34.3 6.5 %collective-permute-start.3 = (f32[264,128]{1,0:T(8,128)S(1)}, f32[264,128]{1,0:T(8,128)S(1)}, u32[]{:S(2)}, u32[]{:S(2)}) collective-permute-start(f32[264,128]{1,0:T(8,128)S(1)} %collective-permute-done.2.refs_15_), channel_id=1, source_target_pairs={{0,1},{1,2},{2,3},{3,4},{4,5},{5,6},{6,7},{7,0},{16,23},{17,16},{1... | collective-permute-start | bytes 405512 | tf_op jit(solution)/shard_map/ppermute | solution.py:155
  34.6 3.3 %copy-start.11 = (f32[264,128]{1,0:T(8,128)}, f32[264,128]{1,0:T(8,128)S(1)}, u32[]{:S(2)}) copy-start(f32[264,128]{1,0:T(8,128)S(1)} %collective-permute-done.12.refs_9_) | copy-start | bytes 405508
  34.6 3.3 %copy-start.12 = (f32[264,128]{1,0:T(8,128)}, f32[264,128]{1,0:T(8,128)S(1)}, u32[]{:S(2)}) copy-start(f32[264,128]{1,0:T(8,128)S(1)} %collective-permute-done.13.refs_12_) | copy-start | bytes 405508
  37.9 0.6 copy-start.13
  64.2 31.4 %all-to-all-start.1 = ((f32[16,256,128]{2,1,0:T(8,128)}), f32[16,256,128]{2,1,0:T(8,128)S(1)}, u32[]{:S(2)}, u32[]{:S(2)}) async-start(f32[16,256,128]{2,1,0:T(8,128)} %get-tuple-element.14), calls=%async_computation.1 | async-start | bytes 4194304 | tf_op jit(solution)/shard_map/all_to_all | solution.py:179
  71.5 1.9 %collective-permute-start.15 = (f32[4,2,128,128]{3,2,1,0:T(8,128)S(1)}, f32[4,2,128,128]{3,2,1,0:T(8,128)S(1)}, u32[]{:S(2)}, u32[]{:S(2)}) collective-permute-start(f32[4,2,128,128]{3,2,1,0:T(8,128)S(1)} %get-tuple-element.13), channel_id=1, source_target_pairs={{0,16},{16,0},{1,17},{17,1},{2,18},{18,2},{3,19},{19,3},{4,20},{20... | collective-permute-start | bytes 1572872 | tf_op jit(solution)/shard_map/ppermute | solution.py:149
  73.5 8.4 %collective-permute-start.17 = (f32[2,128,128]{2,1,0:T(8,128)S(1)}, f32[2,128,128]{2,1,0:T(8,128)S(1)}, u32[]{:S(2)}, u32[]{:S(2)}) collective-permute-start(f32[2,128,128]{2,1,0:T(8,128)S(1)} %get-tuple-element.19), channel_id=1, source_target_pairs={{0,1},{1,2},{2,3},{3,4},{4,5},{5,6},{6,7},{7,0},{16,23},{17,16},{1... | collective-permute-start | bytes 393224 | tf_op jit(solution)/shard_map/ppermute | solution.py:155
  73.6 9.5 %collective-permute-start.19 = (f32[2,128,128]{2,1,0:T(8,128)S(1)}, f32[2,128,128]{2,1,0:T(8,128)S(1)}, u32[]{:S(2)}, u32[]{:S(2)}) collective-permute-start(f32[2,128,128]{2,1,0:T(8,128)S(1)} %get-tuple-element.20), channel_id=1, source_target_pairs={{0,3},{1,4},{2,5},{3,6},{4,7},{5,0},{6,1},{7,2},{16,21},{17,22},{1... | collective-permute-start | bytes 393224 | tf_op jit(solution)/shard_map/ppermute | solution.py:155
  78.3 9.7 %collective-permute-start.18 = (f32[2,128,128]{2,1,0:T(8,128)S(1)}, f32[2,128,128]{2,1,0:T(8,128)S(1)}, u32[]{:S(2)}, u32[]{:S(2)}) collective-permute-start(f32[2,128,128]{2,1,0:T(8,128)S(1)} %get-tuple-element.21), channel_id=1, source_target_pairs={{0,2},{1,3},{2,4},{3,5},{4,6},{5,7},{6,0},{7,1},{16,22},{17,23},{1... | collective-permute-start | bytes 393224 | tf_op jit(solution)/shard_map/ppermute | solution.py:155
  78.3 12.0 %collective-permute-start.16 = (f32[128,128]{1,0:T(8,128)S(1)}, f32[128,128]{1,0:T(8,128)S(1)}, u32[]{:S(2)}, u32[]{:S(2)}) collective-permute-start(f32[128,128]{1,0:T(8,128)S(1)} %slice_bitcast_fusion.3), channel_id=1, source_target_pairs={{0,4},{1,5},{2,6},{3,7},{4,0},{5,1},{6,2},{7,3},{16,20},{17,21},{1... | collective-permute-start | bytes 196616 | tf_op jit(solution)/shard_map/ppermute | solution.py:155
  88.0 2.3 %collective-permute-start.20 = (f32[128,128]{1,0:T(8,128)S(1)}, f32[128,128]{1,0:T(8,128)S(1)}, u32[]{:S(2)}, u32[]{:S(2)}) collective-permute-start(f32[128,128]{1,0:T(8,128)S(1)} %fusion), channel_id=1, source_target_pairs={{0,16},{16,0},{1,17},{17,1},{2,18},{18,2},{3,19},{19,3},{4,20},{20... | collective-permute-start | bytes 196616 | tf_op jit(solution)/shard_map/ppermute | solution.py:149

commit v7 on v6

--- a/solution.py
+++ b/solution.py
@@ -81,18 +81,19 @@
 
 
 def tile_kernel(*refs):
-    packs, kv_ref, mine, theirs, dkv_ref = refs[:BLOCKS], *refs[BLOCKS : BLOCKS + 4]
-    q_turned, g_turned, q_all, g_all, dq = refs[BLOCKS + 4 :]
-    step = pl.program_id(0)
-
-    @pl.when(step == 0)
-    def _():
-        for b in range(BLOCKS):
-            at = slice(b * ROWS, (b + 1) * ROWS)
-            load_block(packs[b], 0, SCALE * LOG2E, 2 * ROWS, LOG2E, at, q_turned, q_all)
-            load_block(packs[b], ROWS, 1.0, 2 * ROWS + 1, 1.0, at, g_turned, g_all)
-        dq[...] = jnp.zeros_like(dq)
-
+    packs, kv_any, mine, theirs, dkv_any = refs[:BLOCKS], *refs[BLOCKS : BLOCKS + 4]
+    q_turned, g_turned, q_all, g_all, kv_ref, dk_ref, dv_ref, sems = refs[BLOCKS + 4 :]
+    fetch = pltpu.make_async_copy(kv_any, kv_ref, sems.at[0])
+    dk_out = pltpu.make_async_copy(dk_ref, dkv_any.at[:, :ROWS, :], sems.at[1])
+    dv_out = pltpu.make_async_copy(dv_ref, dkv_any.at[:, ROWS:, :], sems.at[2])
+    fetch.start()
+
+    for b in range(BLOCKS):
+        at = slice(b * ROWS, (b + 1) * ROWS)
+        load_block(packs[b], 0, SCALE * LOG2E, 2 * ROWS, LOG2E, at, q_turned, q_all)
+        load_block(packs[b], ROWS, 1.0, 2 * ROWS + 1, 1.0, at, g_turned, g_all)
+
+    fetch.wait()
     ones = (lax.broadcasted_iota(jnp.int32, (D, TK), 0) < 3).astype(F32).astype(BF16)
     k = kv_ref[:, :ROWS, :].reshape(TK, D)
     v = kv_ref[:, ROWS:, :].reshape(TK, D)
@@ -110,27 +111,26 @@
         high, low = split(probs)
         part = dot(g_turned[:, at], high)
         dvt += part[:D] + part[D:] + dot(g_turned[:D, at], low)
+        if j == TOKENS // TQ - 1:
+            dv_ref[...] = dvt.T.reshape(BLOCKS, ROWS, D)
+            dv_out.start()
         high, low = split(probs * dprob)
         part = dot(q_turned[:, at], high)
         dkt += part[:D] + part[D:] + dot(q_turned[:D, at], low)
         part = dot(high, k_wide) + dot(low, k_wide)
-        dq[at, :] = dq[at, :] + (part[:, :D] + part[:, D:])
-    dkv_ref[:, :ROWS, :] = (dkt * LN2).T.reshape(TK // ROWS, ROWS, D)
-    dkv_ref[:, ROWS:, :] = dvt.T.reshape(TK // ROWS, ROWS, D)
-
-    @pl.when(step == pl.num_programs(0) - 1)
-    def _():
-        for j in range(CHUNKS):
-            for b in range(2):
-                at = (4 * j + b) * ROWS
-                mine[j, b] = dq[at : at + ROWS] * SCALE
-                at += 2 * ROWS
-                theirs[j, b] = dq[at : at + ROWS] * SCALE
+        part = (part[:, :D] + part[:, D:]) * SCALE
+        for b in range(2):
+            mine[j, b] = part[b * ROWS : (b + 1) * ROWS]
+            theirs[j, b] = part[(b + 2) * ROWS : (b + 3) * ROWS]
+    dk_ref[...] = (dkt * LN2).T.reshape(BLOCKS, ROWS, D)
+    dk_out.start()
+    dv_out.wait()
+    dk_out.wait()
 
 
 def tile_grads(packs, kv):
     half = (CHUNKS, 2, ROWS, D)
-    block = pl.BlockSpec((TK // ROWS, 2 * ROWS, D), lambda i: (i, 0, 0))
+    block = pl.BlockSpec(memory_space=pl.ANY)
     return pl.pallas_call(
         tile_kernel,
         grid=(TOKENS // TK,),
@@ -139,7 +139,9 @@
         out_shape=[shape(*half), shape(*half), pltpu.HBM((BLOCKS, 2 * ROWS, D), F32)],
         scratch_shapes=[pltpu.VMEM((2 * D, TOKENS), BF16)] * 2
         + [pltpu.VMEM((TOKENS, 4 * D), BF16)] * 2
-        + [pltpu.VMEM((TOKENS, D), F32)],
+        + [pltpu.VMEM((BLOCKS, 2 * ROWS, D), F32)]
+        + [pltpu.VMEM((BLOCKS, ROWS, D), F32)] * 2
+        + [pltpu.SemaphoreType.DMA((3,))],
         compiler_params=pltpu.CompilerParams(vmem_limit_bytes=48 * 1024 * 1024),
         cost_estimate=pl.CostEstimate(flops=24_000_000_000, bytes_accessed=8 << 20, transcendentals=TOKENS * TOKENS),
     )(*packs, kv)

time: 98.2 us -> 99.5 us (1.013)
  the two profiles are of different devices: /device:TPU:2 before, /device:TPU:112 now
where the time goes in v7:
time: 99.5 us; the launch traced here: 99.3 us
  starting transfers between devices  43.6 us (44%)
  Pallas kernels  26.8 us (27%)
  waiting for transfers between devices  25.8 us (26%)
  other arithmetic  1.46 us (1%)
    ppermute x11, starting transfers between devices, along(): return lax.ppermute(x, COLUMN, pairs)  27.1 us
    pallas_call x1, Pallas kernels, tile_grads(): pl.pallas_call(tile_kernel, grid=(TOKENS // TK,), in_specs=[pl.BlockSpec(...  24.3 us
    ppermute x11, waiting for transfers between devices, along(): return lax.ppermute(x, COLUMN, pairs)  10.6 us
    all_to_all x1, waiting for transfers between devices, on_device(): dkv = lax.all_to_all(dkv, PLANE, 0, 0)  10.3 us
    all_to_all x1, starting transfers between devices, on_device(): kv = lax.all_to_all(kv, PLANE, 0, 0)  7.41 us
    all_to_all x1, starting transfers between devices, on_device(): dkv = lax.all_to_all(dkv, PLANE, 0, 0)  7.24 us
    ppermute x9, waiting for transfers between devices, swap(): return lax.ppermute(x, 'c', SWAP)  2.82 us
    pallas_call x1, Pallas kernels, pack(): pl.pallas_call(pack_kernel, out_shape=[shape(PACK, D), shape(BLOCKS, 2 *...  2.51 us
  transfers between devices with their start and end apart: 23, of which 10 were waited for; matrix products, arithmetic and copies ran while one was open for 1% of the time, Pallas kernels for 0%

profile of v7, /device:TPU:112, one launch (start us, length us, event | category | flops | bytes accessed | tf_op | source)
XLA Modules:
  0.0 99.3 jit_solution(7503167496376790529)
XLA Ops:
  0.6 2.5 %shard_map.85 = (f32[264,128]{1,0:T(8,128)}, f32[16,256,128]{2,1,0:T(8,128)}) custom-call(f32[128,128]{1,0:T(8,128)} %k.1, f32[128,128]{1,0:T(8,128)} %v.1, f32[128,128]{1,0:T(8,128)} %q.1, f32[128,128]{1,0:T(8,128)} %o.1, f32[128,128]{1,0:T(8,128)} %g.1, f32[1,128]{1,0:T(1,128)} %lse.1), custom_call_target="tpu_custom_call" | custom-call | tf_op jit(solution)/shard_map/pallas_call | solution.py:63
  3.1 7.4 %all-to-all-start = ((f32[16,256,128]{2,1,0:T(8,128)}), f32[16,256,128]{2,1,0:T(8,128)S(1)}, u32[]{:S(2)}, u32[]{:S(2)}) async-start(f32[16,256,128]{2,1,0:T(8,128)} %get-tuple-element.11), calls=%async_computation | async-start | bytes 4194304 | tf_op jit(solution)/shard_map/all_to_all | solution.py:168
  10.6 0.1 collective-permute-start.5
  10.7 3.2 %collective-permute-start = (f32[264,128]{1,0:T(8,128)S(1)}, f32[264,128]{1,0:T(8,128)S(1)}, u32[]{:S(2)}, u32[]{:S(2)}) collective-permute-start(f32[264,128]{1,0:T(8,128)S(1)} %copy-done), channel_id=1, source_target_pairs={{0,1},{1,2},{2,3},{3,4},{4,5},{5,6},{6,7},{7,0},{16,23},{17,16},{1... | collective-permute-start | bytes 405512 | tf_op jit(solution)/shard_map/ppermute | solution.py:157
  13.9 2.0 %collective-permute-done.5.refs_6_ = f32[264,128]{1,0:T(8,128)S(1)} collective-permute-done((f32[264,128]{1,0:T(8,128)S(1)}, f32[264,128]{1,0:T(8,128)S(1)}, u32[]{:S(2)}, u32[]{:S(2)}) %collective-permute-start.5) | collective-permute-done | bytes 135200 | tf_op jit(solution)/shard_map/ppermute | solution.py:163
  15.9 4.3 %collective-permute-start.6 = (f32[264,128]{1,0:T(8,128)S(1)}, f32[264,128]{1,0:T(8,128)S(1)}, u32[]{:S(2)}, u32[]{:S(2)}) collective-permute-start(f32[264,128]{1,0:T(8,128)S(1)} %collective-permute-done.5.refs_6_), channel_id=1, source_target_pairs={{0,1},{1,2},{2,3},{3,4},{4,5},{5,6},{6,7},{7,0},{16,23},{17,16},{1... | collective-permute-start | bytes 405512 | tf_op jit(solution)/shard_map/ppermute | solution.py:157
  20.3 0.0 collective-permute-done.refs_7_
  20.3 0.6 collective-permute-start.1
  20.9 0.0 collective-permute-start.4
  20.9 0.5 collective-permute-start.9
  21.4 1.4 %collective-permute-done.6.refs_10_ = f32[264,128]{1,0:T(8,128)S(1)} collective-permute-done((f32[264,128]{1,0:T(8,128)S(1)}, f32[264,128]{1,0:T(8,128)S(1)}, u32[]{:S(2)}, u32[]{:S(2)}) %collective-permute-start.6) | collective-permute-done | bytes 135200 | tf_op jit(solution)/shard_map/ppermute | solution.py:157
  22.8 3.7 %collective-permute-start.7 = (f32[264,128]{1,0:T(8,128)S(1)}, f32[264,128]{1,0:T(8,128)S(1)}, u32[]{:S(2)}, u32[]{:S(2)}) collective-permute-start(f32[264,128]{1,0:T(8,128)S(1)} %collective-permute-done.6.refs_10_), channel_id=1, source_target_pairs={{0,1},{1,2},{2,3},{3,4},{4,5},{5,6},{6,7},{7,0},{16,23},{17,16},{1... | collective-permute-start | bytes 405512 | tf_op jit(solution)/shard_map/ppermute | solution.py:157
  26.5 0.0 collective-permute-start.10
  26.5 0.0 collective-permute-done.1.refs_11_
  26.5 1.4 %collective-permute-start.2 = (f32[264,128]{1,0:T(8,128)S(1)}, f32[264,128]{1,0:T(8,128)S(1)}, u32[]{:S(2)}, u32[]{:S(2)}) collective-permute-start(f32[264,128]{1,0:T(8,128)S(1)} %collective-permute-done.1.refs_11_), channel_id=1, source_target_pairs={{0,1},{1,2},{2,3},{3,4},{4,5},{5,6},{6,7},{7,0},{16,23},{17,16},{1... | collective-permute-start | bytes 405512 | tf_op jit(solution)/shard_map/ppermute | solution.py:157
  27.9 0.0 collective-permute-done.4.refs_2_
  27.9 0.0 collective-permute-start.11
  27.9 0.0 collective-permute-done.9.refs_4_
  28.0 0.5 collective-permute-start.12
  28.5 0.6 collective-permute-done.7.refs_14_
  29.0 0.0 collective-permute-start.13
  29.0 0.0 collective-permute-done.10.refs_5_
  29.1 3.7 %collective-permute-start.8 = (f32[264,128]{1,0:T(8,128)S(1)}, f32[264,128]{1,0:T(8,128)S(1)}, u32[]{:S(2)}, u32[]{:S(2)}) collective-permute-start(f32[264,128]{1,0:T(8,128)S(1)} %collective-permute-done.7.refs_14_), channel_id=1, source_target_pairs={{0,1},{1,2},{2,3},{3,4},{4,5},{5,6},{6,7},{7,0},{16,23},{17,16},{1... | collective-permute-start | bytes 405512 | tf_op jit(solution)/shard_map/ppermute | solution.py:157
  32.8 0.0 collective-permute-done.11.refs_8_
  32.8 1.4 %collective-permute-start.3 = (f32[264,128]{1,0:T(8,128)S(1)}, f32[264,128]{1,0:T(8,128)S(1)}, u32[]{:S(2)}, u32[]{:S(2)}) collective-permute-start(f32[264,128]{1,0:T(8,128)S(1)} %collective-permute-done.2.refs_15_), channel_id=1, source_target_pairs={{0,1},{1,2},{2,3},{3,4},{4,5},{5,6},{6,7},{7,0},{16,23},{17,16},{1... | collective-permute-start | bytes 405512 | tf_op jit(solution)/shard_map/ppermute | solution.py:157
  34.3 0.0 collective-permute-done.13.refs_12_
  34.3 1.1 %collective-permute-done.8.refs_3_ = f32[264,128]{1,0:T(8,128)S(1)} collective-permute-done((f32[264,128]{1,0:T(8,128)S(1)}, f32[264,128]{1,0:T(8,128)S(1)}, u32[]{:S(2)}, u32[]{:S(2)}) %collective-permute-start.8) | collective-permute-done | bytes 135200 | tf_op jit(solution)/shard_map/ppermute | solution.py:157
  35.4 0.0 collective-permute-done.14.refs_13_
  35.4 0.6 copy-done.13
  36.0 1.9 %collective-permute-done.3.refs_1_ = f32[264,128]{1,0:T(8,128)S(1)} collective-permute-done((f32[264,128]{1,0:T(8,128)S(1)}, f32[264,128]{1,0:T(8,128)S(1)}, u32[]{:S(2)}, u32[]{:S(2)}) %collective-permute-start.3) | collective-permute-done | bytes 135200 | tf_op jit(solution)/shard_map/ppermute | solution.py:157
  38.0 0.0 all-to-all-done.refs_16_
  38.0 24.3 %shard_map.86 = (f32[4,2,128,128]{3,2,1,0:T(8,128)S(1)}, f32[4,2,128,128]{3,2,1,0:T(8,128)S(1)}, f32[16,256,128]{2,1,0:T(8,128)}) custom-call(f32[264,128]{1,0:T(8,128)} %get-tuple-element.10.refs_0_, f32[264,128]{1,0:T(8,128)S(1)} %collective-permute-done.3.refs_1_, f32[264,128]{1,0:T(8,128)} %copy-done.5, f32[264,128]{1,0:T(8,128)S(1)} %collective-permute-done.8.refs_3_, ...), custom_call_target="tpu_custom_call" | custom-call | flops 24000000000 | bytes 8388608 | tf_op jit(solution)/shard_map/pallas_call | solution.py:134
  62.3 7.2 %all-to-all-start.1 = ((f32[16,256,128]{2,1,0:T(8,128)}), f32[16,256,128]{2,1,0:T(8,128)S(1)}, u32[]{:S(2)}, u32[]{:S(2)}) async-start(f32[16,256,128]{2,1,0:T(8,128)} %get-tuple-element.14), calls=%async_computation.1 | async-start | bytes 4194304 | tf_op jit(solution)/shard_map/all_to_all | solution.py:181
  69.5 1.9 %collective-permute-done.15 = f32[4,2,128,128]{3,2,1,0:T(8,128)S(1)} collective-permute-done((f32[4,2,128,128]{3,2,1,0:T(8,128)S(1)}, f32[4,2,128,128]{3,2,1,0:T(8,128)S(1)}, u32[]{:S(2)}, u32[]{:S(2)}) %collective-permute-start.15) | collective-permute-done | bytes 524320 | tf_op jit(solution)/shard_map/ppermute | solution.py:151
  71.4 0.1 add.32
  71.5 2.6 %collective-permute-start.17 = (f32[2,128,128]{2,1,0:T(8,128)S(1)}, f32[2,128,128]{2,1,0:T(8,128)S(1)}, u32[]{:S(2)}, u32[]{:S(2)}) collective-permute-start(f32[2,128,128]{2,1,0:T(8,128)S(1)} %get-tuple-element.19), channel_id=1, source_target_pairs={{0,1},{1,2},{2,3},{3,4},{4,5},{5,6},{6,7},{7,0},{16,23},{17,16},{1... | collective-permute-start | bytes 393224 | tf_op jit(solution)/shard_map/ppermute | solution.py:157
  74.1 0.5 collective-permute-start.19
  74.6 1.4 %collective-permute-start.18 = (f32[2,128,128]{2,1,0:T(8,128)S(1)}, f32[2,128,128]{2,1,0:T(8,128)S(1)}, u32[]{:S(2)}, u32[]{:S(2)}) collective-permute-start(f32[2,128,128]{2,1,0:T(8,128)S(1)} %get-tuple-element.21), channel_id=1, source_target_pairs={{0,2},{1,3},{2,4},{3,5},{4,6},{5,7},{6,0},{7,1},{16,22},{17,23},{1... | collective-permute-start | bytes 393224 | tf_op jit(solution)/shard_map/ppermute | solution.py:157
  76.0 4.2 %collective-permute-start.16 = (f32[128,128]{1,0:T(8,128)S(1)}, f32[128,128]{1,0:T(8,128)S(1)}, u32[]{:S(2)}, u32[]{:S(2)}) collective-permute-start(f32[128,128]{1,0:T(8,128)S(1)} %slice_bitcast_fusion.3), channel_id=1, source_target_pairs={{0,4},{1,5},{2,6},{3,7},{4,0},{5,1},{6,2},{7,3},{16,20},{17,21},{1... | collective-permute-start | bytes 196616 | tf_op jit(solution)/shard_map/ppermute | solution.py:157
  80.2 0.0 collective-permute-done.17
  80.2 1.9 %collective-permute-done.19 = f32[2,128,128]{2,1,0:T(8,128)S(1)} collective-permute-done((f32[2,128,128]{2,1,0:T(8,128)S(1)}, f32[2,128,128]{2,1,0:T(8,128)S(1)}, u32[]{:S(2)}, u32[]{:S(2)}) %collective-permute-start.19) | collective-permute-done | bytes 131104 | tf_op jit(solution)/shard_map/ppermute | solution.py:157
  82.1 3.7 %collective-permute-done.18 = f32[2,128,128]{2,1,0:T(8,128)S(1)} collective-permute-done((f32[2,128,128]{2,1,0:T(8,128)S(1)}, f32[2,128,128]{2,1,0:T(8,128)S(1)}, u32[]{:S(2)}, u32[]{:S(2)}) %collective-permute-start.18) | collective-permute-done | bytes 131104 | tf_op jit(solution)/shard_map/ppermute | solution.py:157
  85.8 0.8 collective-permute-start.20
  86.6 0.0 collective-permute-done.16
  86.6 0.9 collective-permute-done.20
  87.5 0.7 fusion.3
  88.2 10.3 %all-to-all-done.1 = f32[16,256,128]{2,1,0:T(8,128)S(1)} async-done(((f32[16,256,128]{2,1,0:T(8,128)}), f32[16,256,128]{2,1,0:T(8,128)S(1)}, u32[]{:S(2)}, u32[]{:S(2)}) %all-to-all-start.1) | async-done | bytes 2097184 | tf_op jit(solution)/shard_map/all_to_all | solution.py:181
  98.5 0.7 slice_reduce_fusion
  (34 shorter events, 0.1 us)
Async XLA Ops:
  3.1 7.4 %copy-start = (f32[264,128]{1,0:T(8,128)S(1)}, f32[264,128]{1,0:T(8,128)}, u32[]{:S(2)}) copy-start(f32[264,128]{1,0:T(8,128)} %get-tuple-element.10.refs_0_) | copy-start | bytes 405508
  3.1 34.8 %all-to-all-start = ((f32[16,256,128]{2,1,0:T(8,128)}), f32[16,256,128]{2,1,0:T(8,128)S(1)}, u32[]{:S(2)}, u32[]{:S(2)}) async-start(f32[16,256,128]{2,1,0:T(8,128)} %get-tuple-element.11), calls=%async_computation | async-start | bytes 4194304 | tf_op jit(solution)/shard_map/all_to_all | solution.py:168
  10.6 5.4 %collective-permute-start.5 = (f32[264,128]{1,0:T(8,128)S(1)}, f32[264,128]{1,0:T(8,128)S(1)}, u32[]{:S(2)}, u32[]{:S(2)}) collective-permute-start(f32[264,128]{1,0:T(8,128)S(1)} %copy-done), channel_id=1, source_target_pairs={{16,1},{17,2},{18,3},{19,4},{20,5},{21,6},{22,7},{23,0},{0,23},{1,... | collective-permute-start | bytes 405512 | tf_op jit(solution)/shard_map/ppermute | solution.py:163
  10.7 9.6 %collective-permute-start = (f32[264,128]{1,0:T(8,128)S(1)}, f32[264,128]{1,0:T(8,128)S(1)}, u32[]{:S(2)}, u32[]{:S(2)}) collective-permute-start(f32[264,128]{1,0:T(8,128)S(1)} %copy-done), channel_id=1, source_target_pairs={{0,1},{1,2},{2,3},{3,4},{4,5},{5,6},{6,7},{7,0},{16,23},{17,16},{1... | collective-permute-start | bytes 405512 | tf_op jit(solution)/shard_map/ppermute | solution.py:157
  15.9 13.1 %copy-start.1 = (f32[264,128]{1,0:T(8,128)}, f32[264,128]{1,0:T(8,128)S(1)}, u32[]{:S(2)}) copy-start(f32[264,128]{1,0:T(8,128)S(1)} %collective-permute-done.5.refs_6_) | copy-start | bytes 405508
  15.9 6.9 %collective-permute-start.6 = (f32[264,128]{1,0:T(8,128)S(1)}, f32[264,128]{1,0:T(8,128)S(1)}, u32[]{:S(2)}, u32[]{:S(2)}) collective-permute-start(f32[264,128]{1,0:T(8,128)S(1)} %collective-permute-done.5.refs_6_), channel_id=1, source_target_pairs={{0,1},{1,2},{2,3},{3,4},{4,5},{5,6},{6,7},{7,0},{16,23},{17,16},{1... | collective-permute-start | bytes 405512 | tf_op jit(solution)/shard_map/ppermute | solution.py:157
  20.3 17.7 %copy-start.2 = (f32[264,128]{1,0:T(8,128)}, f32[264,128]{1,0:T(8,128)S(1)}, u32[]{:S(2)}) copy-start(f32[264,128]{1,0:T(8,128)S(1)} %collective-permute-done.refs_7_) | copy-start | bytes 405508
  20.3 6.2 %collective-permute-start.1 = (f32[264,128]{1,0:T(8,128)S(1)}, f32[264,128]{1,0:T(8,128)S(1)}, u32[]{:S(2)}, u32[]{:S(2)}) collective-permute-start(f32[264,128]{1,0:T(8,128)S(1)} %collective-permute-done.refs_7_), channel_id=1, source_target_pairs={{0,1},{1,2},{2,3},{3,4},{4,5},{5,6},{6,7},{7,0},{16,23},{17,16},{1... | collective-permute-start | bytes 405512 | tf_op jit(solution)/shard_map/ppermute | solution.py:157
  20.9 7.1 %collective-permute-start.4 = (f32[264,128]{1,0:T(8,128)S(1)}, f32[264,128]{1,0:T(8,128)S(1)}, u32[]{:S(2)}, u32[]{:S(2)}) collective-permute-start(f32[264,128]{1,0:T(8,128)S(1)} %copy-done), channel_id=1, source_target_pairs={{0,16},{16,0},{1,17},{17,1},{2,18},{18,2},{3,19},{19,3},{4,20},{20... | collective-permute-start | bytes 405512 | tf_op jit(solution)/shard_map/ppermute | solution.py:151
  20.9 7.1 %collective-permute-start.9 = (f32[264,128]{1,0:T(8,128)S(1)}, f32[264,128]{1,0:T(8,128)S(1)}, u32[]{:S(2)}, u32[]{:S(2)}) collective-permute-start(f32[264,128]{1,0:T(8,128)S(1)} %collective-permute-done.5.refs_6_), channel_id=1, source_target_pairs={{0,16},{16,0},{1,17},{17,1},{2,18},{18,2},{3,19},{19,3},{4,20},{20... | collective-permute-start | bytes 405512 | tf_op jit(solution)/shard_map/ppermute | solution.py:151
  22.8 15.1 %copy-start.3 = (f32[264,128]{1,0:T(8,128)}, f32[264,128]{1,0:T(8,128)S(1)}, u32[]{:S(2)}) copy-start(f32[264,128]{1,0:T(8,128)S(1)} %collective-permute-done.6.refs_10_) | copy-start | bytes 405508
  22.8 6.2 %collective-permute-start.7 = (f32[264,128]{1,0:T(8,128)S(1)}, f32[264,128]{1,0:T(8,128)S(1)}, u32[]{:S(2)}, u32[]{:S(2)}) collective-permute-start(f32[264,128]{1,0:T(8,128)S(1)} %collective-permute-done.6.refs_10_), channel_id=1, source_target_pairs={{0,1},{1,2},{2,3},{3,4},{4,5},{5,6},{6,7},{7,0},{16,23},{17,16},{1... | collective-permute-start | bytes 405512 | tf_op jit(solution)/shard_map/ppermute | solution.py:157
  26.5 2.6 %collective-permute-start.10 = (f32[264,128]{1,0:T(8,128)S(1)}, f32[264,128]{1,0:T(8,128)S(1)}, u32[]{:S(2)}, u32[]{:S(2)}) collective-permute-start(f32[264,128]{1,0:T(8,128)S(1)} %collective-permute-done.refs_7_), channel_id=1, source_target_pairs={{0,16},{16,0},{1,17},{17,1},{2,18},{18,2},{3,19},{19,3},{4,20},{20... | collective-permute-start | bytes 405512 | tf_op jit(solution)/shard_map/ppermute | solution.py:151
  26.5 11.5 %copy-start.4 = (f32[264,128]{1,0:T(8,128)}, f32[264,128]{1,0:T(8,128)S(1)}, u32[]{:S(2)}) copy-start(f32[264,128]{1,0:T(8,128)S(1)} %collective-permute-done.1.refs_11_) | copy-start | bytes 405508
  26.5 6.3 %collective-permute-start.2 = (f32[264,128]{1,0:T(8,128)S(1)}, f32[264,128]{1,0:T(8,128)S(1)}, u32[]{:S(2)}, u32[]{:S(2)}) collective-permute-start(f32[264,128]{1,0:T(8,128)S(1)} %collective-permute-done.1.refs_11_), channel_id=1, source_target_pairs={{0,1},{1,2},{2,3},{3,4},{4,5},{5,6},{6,7},{7,0},{16,23},{17,16},{1... | collective-permute-start | bytes 405512 | tf_op jit(solution)/shard_map/ppermute | solution.py:157
  27.9 10.0 %copy-start.5 = (f32[264,128]{1,0:T(8,128)}, f32[264,128]{1,0:T(8,128)S(1)}, u32[]{:S(2)}) copy-start(f32[264,128]{1,0:T(8,128)S(1)} %collective-permute-done.4.refs_2_) | copy-start | bytes 405508
  27.9 4.9 %collective-permute-start.11 = (f32[264,128]{1,0:T(8,128)S(1)}, f32[264,128]{1,0:T(8,128)S(1)}, u32[]{:S(2)}, u32[]{:S(2)}) collective-permute-start(f32[264,128]{1,0:T(8,128)S(1)} %collective-permute-done.6.refs_10_), channel_id=1, source_target_pairs={{0,16},{16,0},{1,17},{17,1},{2,18},{18,2},{3,19},{19,3},{4,20},{20... | collective-permute-start | bytes 405512 | tf_op jit(solution)/shard_map/ppermute | solution.py:151
  27.9 10.0 %copy-start.6 = (f32[264,128]{1,0:T(8,128)}, f32[264,128]{1,0:T(8,128)S(1)}, u32[]{:S(2)}) copy-start(f32[264,128]{1,0:T(8,128)S(1)} %collective-permute-done.9.refs_4_) | copy-start | bytes 405508
  28.0 6.3 %collective-permute-start.12 = (f32[264,128]{1,0:T(8,128)S(1)}, f32[264,128]{1,0:T(8,128)S(1)}, u32[]{:S(2)}, u32[]{:S(2)}) collective-permute-start(f32[264,128]{1,0:T(8,128)S(1)} %collective-permute-done.1.refs_11_), channel_id=1, source_target_pairs={{0,16},{16,0},{1,17},{17,1},{2,18},{18,2},{3,19},{19,3},{4,20},{20... | collective-permute-start | bytes 405512 | tf_op jit(solution)/shard_map/ppermute | solution.py:151
  29.0 8.9 %copy-start.7 = (f32[264,128]{1,0:T(8,128)}, f32[264,128]{1,0:T(8,128)S(1)}, u32[]{:S(2)}) copy-start(f32[264,128]{1,0:T(8,128)S(1)} %collective-permute-done.7.refs_14_) | copy-start | bytes 405508
  29.0 5.2 %collective-permute-start.13 = (f32[264,128]{1,0:T(8,128)S(1)}, f32[264,128]{1,0:T(8,128)S(1)}, u32[]{:S(2)}, u32[]{:S(2)}) collective-permute-start(f32[264,128]{1,0:T(8,128)S(1)} %collective-permute-done.7.refs_14_), channel_id=1, source_target_pairs={{0,16},{16,0},{1,17},{17,1},{2,18},{18,2},{3,19},{19,3},{4,20},{20... | collective-permute-start | bytes 405512 | tf_op jit(solution)/shard_map/ppermute | solution.py:151
  29.1 8.9 %copy-start.8 = (f32[264,128]{1,0:T(8,128)}, f32[264,128]{1,0:T(8,128)S(1)}, u32[]{:S(2)}) copy-start(f32[264,128]{1,0:T(8,128)S(1)} %collective-permute-done.10.refs_5_) | copy-start | bytes 405508
  29.1 6.3 %collective-permute-start.8 = (f32[264,128]{1,0:T(8,128)S(1)}, f32[264,128]{1,0:T(8,128)S(1)}, u32[]{:S(2)}, u32[]{:S(2)}) collective-permute-start(f32[264,128]{1,0:T(8,128)S(1)} %collective-permute-done.7.refs_14_), channel_id=1, source_target_pairs={{0,1},{1,2},{2,3},{3,4},{4,5},{5,6},{6,7},{7,0},{16,23},{17,16},{1... | collective-permute-start | bytes 405512 | tf_op jit(solution)/shard_map/ppermute | solution.py:157
  32.8 2.6 %copy-start.9 = (f32[264,128]{1,0:T(8,128)}, f32[264,128]{1,0:T(8,128)S(1)}, u32[]{:S(2)}) copy-start(f32[264,128]{1,0:T(8,128)S(1)} %collective-permute-done.2.refs_15_) | copy-start | bytes 405508
  32.8 2.6 %collective-permute-start.14 = (f32[264,128]{1,0:T(8,128)S(1)}, f32[264,128]{1,0:T(8,128)S(1)}, u32[]{:S(2)}, u32[]{:S(2)}) collective-permute-start(f32[264,128]{1,0:T(8,128)S(1)} %collective-permute-done.2.refs_15_), channel_id=1, source_target_pairs={{0,16},{16,0},{1,17},{17,1},{2,18},{18,2},{3,19},{19,3},{4,20},{20... | collective-permute-start | bytes 405512 | tf_op jit(solution)/shard_map/ppermute | solution.py:151
  32.8 5.2 %copy-start.10 = (f32[264,128]{1,0:T(8,128)}, f32[264,128]{1,0:T(8,128)S(1)}, u32[]{:S(2)}) copy-start(f32[264,128]{1,0:T(8,128)S(1)} %collective-permute-done.11.refs_8_) | copy-start | bytes 405508
  32.8 5.1 %collective-permute-start.3 = (f32[264,128]{1,0:T(8,128)S(1)}, f32[264,128]{1,0:T(8,128)S(1)}, u32[]{:S(2)}, u32[]{:S(2)}) collective-permute-start(f32[264,128]{1,0:T(8,128)S(1)} %collective-permute-done.2.refs_15_), channel_id=1, source_target_pairs={{0,1},{1,2},{2,3},{3,4},{4,5},{5,6},{6,7},{7,0},{16,23},{17,16},{1... | collective-permute-start | bytes 405512 | tf_op jit(solution)/shard_map/ppermute | solution.py:157
  34.3 1.1 %copy-start.11 = (f32[264,128]{1,0:T(8,128)}, f32[264,128]{1,0:T(8,128)S(1)}, u32[]{:S(2)}) copy-start(f32[264,128]{1,0:T(8,128)S(1)} %collective-permute-done.12.refs_9_) | copy-start | bytes 405508
  34.3 1.1 %copy-start.12 = (f32[264,128]{1,0:T(8,128)}, f32[264,128]{1,0:T(8,128)S(1)}, u32[]{:S(2)}) copy-start(f32[264,128]{1,0:T(8,128)S(1)} %collective-permute-done.13.refs_12_) | copy-start | bytes 405508
  35.4 0.6 copy-start.13
  62.3 36.3 %all-to-all-start.1 = ((f32[16,256,128]{2,1,0:T(8,128)}), f32[16,256,128]{2,1,0:T(8,128)S(1)}, u32[]{:S(2)}, u32[]{:S(2)}) async-start(f32[16,256,128]{2,1,0:T(8,128)} %get-tuple-element.14), calls=%async_computation.1 | async-start | bytes 4194304 | tf_op jit(solution)/shard_map/all_to_all | solution.py:181
  69.5 1.9 %collective-permute-start.15 = (f32[4,2,128,128]{3,2,1,0:T(8,128)S(1)}, f32[4,2,128,128]{3,2,1,0:T(8,128)S(1)}, u32[]{:S(2)}, u32[]{:S(2)}) collective-permute-start(f32[4,2,128,128]{3,2,1,0:T(8,128)S(1)} %get-tuple-element.13), channel_id=1, source_target_pairs={{0,16},{16,0},{1,17},{17,1},{2,18},{18,2},{3,19},{19,3},{4,20},{20... | collective-permute-start | bytes 1572872 | tf_op jit(solution)/shard_map/ppermute | solution.py:151
  71.5 8.7 %collective-permute-start.17 = (f32[2,128,128]{2,1,0:T(8,128)S(1)}, f32[2,128,128]{2,1,0:T(8,128)S(1)}, u32[]{:S(2)}, u32[]{:S(2)}) collective-permute-start(f32[2,128,128]{2,1,0:T(8,128)S(1)} %get-tuple-element.19), channel_id=1, source_target_pairs={{0,1},{1,2},{2,3},{3,4},{4,5},{5,6},{6,7},{7,0},{16,23},{17,16},{1... | collective-permute-start | bytes 393224 | tf_op jit(solution)/shard_map/ppermute | solution.py:157
  74.1 7.9 %collective-permute-start.19 = (f32[2,128,128]{2,1,0:T(8,128)S(1)}, f32[2,128,128]{2,1,0:T(8,128)S(1)}, u32[]{:S(2)}, u32[]{:S(2)}) collective-permute-start(f32[2,128,128]{2,1,0:T(8,128)S(1)} %get-tuple-element.20), channel_id=1, source_target_pairs={{0,3},{1,4},{2,5},{3,6},{4,7},{5,0},{6,1},{7,2},{16,21},{17,22},{1... | collective-permute-start | bytes 393224 | tf_op jit(solution)/shard_map/ppermute | solution.py:157
  74.6 11.2 %collective-permute-start.18 = (f32[2,128,128]{2,1,0:T(8,128)S(1)}, f32[2,128,128]{2,1,0:T(8,128)S(1)}, u32[]{:S(2)}, u32[]{:S(2)}) collective-permute-start(f32[2,128,128]{2,1,0:T(8,128)S(1)} %get-tuple-element.21), channel_id=1, source_target_pairs={{0,2},{1,3},{2,4},{3,5},{4,6},{5,7},{6,0},{7,1},{16,22},{17,23},{1... | collective-permute-start | bytes 393224 | tf_op jit(solution)/shard_map/ppermute | solution.py:157
  76.0 10.6 %collective-permute-start.16 = (f32[128,128]{1,0:T(8,128)S(1)}, f32[128,128]{1,0:T(8,128)S(1)}, u32[]{:S(2)}, u32[]{:S(2)}) collective-permute-start(f32[128,128]{1,0:T(8,128)S(1)} %slice_bitcast_fusion.3), channel_id=1, source_target_pairs={{0,4},{1,5},{2,6},{3,7},{4,0},{5,1},{6,2},{7,3},{16,20},{17,21},{1... | collective-permute-start | bytes 196616 | tf_op jit(solution)/shard_map/ppermute | solution.py:157
  85.8 1.7 %collective-permute-start.20 = (f32[128,128]{1,0:T(8,128)S(1)}, f32[128,128]{1,0:T(8,128)S(1)}, u32[]{:S(2)}, u32[]{:S(2)}) collective-permute-start(f32[128,128]{1,0:T(8,128)S(1)} %fusion), channel_id=1, source_target_pairs={{0,16},{16,0},{1,17},{17,1},{2,18},{18,2},{3,19},{19,3},{4,20},{20... | collective-permute-start | bytes 196616 | tf_op jit(solution)/shard_map/ppermute | solution.py:151
